TPU v7x, 128 devices: a whole 4x4x4 slice. The times are simulated.
128 devices in a mesh: seq: 32 (over x, z, core), exp: 4 (over y).
Axes of the slice: x: 4, y: 4, z: 4, core: 2. Of those that a mesh axis runs over, the one named last changes fastest.
Arguments:
- coarse_in: bfloat16 [4096, 1024], P('seq', 'exp'), may hold values from -24 to 24
- norm1_gain: float32 [1024], replicated, may hold values from 0.1 to 1.9
- qkv_weight: bfloat16 [3, 1024, 1024], P(None, None, 'exp'), may hold values from -0.1875 to 0.1875
- head_scale: float32 [16], P('exp'), may hold values from 2.5 to 40, as said below
- out_weight: bfloat16 [1024, 1024], P('exp'), may hold values from -0.1875 to 0.1875
- norm2_gain: float32 [1024], replicated, may hold values from 0.1 to 1.9
- mlp_in: bfloat16 [1024, 4096], P(None, 'exp'), may hold values from -0.1875 to 0.1875
- mlp_out: bfloat16 [4096, 1024], P('exp'), may hold values from -0.09375 to 0.09375
- fine_in: bfloat16 [20480, 1024], P(('seq', 'exp')), may hold values from -24 to 24
- parent_device: int32 [20480, 1], P(('seq', 'exp')), may hold values from 0 to 31; in each aligned block of 160 rows (0 to 159, 160 to 319, ...) at most 10 rows name the same one
- parent_row: int32 [20480], P(('seq', 'exp')), may hold values from 0 to 127
- octant: int32 [20480], P(('seq', 'exp')), may hold values from 0 to 7
- octant_table: bfloat16 [8, 1024], replicated, may hold values from -6 to 6
- norm3_gain: float32 [1024], replicated, may hold values from 0.1 to 1.9
- expert_ids: int32 [20480, 2], P(('seq', 'exp')), may hold values from 0 to 15, all different within a row; in each aligned block of 160 rows (0 to 159, 160 to 319, ...) at most 30 rows name the same one
- expert_gates: float32 [20480, 2], P(('seq', 'exp')), may hold values from 0.2 to 1
- gate_weight: bfloat16 [32, 1024, 2048], P('seq', None, 'exp'), may hold values from -0.1875 to 0.1875
- up_weight: bfloat16 [32, 1024, 2048], P('seq', None, 'exp'), may hold values from -0.1875 to 0.1875
- down_weight: bfloat16 [32, 1024, 2048], P('seq', None, 'exp'), may hold values from -0.09375 to 0.09375
Outputs:
- coarse_out: bfloat16 [4096, 1024], P('seq')
- fine_out: bfloat16 [20480, 1024], P(('seq', 'exp'))
Inputs may be any that keep to these rules, and one draw needn't show every extreme that they name: `parent_device`: among the rows of one device no index appears more than 10 times. `expert_ids`: each row names two different experts; among the rows of one device no expert appears more than 30 times. `head_scale`: one positive scale for each head.
All inputs are finite; a program needn't handle non-finite values.
Results may differ from a plain program's by a relative error of at most 0.0095.
Values may be sent and summed in bfloat16 or wider, within the bound.
No kernel may reach another device: no remote copies, remote signals or barrier semaphores. Data moves between devices by JAX's collectives and lax.ppermute only.
A program may use at most 128 MiB of HBM per device.

v0:
```python
import math

import jax
import jax.numpy as jnp
from jax import lax
from jax.sharding import PartitionSpec as P

EXPERTS = 16
CAP = 30


EPSILON = 1e-06


def rms_scale(vector_in, gain_vec):
    return (
        vector_in
        * lax.rsqrt(jnp.mean(vector_in * vector_in, axis=-1, keepdims=True) + EPSILON)
        * gain_vec
    )


def head_norm(projection, row_count, local_heads, head_dim):
    shaped = projection.reshape(row_count, local_heads, head_dim)
    return (shaped * lax.rsqrt(jnp.mean(shaped * shaped, axis=-1, keepdims=True) + EPSILON)).astype(
        jnp.bfloat16
    )


def per_device(
    coarse_in,
    norm1_gain,
    qkv_weight,
    head_scale,
    out_weight,
    norm2_gain,
    mlp_in,
    mlp_out,
    fine_in,
    parent_device,
    parent_row,
    octant,
    octant_table,
    norm3_gain,
    expert_ids,
    expert_gates,
    gate_weight,
    up_weight,
    down_weight,
):
    seq_devices = lax.axis_size("seq")
    rows_local = coarse_in.shape[0]
    local_heads = head_scale.shape[0]
    head_dim = qkv_weight.shape[2] // local_heads
    features = lax.all_gather(coarse_in, "exp", axis=1, tiled=True)
    residual = features.astype(jnp.float32)
    width = residual.shape[1]
    normed = rms_scale(residual, norm1_gain).astype(jnp.bfloat16)
    projected = jnp.einsum("rd,kdc->krc", normed, qkv_weight, preferred_element_type=jnp.float32)
    queries = head_norm(projected[0], rows_local, local_heads, head_dim)
    key_rows = head_norm(projected[1], rows_local, local_heads, head_dim).reshape(
        rows_local, local_heads * head_dim
    )
    value_rows = projected[2].astype(jnp.bfloat16)
    factor = head_scale / math.sqrt(head_dim)
    row_top = jnp.full((local_heads, rows_local), -jnp.inf, jnp.float32)
    running = jnp.zeros((local_heads, rows_local), jnp.float32)
    weighted = jnp.zeros((local_heads, rows_local, head_dim), jnp.float32)
    key_piece = lax.all_gather(key_rows, "seq", axis=0, tiled=True)
    value_piece = lax.all_gather(value_rows, "seq", axis=0, tiled=True)
    row_count = key_piece.shape[0]
    key_heads = key_piece.reshape(row_count, local_heads, head_dim)
    value_heads = value_piece.reshape(row_count, local_heads, head_dim)
    scores = (
        jnp.einsum("qhc,khc->hqk", queries, key_heads, preferred_element_type=jnp.float32)
        * factor[:, None, None]
    )
    new_top = jnp.max(scores, axis=-1)
    weights = jnp.exp(scores - new_top[:, :, None])
    rescale = jnp.exp(row_top - new_top)
    running = running * rescale + jnp.sum(weights, axis=-1)
    weighted = weighted * rescale[:, :, None] + jnp.einsum(
        "hqk,khc->hqc",
        weights.astype(jnp.bfloat16),
        value_heads,
        preferred_element_type=jnp.float32,
    )
    row_top, running, weighted = (new_top, running, weighted)
    attended = (
        jnp.transpose(weighted / running[:, :, None], (1, 0, 2))
        .reshape(rows_local, local_heads * head_dim)
        .astype(jnp.bfloat16)
    )
    attn_part = jnp.dot(attended, out_weight, preferred_element_type=jnp.float32)
    mixed_sum = residual + lax.psum(attn_part.astype(jnp.bfloat16), "exp").astype(jnp.float32)
    normed2 = rms_scale(mixed_sum, norm2_gain).astype(jnp.bfloat16)
    inner_coarse = jax.nn.gelu(jnp.dot(normed2, mlp_in, preferred_element_type=jnp.float32)).astype(
        jnp.bfloat16
    )
    mlp_part = jnp.dot(inner_coarse, mlp_out, preferred_element_type=jnp.float32)
    coarse_new = (
        mixed_sum + lax.psum(mlp_part.astype(jnp.bfloat16), "exp").astype(jnp.float32)
    ).astype(jnp.bfloat16)
    fine_count = fine_in.shape[0]
    owner_rows = parent_device[:, 0]
    target = owner_rows * rows_local + parent_row
    block_rows = lax.all_gather(coarse_new, "seq", axis=0, tiled=True)
    row_count = block_rows.shape[0]
    chosen = (target[:, None] == jnp.arange(row_count, dtype=jnp.int32)[None, :]).astype(
        jnp.bfloat16
    )
    parents = jnp.dot(chosen, block_rows, preferred_element_type=jnp.float32)
    octant_hot = (octant[:, None] == jnp.arange(8, dtype=jnp.int32)[None, :]).astype(jnp.bfloat16)
    octant_rows = jnp.dot(octant_hot, octant_table, preferred_element_type=jnp.float32)
    fine_sum = fine_in.astype(jnp.float32) + parents + octant_rows
    fine_norm = rms_scale(fine_sum, norm3_gain).astype(jnp.bfloat16)
    flat_ids = expert_ids.reshape(-1)
    member = (flat_ids[:, None] == jnp.arange(EXPERTS, dtype=jnp.int32)[None, :]).astype(jnp.int32)
    expert_slot = jnp.sum(member * (jnp.cumsum(member, axis=0) - 1), axis=1)
    token_of = jnp.arange(2 * fine_count, dtype=jnp.int32) // 2
    outgoing = (
        jnp.zeros((EXPERTS, CAP, width), jnp.bfloat16)
        .at[flat_ids, expert_slot]
        .set(fine_norm[token_of])
    )
    outgoing = jnp.broadcast_to(outgoing[:, None], (EXPERTS, 2, CAP, width)).reshape(
        2 * EXPERTS, CAP, width
    )
    local_halves = gate_weight.shape[0]
    arrived = lax.all_to_all(outgoing, "seq", split_axis=0, concat_axis=0, tiled=True)
    slot_count = arrived.shape[1]
    grouped = arrived.reshape(seq_devices, local_halves, slot_count, width)
    pooled = lax.all_gather(grouped, "exp", axis=2, tiled=True)
    gate_part = jnp.einsum(
        "shrd,hdf->shrf", pooled, gate_weight, preferred_element_type=jnp.float32
    )
    up_part = jnp.einsum("shrd,hdf->shrf", pooled, up_weight, preferred_element_type=jnp.float32)
    inner_act = (jax.nn.silu(gate_part) * up_part).astype(jnp.bfloat16)
    partial_out = jnp.einsum(
        "shrf,hdf->shrd", inner_act, down_weight, preferred_element_type=jnp.float32
    )
    result = lax.psum_scatter(
        partial_out.astype(jnp.bfloat16), "exp", scatter_dimension=2, tiled=True
    ).astype(jnp.float32)
    returned = lax.all_to_all(
        result.reshape(seq_devices * local_halves, slot_count, width).astype(jnp.bfloat16),
        "seq",
        split_axis=0,
        concat_axis=0,
        tiled=True,
    ).astype(jnp.float32)
    halves_sum = jnp.sum(returned.reshape(EXPERTS, 2, CAP, width), axis=1)
    flat_out = halves_sum.reshape(EXPERTS * CAP, width)[flat_ids * CAP + expert_slot]
    expert_mix = jnp.sum(flat_out.reshape(fine_count, 2, width) * expert_gates[:, :, None], axis=1)
    fine_out = (fine_sum + expert_mix).astype(jnp.bfloat16)
    return (coarse_new, fine_out)


def solution(mesh):
    return jax.shard_map(
        per_device,
        mesh=mesh,
        in_specs=(
            P("seq", "exp"),
            P(),
            P(None, None, "exp"),
            P("exp"),
            P("exp", None),
            P(),
            P(None, "exp"),
            P("exp", None),
            P(("seq", "exp"), None),
            P(("seq", "exp"), None),
            P(("seq", "exp")),
            P(("seq", "exp")),
            P(),
            P(),
            P(("seq", "exp"), None),
            P(("seq", "exp"), None),
            P("seq", None, "exp"),
            P("seq", None, "exp"),
            P("seq", None, "exp"),
        ),
        out_specs=(P("seq", None), P(("seq", "exp"), None)),
        check_vma=False,
    )
```

profile of v0, /device:TPU:1, one launch (start us, length us, event | category | flops | bytes accessed | tf_op | source)
XLA Modules:
  0.0 611.4 jit_solution(17575862740619898372)
XLA Ops:
  7.2 11.6 %all_gather.15 = bf16[128,1024]{1,0:T(8,128)(2,1)S(1)} all-gather(bf16[128,256]{1,0:T(8,128)(2,1)} %param.19), channel_id=1, replica_groups=mesh['seq'=32,'exp'=4] {'exp'}, dimensions={1}, use_global_device_ids=true | all-gather | bytes 327680 | tf_op jit(solution)/shard_map/all_gather | solution.py:55
  19.0 1.8 convolution_bitcast_fusion
  22.7 47.7 %all-gather.7.cloned.1.call-done = bf16[4096,256]{1,0:T(8,128)(2,1)} async-done(((bf16[128,256]{1,0:T(8,128)(2,1)}), bf16[4096,256]{1,0:T(8,128)(2,1)}) %all-gather.7.cloned.1.call-update) | async-done | bytes 2097168 | tf_op jit(solution)/shard_map/all_gather | solution.py:69
  70.4 4.1 copy.54
  74.5 3.0 multiply_reduce_fusion
  79.0 1.7 copy-done.2
  80.7 35.8 %all-gather.11.cloned.1.call-done = bf16[1,4096,256]{2,1,0:T(8,128)(2,1)} async-done(((bf16[1,128,256]{2,1,0:T(8,128)(2,1)}), bf16[1,4096,256]{2,1,0:T(8,128)(2,1)}) %all-gather.11.cloned.1.call-update) | async-done | bytes 2097168 | tf_op jit(solution)/shard_map/all_gather | solution.py:70
  116.5 4.1 copy.55
  120.6 5.9 fusion.32
  127.6 38.5 %all-reduce.4.cloned.1.call-done = bf16[128,1024]{1,0:T(8,128)(2,1)} async-done(((bf16[128,1024]{1,0:T(8,128)(2,1)}), bf16[128,1024]{1,0:T(8,128)(2,1)}) %all-reduce.4.cloned.1.call-update) | async-done | bytes 262160 | tf_op jit(solution)/shard_map/psum | solution.py:95
  167.3 3.3 convolution_convert_fusion
  170.7 42.2 %all-reduce.6.cloned.1.call-done = bf16[128,1024]{1,0:T(8,128)(2,1)} async-done(((bf16[128,1024]{1,0:T(8,128)(2,1)}), bf16[128,1024]{1,0:T(8,128)(2,1)}) %all-reduce.6.cloned.1.call-update) | async-done | bytes 262160 | tf_op jit(solution)/shard_map/psum | solution.py:102
  212.9 1.8 add_convert_fusion.1
  216.9 54.8 %all-gather.9.cloned.1.call-done = bf16[4096,1024]{1,0:T(8,128)(2,1)} async-done(((bf16[128,1024]{1,0:T(8,128)(2,1)}), bf16[4096,1024]{1,0:T(8,128)(2,1)}) %all-gather.9.cloned.1.call-update) | async-done | bytes 8388624 | tf_op jit(solution)/shard_map/all_gather | solution.py:107
  271.7 5.0 fusion.22
  277.2 2.1 gather_fusion
  279.4 20.9 %scatter_fusion = bf16[16,30,1024]{2,0,1:T(8,128)(2,1)S(1)} fusion(bf16[16,30,1024]{2,0,1:T(8,128)(2,1)S(1)} %broadcast_in_dim.10, s32[320]{0:T(512)S(1)} %get-tuple-element.3, bf16[320,1024]{1,0:T(8,128)(2,1)S(1)} %gather_fusion), kind=kCustom, calls=%fused_computation.2 | custom fusion | bytes 1968640 | tf_op jit(solution)/shard_map/scatter | solution.py:124
  301.1 33.4 %all_to_all.10 = bf16[32,30,1024]{2,1,0:T(8,128)(2,1)S(1)} all-to-all(bf16[32,30,1024]{2,1,0:T(8,128)(2,1)S(1)} %bitcast.111), channel_id=1, replica_groups=mesh['seq'=32,'exp'=4] {'seq'}, dimensions={0} | all-to-all | bytes 3932160 | tf_op jit(solution)/shard_map/all_to_all | solution.py:130
  334.5 2.4 copy.61
  337.6 75.9 %all-gather.13.cloned.1.call-done = bf16[32,120,1024]{2,0,1:T(8,128)(2,1)} async-done(((bf16[32,30,1024]{2,0,1:T(8,128)(2,1)}), bf16[32,120,1024]{2,0,1:T(8,128)(2,1)}) %all-gather.13.cloned.1.call-update) | async-done | bytes 7864336 | tf_op jit(solution)/shard_map/all_gather | solution.py:133
  413.4 23.6 %fusion.4 = f32[32,120,512]{2,1,0:T(8,128)} fusion(bf16[32,120,1024]{2,0,1:T(8,128)(2,1)} %all-gather.13.cloned.1.call-done, bf16[1,1024,512]{2,1,0:T(8,128)(2,1)S(1)} %copy-done.12), kind=kOutput, calls=%fused_computation.13 | convolution fusion | flops 4026531840 | bytes 16777216 | tf_op jit(solution)/shard_map/shrd,hdf->shrf/dot_general | solution.py:137
  437.0 22.2 %convert_bitcast_fusion = bf16[32,1,120,1024]{3,2,0,1:T(8,128)(2,1)} fusion(f32[32,120,512]{2,1,0:T(8,128)} %fusion.4, bf16[32,120,1024]{2,0,1:T(8,128)(2,1)} %all-gather.13.cloned.1.call-done, bf16[1,1024,512]{2,1,0:T(8,128)(2,1)S(1)} %copy-done.13, bf16[1,1024,512]{2,1,0:T(8,128)(2,1)} %param.35), kind=kOutput, calls=%fused_computation.12 | convolution fusion | flops 8068792320 | bytes 25690112 | tf_op jit(solution)/shard_map/shrf,hdf->shrd/dot_general | solution.py:139
  459.2 10.7 %copy.64 = bf16[32,1,120,1024]{3,0,1,2:T(8,128)(2,1)} copy(bf16[32,1,120,1024]{3,2,0,1:T(8,128)(2,1)} %convert_bitcast_fusion) | data formatting | bytes 15728640 | tf_op jit(solution)/shard_map/convert_element_type | solution.py:143
  470.0 77.9 %reduce-scatter.2.cloned.1.call-done = bf16[32,1,30,1024]{3,0,1,2:T(8,128)(2,1)} async-done(((bf16[32,1,120,1024]{3,0,1,2:T(8,128)(2,1)}), bf16[32,1,30,1024]{3,0,1,2:T(8,128)(2,1)}) %reduce-scatter.2.cloned.1.call-update) | async-done | bytes 1966096 | tf_op jit(solution)/shard_map/reduce_scatter | solution.py:142
  547.9 4.0 copy.65
  551.9 7.6 %all-to-all-start.1 = ((bf16[32,30,1024]{2,1,0:T(8,128)(2,1)}), bf16[32,30,1024]{2,1,0:T(8,128)(2,1)S(1)}, u32[]{:S(2)}, u32[]{:S(2)}) async-start(bf16[32,30,1024]{2,1,0:T(8,128)(2,1)} %copy.65), calls=%async_computation.2 | async-start | bytes 4194304 | tf_op jit(solution)/shard_map/all_to_all | solution.py:145
  559.7 28.2 %all-to-all-done.1 = bf16[32,30,1024]{2,1,0:T(8,128)(2,1)S(1)} async-done(((bf16[32,30,1024]{2,1,0:T(8,128)(2,1)}), bf16[32,30,1024]{2,1,0:T(8,128)(2,1)S(1)}, u32[]{:S(2)}, u32[]{:S(2)}) %all-to-all-start.1) | async-done | bytes 1966112 | tf_op jit(solution)/shard_map/all_to_all | solution.py:145
  587.8 1.8 convert_reduce_fusion
  589.7 2.8 reshape.257
  592.5 5.0 gather_fusion.1
  597.5 2.9 reshape.258
  600.5 3.0 multiply_reduce_fusion.1
  (91 shorter events, 10.9 us)
Async XLA Ops:
  7.2 160.1 %copy-start = (bf16[1024,1024]{1,0:T(8,128)(2,1)S(1)}, bf16[1024,1024]{1,0:T(8,128)(2,1)}, u32[]{:S(2)}) copy-start(bf16[1024,1024]{1,0:T(8,128)(2,1)} %param.26) | copy-start | bytes 6291460
  7.2 15.5 %copy-start.16 = (f32[4]{0:T(128)S(1)}, f32[4]{0:T(128)}, u32[]{:S(2)}) copy-start(f32[4]{0:T(128)} %param.22) | copy-start | bytes 52
  7.2 63.2 %all-gather.7.cloned.1.call-start = ((), (), s32[]{:S(2)}) async-start(), calls=%async_computation.3 | async-start | bytes 2162688 | tf_op jit(solution)/shard_map/all_gather | solution.py:69
  21.8 94.7 %all-gather.11.cloned.1.call-start = ((), (), s32[]{:S(2)}) async-start(), calls=%async_computation.8 | async-start | bytes 2162688 | tf_op jit(solution)/shard_map/all_gather | solution.py:70
  22.5 143.6 %all-reduce.4.cloned.1.call-start = ((), (), s32[]{:S(2)}) async-start(), calls=%async_computation.4 | async-start | bytes 524288 | tf_op jit(solution)/shard_map/psum | solution.py:95
  77.5 3.2 copy-start.2
  120.6 5.9 copy-start.4
  120.6 46.7 %copy-start.15 = (f32[1024]{0:T(1024)S(1)}, f32[1024]{0:T(1024)}, u32[]{:S(2)}) copy-start(f32[1024]{0:T(1024)} %param.24) | copy-start | bytes 12292
  127.5 87.5 %copy-start.7 = (s32[160,2]{0,1:T(2,128)S(1)}, s32[160,2]{0,1:T(2,128)}, u32[]{:S(2)}) copy-start(s32[160,2]{0,1:T(2,128)} %param.33) | copy-start | bytes 3844
  127.5 89.1 %copy-start.10 = (s32[160,1]{0,1:T(1,128)S(1)}, s32[160,1]{0,1:T(1,128)}, u32[]{:S(2)}) copy-start(s32[160,1]{0,1:T(1,128)} %param.28) | copy-start | bytes 1924
  127.5 89.1 %copy-start.9 = (s32[160]{0:T(256)S(1)}, s32[160]{0:T(256)}, u32[]{:S(2)}) copy-start(s32[160]{0:T(256)} %param.29) | copy-start | bytes 1924
  127.5 144.1 %copy-start.14 = (bf16[160,1024]{1,0:T(8,128)(2,1)S(1)}, bf16[160,1024]{1,0:T(8,128)(2,1)}, u32[]{:S(2)}) copy-start(bf16[160,1024]{1,0:T(8,128)(2,1)} %param.27) | copy-start | bytes 983044
  127.5 85.4 %all-reduce.6.cloned.1.call-start = ((), (), s32[]{:S(2)}) async-start(), calls=%async_computation.5 | async-start | bytes 524288 | tf_op jit(solution)/shard_map/psum | solution.py:102
  166.1 46.8 %copy-start.3 = (bf16[128,1024]{1,0:T(8,128)(2,1)S(1)}, bf16[128,1024]{1,0:T(8,128)(2,1)}, u32[]{:S(2)}) copy-start(bf16[128,1024]{1,0:T(8,128)(2,1)} %all-reduce.4.cloned.1.call-done) | copy-start | bytes 786436
  170.6 101.0 %all-gather.9.cloned.1.call-start = ((), (), s32[]{:S(2)}) async-start(), calls=%async_computation.6 | async-start | bytes 8650752 | tf_op jit(solution)/shard_map/all_gather | solution.py:107
  214.7 198.7 %all-gather.13.cloned.1.call-start = ((), (), s32[]{:S(2)}) async-start(), calls=%async_computation.9 | async-start | bytes 9830400 | tf_op jit(solution)/shard_map/all_gather | solution.py:133
  216.8 59.8 %copy-start.5 = (bf16[8,1024]{1,0:T(8,128)(2,1)S(1)}, bf16[8,1024]{1,0:T(8,128)(2,1)}, u32[]{:S(2)}) copy-start(bf16[8,1024]{1,0:T(8,128)(2,1)} %param.31) | copy-start | bytes 49156
  216.8 59.8 %copy-start.11 = (s32[160]{0:T(256)S(1)}, s32[160]{0:T(256)}, u32[]{:S(2)}) copy-start(s32[160]{0:T(256)} %param.30) | copy-start | bytes 1924
  216.8 60.2 %copy-start.6 = (f32[1024]{0:T(1024)S(1)}, f32[1024]{0:T(1024)}, u32[]{:S(2)}) copy-start(f32[1024]{0:T(1024)} %param.32) | copy-start | bytes 12292
  334.5 78.9 %copy-start.12 = (bf16[1,1024,512]{2,1,0:T(8,128)(2,1)S(1)}, bf16[1,1024,512]{2,1,0:T(8,128)(2,1)}, u32[]{:S(2)}) copy-start(bf16[1,1024,512]{2,1,0:T(8,128)(2,1)} %param.36) | copy-start | bytes 3145732
  337.0 100.0 %copy-start.13 = (bf16[1,1024,512]{2,1,0:T(8,128)(2,1)S(1)}, bf16[1,1024,512]{2,1,0:T(8,128)(2,1)}, u32[]{:S(2)}) copy-start(bf16[1,1024,512]{2,1,0:T(8,128)(2,1)} %param.37) | copy-start | bytes 3145732
  337.0 210.9 %reduce-scatter.2.cloned.1.call-start = ((), (), s32[]{:S(2)}) async-start(), calls=%async_computation.7 | async-start | bytes 9830400 | tf_op jit(solution)/shard_map/reduce_scatter | solution.py:142
  470.0 89.5 %copy-start.8 = (f32[160,2]{0,1:T(2,128)S(1)}, f32[160,2]{0,1:T(2,128)}, u32[]{:S(2)}) copy-start(f32[160,2]{0,1:T(2,128)} %param.34) | copy-start | bytes 3844
  551.9 35.9 %all-to-all-start.1 = ((bf16[32,30,1024]{2,1,0:T(8,128)(2,1)}), bf16[32,30,1024]{2,1,0:T(8,128)(2,1)S(1)}, u32[]{:S(2)}, u32[]{:S(2)}) async-start(bf16[32,30,1024]{2,1,0:T(8,128)(2,1)} %copy.65), calls=%async_computation.2 | async-start | bytes 4194304 | tf_op jit(solution)/shard_map/all_to_all | solution.py:145
  592.5 11.9 %copy-start.1 = (bf16[1024,1024]{1,0:T(8,128)(2,1)S(1)}, bf16[1024,1024]{1,0:T(8,128)(2,1)}, u32[]{:S(2)}) copy-start(bf16[1024,1024]{1,0:T(8,128)(2,1)} %param.26) | copy-start | bytes 6291460
Sparse Core Ops, SparseCore 0:
  21.9 48.4 all-gather.6
  73.2 43.2 all-gather.10
  127.7 38.3 all-reduce.3
  170.8 42.0 all-reduce.5
  215.6 56.0 all-gather.8
  337.1 76.2 all-gather.12
  470.1 77.7 reduce-scatter.1
where the time goes:
time: 618 us; the launch traced here: 611 us
  waiting for transfers between devices  401 us (65%)
  matrix products  66.1 us (11%)
  local copies, waits for them, and re-layouts  63.5 us (10%)
  blocking collectives  45 us (7%)
  between operations  14.7 us (2%)
  other arithmetic  12.3 us (2%)
  starting transfers between devices  8.73 us (1%)
    reduce_scatter x1, waiting for transfers between devices, per_device(): lax.psum_scatter(partial_out.astype(jnp.bfloat16), 'exp', scatter_dimensi...  77.9 us
    all_gather x1, waiting for transfers between devices, per_device(): pooled = lax.all_gather(grouped, 'exp', axis=2, tiled=True)  75.9 us
    all_gather x1, waiting for transfers between devices, per_device(): block_rows = lax.all_gather(coarse_new, 'seq', axis=0, tiled=True)  54.8 us
    all_gather x1, waiting for transfers between devices, per_device(): key_piece = lax.all_gather(key_rows, 'seq', axis=0, tiled=True)  47.7 us
    psum x1, waiting for transfers between devices, per_device(): lax.psum(mlp_part.astype(jnp.bfloat16), 'exp').astype(jnp.float32)  42.2 us
    psum x1, waiting for transfers between devices, per_device(): lax.psum(attn_part.astype(jnp.bfloat16), 'exp').astype(jnp.float32)  38.5 us
    all_gather x1, waiting for transfers between devices, per_device(): value_piece = lax.all_gather(value_rows, 'seq', axis=0, tiled=True)  35.8 us
    all_to_all x1, blocking collectives, per_device(): lax.all_to_all(outgoing, 'seq', split_axis=0, concat_axis=0, tiled=True)  33.4 us
  transfers between devices with their start and end apart: 8, of which 8 were waited for; matrix products, arithmetic and copies ran while one was open for 2% of the time, Pallas kernels for 0%

commit v1 on v0

v1 whole, which is shorter than its diff:
```python
import math

import jax
import jax.numpy as jnp
from jax import lax
from jax.experimental import pallas as pl
from jax.experimental.pallas import tpu as pltpu
from jax.sharding import PartitionSpec as P

EPSILON = 1e-06
BF = jnp.bfloat16
F32 = jnp.float32
VMEM = 56 * 1024 * 1024

N_SEQ = 32
N_EXP = 4
ROWS = 128
D = 1024
HEADS = 4
HD = 64
FINE = 160
EXPERTS = 16
SLOTS = 32
PSLOTS = 16
QUADS = [[4 * a + b for b in range(4)] for a in range(8)]
SWAP = [(i, i ^ 1) for i in range(N_SEQ)]


def call(kernel, out_shape, *args, flops=0, nbytes=0, smem=(), **kw):
    space = [
        pl.BlockSpec(memory_space=pltpu.SMEM if i in smem else pltpu.VMEM) for i in range(len(args))
    ]
    outs = jax.tree.map(lambda _: pl.BlockSpec(memory_space=pltpu.VMEM), out_shape)
    return pl.pallas_call(
        kernel,
        out_shape=out_shape,
        in_specs=space,
        out_specs=outs,
        compiler_params=pltpu.CompilerParams(vmem_limit_bytes=VMEM),
        cost_estimate=pl.CostEstimate(flops=flops, bytes_accessed=nbytes, transcendentals=0),
        **kw,
    )(*args)


def sds(shape, dtype):
    return jax.ShapeDtypeStruct(shape, dtype)


def dot(a, b):
    return jnp.dot(a, b, preferred_element_type=F32)


def dot_nt(a, b):
    return lax.dot_general(a, b, (((1,), (1,)), ((), ())), preferred_element_type=F32)


def iota(shape, dim):
    return lax.broadcasted_iota(jnp.int32, shape, dim)


def rms(x, gain):
    return x * lax.rsqrt(jnp.mean(x * x, axis=-1, keepdims=True) + EPSILON) * gain


def hot(cond):
    return jnp.where(cond, 1.0, 0.0).astype(BF)


def route_kernel(pd_ref, pdt_ref, prow_ref, ids_ref, idst_ref, pidx_ref, didx_ref, didxt_ref, req_ref):
    before = hot(iota((FINE, FINE), 0) > iota((FINE, FINE), 1))
    beforet = hot(iota((FINE, FINE), 0) < iota((FINE, FINE), 1))
    pd, pdt = pd_ref[...], pdt_ref[...]
    member = hot(pd == iota((FINE, N_SEQ), 1))
    rank = jnp.sum(member.astype(F32) * dot(before, member), axis=1, keepdims=True)
    pidx_ref[...] = pd * PSLOTS + rank.astype(jnp.int32)
    membert = hot(pdt == iota((N_SEQ, FINE), 0))
    rankt = jnp.sum(membert.astype(F32) * dot(membert, beforet), axis=0, keepdims=True)
    pidxt = pdt * PSLOTS + rankt.astype(jnp.int32)
    wanted = hot(pidxt == iota((N_SEQ * PSLOTS, FINE), 0))
    rows = jnp.broadcast_to(prow_ref[...].astype(F32), (FINE, ROWS)).astype(BF)
    req_ref[...] = dot(wanted, rows).astype(BF).reshape(N_SEQ, PSLOTS, ROWS)
    m = [hot(ids_ref[:, k : k + 1] == iota((FINE, EXPERTS), 1)) for k in range(2)]
    ahead = dot(before, m[0] + m[1])
    mt = [hot(idst_ref[k : k + 1, :] == iota((EXPERTS, FINE), 0)) for k in range(2)]
    aheadt = dot(mt[0] + mt[1], beforet)
    for k in range(2):
        r = jnp.sum(m[k].astype(F32) * ahead, axis=1, keepdims=True)
        didx_ref[:, k : k + 1] = ids_ref[:, k : k + 1] * SLOTS + r.astype(jnp.int32)
        rt = jnp.sum(mt[k].astype(F32) * aheadt, axis=0, keepdims=True)
        didxt_ref[k : k + 1, :] = idst_ref[k : k + 1, :] * SLOTS + rt.astype(jnp.int32)


def qkv_kernel(feats_ref, gain_ref, w_ref, req_ref, q_ref, kv_ref):
    x = jnp.concatenate([feats_ref[c].astype(F32) for c in range(N_EXP)], axis=1)
    normed = rms(x, gain_ref[...]).astype(BF)
    proj = [dot(normed, w_ref[i]) for i in range(3)]
    for h in range(HEADS):
        piece = [p[:, h * HD : (h + 1) * HD] for p in proj]
        q, k = [
            v * lax.rsqrt(jnp.mean(v * v, axis=-1, keepdims=True) + EPSILON) for v in piece[:2]
        ]
        q_ref[h] = jnp.concatenate([q, jnp.zeros_like(q)], axis=1).astype(BF)
        kv = jnp.concatenate([k, piece[2]], axis=1).astype(BF)
        for t in range(h, N_SEQ, HEADS):
            kv_ref[t, 0:ROWS, :] = kv
    kv_ref[:, ROWS : ROWS + PSLOTS, :] = req_ref[...]


def attn_kernel(scale_ref, q_ref, kv_ref, out_ref):
    kv = kv_ref[:, 0:ROWS, :].reshape(N_SEQ * ROWS, 2 * HD)
    vones = jnp.where(iota(kv.shape, 1) < HD, jnp.ones_like(kv), kv)
    c = scale_ref[0, 0]
    for b in range(4):
        s = dot_nt(q_ref[b], kv)
        top = jnp.max(s, axis=-1, keepdims=True)
        p = jnp.exp2((s - top) * c).astype(BF)
        o = dot(p, vones)
        out_ref[b] = (o[:, HD:] / o[:, :HD]).astype(BF)


def proj_kernel(att_ref, w_ref, out_ref):
    acc = dot(att_ref[0], w_ref[0:HD, :])
    for h in range(1, HEADS):
        acc = acc + dot(att_ref[h], w_ref[h * HD : (h + 1) * HD, :])
    out_ref[...] = acc.astype(BF)


def mixed_kernel(y_ref, parts_ref, feats_ref, gain_ref, mixed_ref, normed_ref):
    start = pl.multiple_of(y_ref[0, 0] * 32, 32)
    x = jnp.concatenate(
        [feats_ref[c, pl.ds(start, 32), :].astype(F32) for c in range(N_EXP)], axis=1
    )
    total = parts_ref[0].astype(F32)
    for c in range(1, N_EXP):
        total = total + parts_ref[c].astype(F32)
    mixed = x + total
    mixed_ref[...] = mixed
    normed_ref[...] = rms(mixed, gain_ref[...]).astype(BF)


def mlp_kernel(x_ref, win_ref, wout_ref, out_ref):
    inner = jax.nn.gelu(dot(x_ref[...], win_ref[...])).astype(BF)
    out_ref[...] = dot(inner, wout_ref[...]).astype(BF)


def coarse_kernel(parts_ref, mixed_ref, out_ref):
    total = parts_ref[0].astype(F32)
    for c in range(1, N_EXP):
        total = total + parts_ref[c].astype(F32)
    out_ref[...] = (mixed_ref[...] + total).astype(BF)


def serve_kernel(kv_ref, coarse_ref, out_ref):
    req = kv_ref[:, ROWS : ROWS + PSLOTS, :].reshape(N_SEQ * PSLOTS, ROWS)
    chosen = hot(req.astype(F32) == iota(req.shape, 1).astype(F32))
    out_ref[...] = dot(chosen, coarse_ref[...]).astype(BF)


def fine_kernel(rows_ref, pidx_ref, fine_ref, oct_ref, table_ref, gain_ref, didxt_ref, sum_ref, out_ref):
    pick = hot(pidx_ref[...] == iota((FINE, N_SEQ * PSLOTS), 1))
    parents = dot(pick, rows_ref[...])
    octs = dot(hot(oct_ref[...] == iota((FINE, 8), 1)), table_ref[...])
    fine_sum = fine_ref[...].astype(F32) + parents + octs
    sum_ref[...] = fine_sum
    normed = rms(fine_sum, gain_ref[...]).astype(BF)
    slot = iota((EXPERTS * SLOTS, FINE), 0)
    place = hot((didxt_ref[0:1, :] == slot) | (didxt_ref[1:2, :] == slot))
    out_ref[...] = dot(place, normed).astype(BF)


def ffn_kernel(x1_ref, x2_ref, gate_ref, up_ref, down_ref, o1_ref, o2_ref, a1, a2):
    j = pl.program_id(0)
    for x_ref, a in ((x1_ref, a1), (x2_ref, a2)):
        x = x_ref[...]
        g = dot(x, gate_ref[0])
        u = dot(x, up_ref[0])
        act = (0.5 * g * (1.0 + jnp.tanh(0.5 * g)) * u).astype(BF)
        part = dot_nt(act, down_ref[0])

        @pl.when(j == 0)
        def _():
            a[...] = part

        @pl.when(j > 0)
        def _():
            a[...] += part

    @pl.when(j == N_EXP - 1)
    def _():
        o1_ref[...] = a1[...]
        o2_ref[...] = a2[...].astype(BF)


def ffn(x1, x2, gate, up, down):
    n = EXPERTS * SLOTS
    whole = pl.BlockSpec((n, D), lambda j: (0, 0))
    piece = pl.BlockSpec((1, D, 512), lambda j: (j, 0, 0))
    return pl.pallas_call(
        ffn_kernel,
        grid=(N_EXP,),
        in_specs=[whole, whole, piece, piece, piece],
        out_specs=[whole, whole],
        out_shape=[sds((n, D), F32), sds((n, D), BF)],
        scratch_shapes=[pltpu.VMEM((n, D), F32), pltpu.VMEM((n, D), F32)],
        compiler_params=pltpu.CompilerParams(vmem_limit_bytes=VMEM),
        cost_estimate=pl.CostEstimate(
            flops=2 * 2 * n * D * 2048 * 3, bytes_accessed=18 << 20, transcendentals=0
        ),
    )(x1, x2, gate, up, down)


def combine_kernel(ret_ref, didx_ref, gates_ref, sum_ref, out_ref):
    ret = ret_ref[...]
    total = sum_ref[...]
    for k in range(2):
        pick = hot(didx_ref[:, k : k + 1] == iota((FINE, EXPERTS * SLOTS), 1))
        total = total + gates_ref[:, k : k + 1] * dot(pick, ret)
    out_ref[...] = total.astype(BF)


def per_device(
    coarse_in,
    norm1_gain,
    qkv_weight,
    head_scale,
    out_weight,
    norm2_gain,
    mlp_in,
    mlp_out,
    fine_in,
    parent_device,
    parent_row,
    octant,
    octant_table,
    norm3_gain,
    expert_ids,
    expert_gates,
    gate_weight,
    up_weight,
    down_weight,
):
    s = lax.axis_index("seq")
    y = lax.axis_index("exp")
    gate = lax.all_gather(gate_weight, "exp", axis=0, tiled=True)
    up = lax.all_gather(up_weight, "exp", axis=0, tiled=True)
    down = lax.all_gather(down_weight, "exp", axis=0, tiled=True)

    pidx, didx, didxt, req = call(
        route_kernel,
        [
            sds((FINE, 1), jnp.int32),
            sds((FINE, 2), jnp.int32),
            sds((2, FINE), jnp.int32),
            sds((N_SEQ, PSLOTS, ROWS), BF),
        ],
        parent_device,
        parent_device.reshape(1, FINE),
        parent_row.reshape(FINE, 1),
        expert_ids,
        expert_ids.T,
    )
    feats = lax.all_gather(coarse_in, "exp", axis=0, tiled=False)
    q, kv = call(
        qkv_kernel,
        [sds((HEADS, ROWS, 2 * HD), BF), sds((N_SEQ, ROWS + PSLOTS, 2 * HD), BF)],
        feats,
        norm1_gain.reshape(1, D),
        qkv_weight,
        req,
    )
    q = lax.all_to_all(q, "seq", 0, 0, axis_index_groups=QUADS, tiled=True)
    kv = lax.all_to_all(kv, "seq", 0, 0, tiled=True)
    scale = lax.dynamic_slice(head_scale, (s % 4,), (1,)) * (math.log2(math.e) / math.sqrt(HD))
    att = call(
        attn_kernel, sds((HEADS, ROWS, HD), BF), scale.reshape(1, 1), q, kv, smem=(0,)
    )
    att = lax.all_to_all(att, "seq", 0, 0, axis_index_groups=QUADS, tiled=True)
    part = call(proj_kernel, sds((ROWS, D), BF), att, out_weight)
    parts = lax.all_to_all(part.reshape(N_EXP, 32, D), "exp", 0, 0, tiled=True)
    mixed, normed2 = call(
        mixed_kernel,
        [sds((32, D), F32), sds((32, D), BF)],
        y.astype(jnp.int32).reshape(1, 1),
        parts,
        feats,
        norm2_gain.reshape(1, D),
        smem=(0,),
    )
    normed2 = lax.all_gather(normed2, "exp", axis=0, tiled=True)
    part = call(mlp_kernel, sds((ROWS, D), BF), normed2, mlp_in, mlp_out)
    parts = lax.all_to_all(part.reshape(N_EXP, 32, D), "exp", 0, 0, tiled=True)
    rows = call(coarse_kernel, sds((32, D), BF), parts, mixed)
    coarse_new = lax.all_gather(rows, "exp", axis=0, tiled=True)
    served = call(serve_kernel, sds((N_SEQ * PSLOTS, D), BF), kv, coarse_new)
    served = lax.all_to_all(served, "seq", 0, 0, tiled=True)
    fine_sum, outgoing = call(
        fine_kernel,
        [sds((FINE, D), F32), sds((EXPERTS * SLOTS, D), BF)],
        served,
        pidx,
        fine_in,
        octant.reshape(FINE, 1),
        octant_table,
        norm3_gain.reshape(1, D),
        didxt,
    )
    mine = lax.all_to_all(outgoing, "seq", 0, 0, tiled=True)
    other = lax.ppermute(mine, "seq", SWAP)
    part_mine, part_other = ffn(mine, other, gate, up, down)
    from_other = lax.ppermute(part_other, "seq", SWAP)
    result = (part_mine + from_other.astype(F32)).astype(BF)
    returned = lax.all_to_all(result, "seq", 0, 0, tiled=True)
    fine_out = call(
        combine_kernel, sds((FINE, D), BF), returned, didx, expert_gates, fine_sum
    )
    return (coarse_new, fine_out)


def solution(mesh):
    return jax.shard_map(
        per_device,
        mesh=mesh,
        in_specs=(
            P("seq", "exp"),
            P(),
            P(None, None, "exp"),
            P("exp"),
            P("exp", None),
            P(),
            P(None, "exp"),
            P("exp", None),
            P(("seq", "exp"), None),
            P(("seq", "exp"), None),
            P(("seq", "exp")),
            P(("seq", "exp")),
            P(),
            P(),
            P(("seq", "exp"), None),
            P(("seq", "exp"), None),
            P("seq", None, "exp"),
            P("seq", None, "exp"),
            P("seq", None, "exp"),
        ),
        out_specs=(P("seq", None), P(("seq", "exp"), None)),
        check_vma=False,
    )
```

time: 618 us -> 259 us (0.42)
  waiting for transfers between devices: 401 us -> 66.3 us
  matrix products: 66.1 us -> 0 us
  local copies, waits for them, and re-layouts: 63.5 us -> 11.5 us
  Pallas kernels: 0 us -> 50.7 us
  blocking collectives: 45 us -> 84.2 us
  starting transfers between devices: 8.73 us -> 27.9 us
  other arithmetic: 12.3 us -> 2.95 us
    all_gather x4 -> x3, waiting for transfers between devices: 214 us -> 0.02 us  [the longest x1 0.01 us: per_device(): down = lax.all_gather(down_weight, 'exp', axis=0, tiled=True)]
    psum x2 -> x0, waiting for transfers between devices: 80.7 us -> none  [the longest x1 42.2 us: per_device(): lax.psum(mlp_part.astype(jnp.bfloat16), 'exp').astype(jnp.float32)]
    reduce_scatter x1 -> x0, waiting for transfers between devices: 77.9 us -> none  [per_device(): lax.psum_scatter(partial_out.astype(jnp.bfloat16), 'exp', scatter_dimensi...]
    dot_general x9 -> x0, matrix products: 66.1 us -> none  [the longest x1 23.6 us: per_device(): jnp.einsum('shrd,hdf->shrf', pooled, up_weight, preferred_element_type=jn...]
    pallas_call x0 -> x11, Pallas kernels: none -> 50.7 us  [the longest x10 29.8 us: call(): pl.pallas_call(kernel, out_shape=out_shape, in_specs=space, out_specs=out...]
    all_to_all x1 -> x4, waiting for transfers between devices: 28.2 us -> 59 us  [the longest x1 17.1 us: per_device(): kv = lax.all_to_all(kv, 'seq', 0, 0, tiled=True)]
    all_gather x1 -> x3, blocking collectives: 11.6 us -> 36.1 us  [the longest x1 12.3 us: per_device(): normed2 = lax.all_gather(normed2, 'exp', axis=0, tiled=True)]
    scatter x2 -> x0, local copies, waits for them, and re-layouts: 21.4 us -> none  [per_device(): outgoing = jnp.zeros((EXPERTS, CAP, width), jnp.bfloat16).at[flat_ids, ex...]
  transfers between devices with their start and end apart: 8 -> 9, of which waited for: 8 -> 6; matrix products, arithmetic and copies ran while one was open for 2% -> 2% of each run, Pallas kernels for 0% -> 10%
where the time goes in v1:
time: 259 us; the launch traced here: 258 us
  blocking collectives  84.2 us (33%)
  waiting for transfers between devices  66.3 us (26%)
  Pallas kernels  50.7 us (20%)
  starting transfers between devices  27.9 us (11%)
  between operations  14.5 us (6%)
  local copies, waits for them, and re-layouts  11.5 us (4%)
  other arithmetic  2.95 us (1%)
    pallas_call x10, Pallas kernels, call(): pl.pallas_call(kernel, out_shape=out_shape, in_specs=space, out_specs=out...  29.8 us
    pallas_call x1, Pallas kernels, ffn(): pl.pallas_call(ffn_kernel, grid=(N_EXP,), in_specs=[whole, whole, piece,...  20.9 us
    all_to_all x1, blocking collectives, per_device(): mine = lax.all_to_all(outgoing, 'seq', 0, 0, tiled=True)  20.9 us
    all_to_all x1, waiting for transfers between devices, per_device(): kv = lax.all_to_all(kv, 'seq', 0, 0, tiled=True)  17.1 us
    all_to_all x1, waiting for transfers between devices, per_device(): served = lax.all_to_all(served, 'seq', 0, 0, tiled=True)  16.1 us
    all_to_all x1, waiting for transfers between devices, per_device(): returned = lax.all_to_all(result, 'seq', 0, 0, tiled=True)  16.1 us
    all_gather x1, blocking collectives, per_device(): normed2 = lax.all_gather(normed2, 'exp', axis=0, tiled=True)  12.3 us
    all_gather x1, blocking collectives, per_device(): feats = lax.all_gather(coarse_in, 'exp', axis=0, tiled=False)  11.9 us
  transfers between devices with their start and end apart: 9, of which 6 were waited for; matrix products, arithmetic and copies ran while one was open for 2% of the time, Pallas kernels for 10%

profile of v1, /device:TPU:1, one launch (start us, length us, event | category | flops | bytes accessed | tf_op | source)
XLA Modules:
  0.0 258.1 jit_solution(10815580158639569114)
XLA Ops:
  11.7 2.1 shard_map.194
  13.8 11.9 %all-gather = bf16[512,256]{1,0:T(8,128)(2,1)} all-gather(bf16[128,256]{1,0:T(8,128)(2,1)S(1)} %copy-done.6), channel_id=2, replica_groups=mesh['seq'=32,'exp'=4] {'exp'}, dimensions={0}, use_global_device_ids=true | all-gather | bytes 327680 | tf_op jit(solution)/shard_map/all_gather | solution.py:262
  25.7 4.0 %shard_map.195 = (bf16[4,128,128]{2,1,0:T(8,128)(2,1)}, bf16[32,144,128]{2,1,0:T(8,128)(2,1)}) custom-call(bf16[4,128,256]{2,1,0:T(8,128)(2,1)} %bitcast.21, f32[1,1024]{1,0:T(1,128)} %bitcast.29, bf16[3,1024,256]{2,1,0:T(8,128)(2,1)} %w_ref.2, bf16[32,16,128]{2,1,0:T(8,128)(2,1)} %get-tuple-element.14.req_ref), custom_call_target="tpu_custom_call" | custom-call | tf_op jit(solution)/shard_map/pallas_call | solution.py:34
  29.7 11.4 %all_to_all.58.q_ref = bf16[4,128,128]{2,1,0:T(8,128)(2,1)} all-to-all(bf16[4,128,128]{2,1,0:T(8,128)(2,1)} %get-tuple-element.15), channel_id=1, replica_groups={{0,4,8,12},{16,20,24,28},{32,36,40,44},{48,52,56,60},{64,68,72,76},{80,..., dimensions={0} | all-to-all | bytes 262144 | tf_op jit(solution)/shard_map/all_to_all | solution.py:271
  41.1 8.6 %all-to-all-start.1 = ((bf16[32,144,128]{2,1,0:T(8,128)(2,1)}), bf16[32,144,128]{2,1,0:T(8,128)(2,1)S(1)}, u32[]{:S(2)}, u32[]{:S(2)}) async-start(bf16[32,144,128]{2,1,0:T(8,128)(2,1)} %get-tuple-element.16), calls=%async_computation.1 | async-start | bytes 2359296 | tf_op jit(solution)/shard_map/all_to_all | solution.py:272
  50.9 17.1 %all-to-all-done.1.kv_ref = bf16[32,144,128]{2,1,0:T(8,128)(2,1)S(1)} async-done(((bf16[32,144,128]{2,1,0:T(8,128)(2,1)}), bf16[32,144,128]{2,1,0:T(8,128)(2,1)S(1)}, u32[]{:S(2)}, u32[]{:S(2)}) %all-to-all-start.1) | async-done | bytes 1179680 | tf_op jit(solution)/shard_map/all_to_all | solution.py:272
  68.0 1.0 copy-done
  69.0 5.4 %shard_map.196 = bf16[4,128,64]{2,1,0:T(8,128)(2,1)} custom-call(f32[1,1]{1,0:T(1,128)} %bitcast.1.scale_ref, bf16[4,128,128]{2,1,0:T(8,128)(2,1)} %all_to_all.58.q_ref, bf16[32,144,128]{2,1,0:T(8,128)(2,1)} %copy-done), custom_call_target="tpu_custom_call" | custom-call | tf_op jit(solution)/shard_map/pallas_call | solution.py:34
  74.4 1.0 copy.32
  75.4 6.3 %all_to_all.59 = bf16[4,128,64]{1,2,0:T(8,128)(2,1)S(1)} all-to-all(bf16[4,128,64]{1,2,0:T(8,128)(2,1)S(1)} %copy.32), channel_id=1, replica_groups={{0,4,8,12},{16,20,24,28},{32,36,40,44},{48,52,56,60},{64,68,72,76},{80,..., dimensions={0} | all-to-all | bytes 131072 | tf_op jit(solution)/shard_map/all_to_all | solution.py:277
  82.5 2.2 shard_map.197
  84.7 3.8 %all-to-all-start.3 = ((bf16[4,32,1024]{2,1,0:T(8,128)(2,1)}), bf16[4,32,1024]{2,1,0:T(8,128)(2,1)S(1)}, u32[]{:S(2)}, u32[]{:S(2)}) async-start(bf16[4,32,1024]{2,1,0:T(8,128)(2,1)} %bitcast.23), calls=%async_computation.3 | async-start | bytes 524288 | tf_op jit(solution)/shard_map/all_to_all | solution.py:279
  88.5 9.6 %all-to-all-done.3.parts_ref = bf16[4,32,1024]{2,1,0:T(8,128)(2,1)S(1)} async-done(((bf16[4,32,1024]{2,1,0:T(8,128)(2,1)}), bf16[4,32,1024]{2,1,0:T(8,128)(2,1)S(1)}, u32[]{:S(2)}, u32[]{:S(2)}) %all-to-all-start.3) | async-done | bytes 262176 | tf_op jit(solution)/shard_map/all_to_all | solution.py:279
  98.8 1.8 shard_map.198
  100.6 12.3 %all_gather.23.x_ref = bf16[128,1024]{1,0:T(8,128)(2,1)} all-gather(bf16[32,1024]{1,0:T(8,128)(2,1)} %get-tuple-element.17), channel_id=1, replica_groups=mesh['seq'=32,'exp'=4] {'exp'}, dimensions={0}, use_global_device_ids=true | all-gather | bytes 327680 | tf_op jit(solution)/shard_map/all_gather | solution.py:289
  112.9 3.8 %shard_map.199 = bf16[128,1024]{1,0:T(8,128)(2,1)} custom-call(bf16[128,1024]{1,0:T(8,128)(2,1)} %all_gather.23.x_ref, bf16[1024,1024]{1,0:T(8,128)(2,1)} %win_ref.1, bf16[1024,1024]{1,0:T(8,128)(2,1)} %wout_ref.1), custom_call_target="tpu_custom_call" | custom-call | tf_op jit(solution)/shard_map/pallas_call | solution.py:34
  116.7 9.6 %all_to_all.60.parts_ref = bf16[4,32,1024]{2,1,0:T(8,128)(2,1)} all-to-all(bf16[4,32,1024]{2,1,0:T(8,128)(2,1)} %bitcast.24), channel_id=1, replica_groups=mesh['seq'=32,'exp'=4] {'exp'}, dimensions={0} | all-to-all | bytes 524288 | tf_op jit(solution)/shard_map/all_to_all | solution.py:291
  126.4 1.7 shard_map.200
  128.0 11.9 %all_gather.24.coarse_ref = bf16[128,1024]{1,0:T(8,128)(2,1)} all-gather(bf16[32,1024]{1,0:T(8,128)(2,1)} %shard_map.200), channel_id=1, replica_groups=mesh['seq'=32,'exp'=4] {'exp'}, dimensions={0}, use_global_device_ids=true | all-gather | bytes 327680 | tf_op jit(solution)/shard_map/all_gather | solution.py:293
  139.9 2.7 %shard_map.201 = bf16[512,1024]{1,0:T(8,128)(2,1)} custom-call(bf16[32,144,128]{2,1,0:T(8,128)(2,1)} %copy-done, bf16[128,1024]{1,0:T(8,128)(2,1)} %all_gather.24.coarse_ref), custom_call_target="tpu_custom_call" | custom-call | tf_op jit(solution)/shard_map/pallas_call | solution.py:34
  142.6 11.0 %all-to-all-start.5 = ((bf16[32,16,1024]{2,1,0:T(8,128)(2,1)}), bf16[32,16,1024]{2,1,0:T(8,128)(2,1)S(1)}, u32[]{:S(2)}, u32[]{:S(2)}) async-start(bf16[32,16,1024]{2,1,0:T(8,128)(2,1)} %bitcast.20), calls=%async_computation.5 | async-start | bytes 2097152 | tf_op jit(solution)/shard_map/all_to_all | solution.py:295
  154.4 16.1 %all-to-all-done.5 = bf16[32,16,1024]{2,1,0:T(8,128)(2,1)S(1)} async-done(((bf16[32,16,1024]{2,1,0:T(8,128)(2,1)}), bf16[32,16,1024]{2,1,0:T(8,128)(2,1)S(1)}, u32[]{:S(2)}, u32[]{:S(2)}) %all-to-all-start.5) | async-done | bytes 1048608 | tf_op jit(solution)/shard_map/all_to_all | solution.py:295
  170.5 1.0 copy-done.1
  171.5 3.4 %shard_map.202 = (f32[160,1024]{1,0:T(8,128)}, bf16[512,1024]{1,0:T(8,128)(2,1)}) custom-call(bf16[512,1024]{1,0:T(8,128)(2,1)} %bitcast.18, s32[160,1]{1,0:T(8,128)} %get-tuple-element.19.pidx_ref, bf16[160,1024]{1,0:T(8,128)(2,1)} %fine_ref.1, s32[160,1]{1,0:T(8,128)} %copy.34.oct_ref, bf16[8,1024]{1,0:T(8,128)(2,1)} %table_ref.1, f32[1,1024]{1,0:T(1,128)} %bitcast.31, ...), custom_call_target="tpu_custom_call" | custom-call | tf_op jit(solution)/shard_map/pallas_call | solution.py:34
  174.9 20.9 %all_to_all.61 = bf16[32,16,1024]{2,1,0:T(8,128)(2,1)S(1)} all-to-all(bf16[32,16,1024]{2,1,0:T(8,128)(2,1)} %bitcast.27), channel_id=1, replica_groups=mesh['seq'=32,'exp'=4] {'seq'}, dimensions={0} | all-to-all | bytes 2097152 | tf_op jit(solution)/shard_map/all_to_all | solution.py:307
  195.9 2.5 collective-permute-done.x2_ref
  199.4 20.9 %shard_map.203 = (f32[512,1024]{1,0:T(8,128)}, bf16[512,1024]{1,0:T(8,128)(2,1)}) custom-call(bf16[512,1024]{1,0:T(8,128)(2,1)} %bitcast.26, bf16[512,1024]{1,0:T(8,128)(2,1)} %copy-done.12, bf16[4,1024,512]{2,1,0:T(8,128)(2,1)} %all-gather.5.cloned.1.call-done.gate_ref, bf16[4,1024,512]{2,1,0:T(8,128)(2,1)} %all-gather.7.cloned.1.call-done.up_ref, ...), custom_call_target="tpu_custom_call" | custom-call | flops 12884901888 | bytes 18874368 | tf_op jit(solution)/shard_map/pallas_call | solution.py:198
  220.4 2.7 %collective-permute-done.1 = bf16[512,1024]{1,0:T(8,128)(2,1)S(1)} collective-permute-done((bf16[512,1024]{1,0:T(8,128)(2,1)}, bf16[512,1024]{1,0:T(8,128)(2,1)S(1)}, u32[]{:S(2)}, u32[]{:S(2)}) %collective-permute-start.1) | collective-permute-done | bytes 1048608 | tf_op jit(solution)/shard_map/ppermute | solution.py:310
  223.2 3.0 %add_convert_fusion = bf16[512,1024]{1,0:T(8,128)(2,1)} fusion(f32[512,1024]{1,0:T(8,128)} %get-tuple-element.22, bf16[512,1024]{1,0:T(8,128)(2,1)S(1)} %collective-permute-done.1), kind=kLoop, calls=%fused_computation | loop fusion | flops 1572864 | bytes 4194304 | tf_op jit(solution)/shard_map/convert_element_type | solution.py:311
  226.1 4.1 %all-to-all-start.7 = ((bf16[32,16,1024]{2,1,0:T(8,128)(2,1)}), bf16[32,16,1024]{2,1,0:T(8,128)(2,1)S(1)}, u32[]{:S(2)}, u32[]{:S(2)}) async-start(bf16[32,16,1024]{2,1,0:T(8,128)(2,1)} %bitcast.16), calls=%async_computation.7 | async-start | bytes 2097152 | tf_op jit(solution)/shard_map/all_to_all | solution.py:312
  231.0 16.1 %all-to-all-done.7 = bf16[32,16,1024]{2,1,0:T(8,128)(2,1)S(1)} async-done(((bf16[32,16,1024]{2,1,0:T(8,128)(2,1)}), bf16[32,16,1024]{2,1,0:T(8,128)(2,1)S(1)}, u32[]{:S(2)}, u32[]{:S(2)}) %all-to-all-start.7) | async-done | bytes 1048608 | tf_op jit(solution)/shard_map/all_to_all | solution.py:312
  248.1 2.8 %shard_map.204 = bf16[160,1024]{1,0:T(8,128)(2,1)} custom-call(bf16[512,1024]{1,0:T(8,128)(2,1)} %bitcast.19, s32[160,2]{1,0:T(8,128)} %get-tuple-element.24.didx_ref, f32[160,2]{1,0:T(8,128)} %copy.35.gates_ref, f32[160,1024]{1,0:T(8,128)} %get-tuple-element.25.sum_ref), custom_call_target="tpu_custom_call" | custom-call | tf_op jit(solution)/shard_map/pallas_call | solution.py:34
  (45 shorter events, 10.9 us)
Async XLA Ops:
  7.2 2.3 copy-start.8
  7.2 3.0 %copy-start.10 = (s32[160]{0:T(256)S(1)}, s32[160]{0:T(256)}, u32[]{:S(2)}) copy-start(s32[160]{0:T(256)} %param.29) | copy-start | bytes 1924
  7.2 3.8 %copy-start.7 = (s32[160,2]{0,1:T(2,128)S(1)}, s32[160,2]{0,1:T(2,128)}, u32[]{:S(2)}) copy-start(s32[160,2]{0,1:T(2,128)} %param.33) | copy-start | bytes 3844
  7.2 6.6 %copy-start.6 = (bf16[128,256]{1,0:T(8,128)(2,1)S(1)}, bf16[128,256]{1,0:T(8,128)(2,1)}, u32[]{:S(2)}) copy-start(bf16[128,256]{1,0:T(8,128)(2,1)} %param.19) | copy-start | bytes 196612
  7.2 191.2 %all-gather.5.cloned.1.call-start = ((), (), s32[]{:S(2)}) async-start(), calls=%async_computation.8 | async-start | bytes 5242880 | tf_op jit(solution)/shard_map/all_gather | solution.py:244
  7.9 190.5 %all-gather.7.cloned.1.call-start = ((), (), s32[]{:S(2)}) async-start(), calls=%async_computation.9 | async-start | bytes 5242880 | tf_op jit(solution)/shard_map/all_gather | solution.py:245
  8.7 189.7 %all-gather.9.cloned.1.call-start = ((), (), s32[]{:S(2)}) async-start(), calls=%async_computation.10 | async-start | bytes 5242880 | tf_op jit(solution)/shard_map/all_gather | solution.py:246
  25.7 24.0 %copy-start.13 = (f32[4]{0:T(128)S(1)}, f32[4]{0:T(128)}, u32[]{:S(2)}) copy-start(f32[4]{0:T(128)} %param.22) | copy-start | bytes 52
  41.1 26.9 %all-to-all-start.1 = ((bf16[32,144,128]{2,1,0:T(8,128)(2,1)}), bf16[32,144,128]{2,1,0:T(8,128)(2,1)S(1)}, u32[]{:S(2)}, u32[]{:S(2)}) async-start(bf16[32,144,128]{2,1,0:T(8,128)(2,1)} %get-tuple-element.16), calls=%async_computation.1 | async-start | bytes 2359296 | tf_op jit(solution)/shard_map/all_to_all | solution.py:272
  68.0 1.0 copy-start
  84.7 13.4 %all-to-all-start.3 = ((bf16[4,32,1024]{2,1,0:T(8,128)(2,1)}), bf16[4,32,1024]{2,1,0:T(8,128)(2,1)S(1)}, u32[]{:S(2)}, u32[]{:S(2)}) async-start(bf16[4,32,1024]{2,1,0:T(8,128)(2,1)} %bitcast.23), calls=%async_computation.3 | async-start | bytes 524288 | tf_op jit(solution)/shard_map/all_to_all | solution.py:279
  98.1 0.7 copy-start.4
  139.9 13.7 %copy-start.11 = (s32[160]{0:T(256)S(1)}, s32[160]{0:T(256)}, u32[]{:S(2)}) copy-start(s32[160]{0:T(256)} %param.30) | copy-start | bytes 1924
  142.6 27.9 %all-to-all-start.5 = ((bf16[32,16,1024]{2,1,0:T(8,128)(2,1)}), bf16[32,16,1024]{2,1,0:T(8,128)(2,1)S(1)}, u32[]{:S(2)}, u32[]{:S(2)}) async-start(bf16[32,16,1024]{2,1,0:T(8,128)(2,1)} %bitcast.20), calls=%async_computation.5 | async-start | bytes 2097152 | tf_op jit(solution)/shard_map/all_to_all | solution.py:295
  170.5 1.0 copy-start.1
  195.7 2.7 %copy-start.5 = (bf16[32,16,1024]{2,1,0:T(8,128)(2,1)}, bf16[32,16,1024]{2,1,0:T(8,128)(2,1)S(1)}, u32[]{:S(2)}) copy-start(bf16[32,16,1024]{2,1,0:T(8,128)(2,1)S(1)} %all_to_all.61) | copy-start | bytes 3145732
  195.7 2.7 %collective-permute-start = (bf16[512,1024]{1,0:T(8,128)(2,1)S(1)}, bf16[512,1024]{1,0:T(8,128)(2,1)S(1)}, u32[]{:S(2)}, u32[]{:S(2)}) collective-permute-start(bf16[512,1024]{1,0:T(8,128)(2,1)S(1)} %bitcast.25), channel_id=1, source_target_pairs={{0,4},{4,0},{8,12},{12,8},{16,20},{20,16},{24,28},{28,24},{32,36},... | collective-permute-start | bytes 3145736 | tf_op jit(solution)/shard_map/ppermute | solution.py:308
  198.4 1.0 copy-start.12
  220.3 2.9 %collective-permute-start.1 = (bf16[512,1024]{1,0:T(8,128)(2,1)}, bf16[512,1024]{1,0:T(8,128)(2,1)S(1)}, u32[]{:S(2)}, u32[]{:S(2)}) collective-permute-start(bf16[512,1024]{1,0:T(8,128)(2,1)} %get-tuple-element.23), channel_id=1, source_target_pairs={{0,4},{4,0},{8,12},{12,8},{16,20},{20,16},{24,28},{28,24},{32,36},... | collective-permute-start | bytes 3145736 | tf_op jit(solution)/shard_map/ppermute | solution.py:310
  226.1 4.1 %copy-start.9 = (f32[160,2]{0,1:T(2,128)S(1)}, f32[160,2]{0,1:T(2,128)}, u32[]{:S(2)}) copy-start(f32[160,2]{0,1:T(2,128)} %param.34) | copy-start | bytes 3844
  226.1 24.8 %copy-start.3 = (bf16[128,1024]{1,0:T(8,128)(2,1)S(1)}, bf16[128,1024]{1,0:T(8,128)(2,1)}, u32[]{:S(2)}) copy-start(bf16[128,1024]{1,0:T(8,128)(2,1)} %all_gather.24.coarse_ref) | copy-start | bytes 786436
  226.1 21.0 %all-to-all-start.7 = ((bf16[32,16,1024]{2,1,0:T(8,128)(2,1)}), bf16[32,16,1024]{2,1,0:T(8,128)(2,1)S(1)}, u32[]{:S(2)}, u32[]{:S(2)}) async-start(bf16[32,16,1024]{2,1,0:T(8,128)(2,1)} %bitcast.16), calls=%async_computation.7 | async-start | bytes 2097152 | tf_op jit(solution)/shard_map/all_to_all | solution.py:312
  247.1 1.0 copy-start.2
Sparse Core Ops, SparseCore 0:
  9.7 51.8 all-gather.4
  63.2 53.5 all-gather.6
  118.5 50.3 all-gather.8

commit v2 on v1

v2 whole, which is shorter than its diff:
```python
import functools
import math

import jax
import jax.numpy as jnp
from jax import lax
from jax.experimental import pallas as pl
from jax.experimental.pallas import tpu as pltpu
from jax.sharding import PartitionSpec as P

EPSILON = 1e-06
BF = jnp.bfloat16
F32 = jnp.float32

N_SEQ = 32
N_EXP = 4
ROWS = 128
D = 1024
HEADS = 4
HD = 64
FINE = 160
EXPERTS = 16
SLOTS = 32
PSLOTS = 16
SIXTEENS = [[16 * a + b for b in range(16)] for a in range(8)]
SWAP = [(i, i ^ 1) for i in range(N_SEQ)]


def nbytes(x):
    return math.prod(x.shape) * x.dtype.itemsize


def call(kernel, out_shape, *args, smem=(), flops=0, spare=6, ready=(), **kw):
    space = [
        pl.BlockSpec(memory_space=pltpu.SMEM if i in smem else pltpu.VMEM) for i in range(len(args))
    ]
    outs = jax.tree.map(lambda _: pl.BlockSpec(memory_space=pltpu.VMEM), out_shape)
    moved = sum(nbytes(a) for a in args) + sum(nbytes(o) for o in jax.tree.leaves(out_shape))
    return pl.pallas_call(
        kernel,
        out_shape=out_shape,
        in_specs=space + [pl.BlockSpec(memory_space=pl.ANY)] * len(ready),
        out_specs=outs,
        compiler_params=pltpu.CompilerParams(vmem_limit_bytes=2 * moved + (spare << 20)),
        cost_estimate=pl.CostEstimate(flops=flops, bytes_accessed=1, transcendentals=0),
        **kw,
    )(*args, *ready)


def sds(shape, dtype):
    return jax.ShapeDtypeStruct(shape, dtype)


def dot(a, b):
    return jnp.dot(a, b, preferred_element_type=F32)


def dot_nt(a, b):
    return lax.dot_general(a, b, (((1,), (1,)), ((), ())), preferred_element_type=F32)


def iota(shape, dim):
    return lax.broadcasted_iota(jnp.int32, shape, dim)


def rms(x, gain):
    return x * lax.rsqrt(jnp.mean(x * x, axis=-1, keepdims=True) + EPSILON) * gain


def hot(cond):
    return jnp.where(cond, 1.0, 0.0).astype(BF)


def upright(row):
    n = row.shape[1]
    return jnp.sum(jnp.where(iota((n, n), 0) == iota((n, n), 1), row, jnp.zeros_like(row)), axis=1, keepdims=True)


def route_kernel(pdt_ref, prow_ref, idst_ref, pidx_ref, didx_ref, didxt_ref, req_ref):
    before = hot(iota((FINE, FINE), 0) < iota((FINE, FINE), 1))
    pdt = pdt_ref[...]
    member = hot(pdt == iota((N_SEQ, FINE), 0))
    rank = jnp.sum(member.astype(F32) * dot(member, before), axis=0, keepdims=True)
    pidxt = pdt.astype(F32) * PSLOTS + rank
    pidx_ref[...] = upright(pidxt).astype(jnp.int32)
    wanted = hot(pidxt == iota((N_SEQ * PSLOTS, FINE), 0).astype(F32))
    rows = jnp.broadcast_to(upright(prow_ref[...].astype(F32)), (FINE, ROWS)).astype(BF)
    req_ref[...] = dot(wanted, rows).astype(BF).reshape(N_SEQ, PSLOTS, ROWS)
    m = [hot(idst_ref[k : k + 1, :] == iota((EXPERTS, FINE), 0)) for k in range(2)]
    ahead = dot(m[0] + m[1], before)
    for k in range(2):
        r = jnp.sum(m[k].astype(F32) * ahead, axis=0, keepdims=True)
        slot = idst_ref[k : k + 1, :].astype(F32) * SLOTS + r
        didxt_ref[k : k + 1, :] = slot.astype(jnp.int32)
        didx_ref[:, k : k + 1] = upright(slot).astype(jnp.int32)


def around(y, k):
    return lax.rem(y - k + N_EXP, N_EXP)


def qkv_kernel(at_ref, f0_ref, f1_ref, f2_ref, f3_ref, gain_ref, w_ref, req_ref, x_ref, q0_ref, q1_ref, q2_ref, q3_ref, kv_ref, xs, qs):
    y, me = at_ref[0, 0], at_ref[0, 1]
    for k, f_ref in enumerate((f0_ref, f1_ref, f2_ref, f3_ref)):
        xs[around(y, k)] = f_ref[...]
    whole = jnp.concatenate([xs[c] for c in range(N_EXP)], axis=1)
    x_ref[...] = whole
    normed = rms(whole.astype(F32), gain_ref[...]).astype(BF)
    proj = [dot(normed, w_ref[i]) for i in range(3)]
    for h in range(HEADS):
        piece = [p[:, h * HD : (h + 1) * HD] for p in proj]
        q, k = [
            v * lax.rsqrt(jnp.mean(v * v, axis=-1, keepdims=True) + EPSILON) for v in piece[:2]
        ]
        qs[h] = jnp.concatenate([q, jnp.zeros_like(q)], axis=1).astype(BF)
        kv = jnp.concatenate([k, piece[2]], axis=1).astype(BF)
        for t in range(h, N_SEQ, HEADS):
            kv_ref[t, 0:ROWS, :] = kv
    kv_ref[:, ROWS : ROWS + PSLOTS, :] = req_ref[...]
    for k, q_ref in enumerate((q0_ref, q1_ref, q2_ref, q3_ref)):
        q_ref[...] = qs[me ^ k]


def attn_kernel(scale_ref, at_ref, q0_ref, q1_ref, q2_ref, q3_ref, kv_ref, out_ref):
    kv = kv_ref[:, 0:ROWS, :].reshape(N_SEQ * ROWS, 2 * HD)
    vones = jnp.where(iota(kv.shape, 1) < HD, jnp.ones_like(kv), kv)
    c = scale_ref[0, 0]
    me = at_ref[0, 1]
    for b, q_ref in enumerate((q0_ref, q1_ref, q2_ref, q3_ref)):
        s = dot_nt(q_ref[...], kv)
        top = jnp.max(s, axis=-1, keepdims=True)
        p = jnp.exp2((s - top) * c).astype(BF)
        o = dot(p, vones)
        o = o[:, HD:] / o[:, :HD]
        half = ROWS // 2
        packed = jnp.concatenate([o[:half], o[half:]], axis=1).astype(BF)
        for z in range(N_EXP):
            out_ref[(me ^ b) * N_EXP + z] = packed


def block_kernel(at_ref, att_ref, x_ref, gain_ref, wo_ref, win_ref, wout_ref, *rest):
    mixed_ref, part_ref, scr, wbuf, sem = rest[-5:]
    copies = [
        pltpu.make_async_copy(src, dst, sem.at[i])
        for i, (src, dst) in enumerate(
            (
                (wo_ref, wbuf.at[0]),
                (win_ref, wbuf.at[1]),
                (wout_ref, wbuf.at[2]),
            )
        )
    ]
    for c in copies:
        c.start()
    heads = []
    for z in range(N_EXP):
        for h in range(HEADS):
            a = att_ref[h * N_EXP + z]
            heads.append(jnp.concatenate([a[:, :HD], a[:, HD:]], axis=0))
    att = jnp.concatenate(heads, axis=1)
    copies[0].wait()
    mixed = x_ref[...].astype(F32) + dot(att, wbuf[0])
    for c in range(N_EXP):
        scr[c] = mixed[:, c * 256 : (c + 1) * 256]
    mixed_ref[...] = scr[at_ref[0, 0]]
    normed = rms(mixed, gain_ref[...]).astype(BF)
    copies[1].wait()
    inner = jax.nn.gelu(dot(normed, wbuf[1])).astype(BF)
    copies[2].wait()
    part = dot(inner, wbuf[2]).astype(BF)
    for c in range(N_EXP):
        part_ref[c] = part[:, c * 256 : (c + 1) * 256]


def block(at, att, x, gain, wo, win, wout, *ready):
    vm = pl.BlockSpec(memory_space=pltpu.VMEM)
    hbm = pl.BlockSpec(memory_space=pl.ANY)
    return pl.pallas_call(
        block_kernel,
        in_specs=[pl.BlockSpec(memory_space=pltpu.SMEM), vm, vm, vm] + [hbm] * (3 + len(ready)),
        out_specs=[vm, vm],
        out_shape=[sds((ROWS, 256), F32), sds((N_EXP, ROWS, 256), BF)],
        scratch_shapes=[
            pltpu.VMEM((N_EXP, ROWS, 256), F32),
            pltpu.VMEM((3, D, D), BF),
            pltpu.SemaphoreType.DMA((3,)),
        ],
        compiler_params=pltpu.CompilerParams(vmem_limit_bytes=58 << 20),
        cost_estimate=pl.CostEstimate(flops=1, bytes_accessed=1, transcendentals=0),
    )(at, att, x, gain, wo, win, wout, *ready)


def coarse_kernel(parts_ref, mixed_ref, out_ref):
    total = parts_ref[0].astype(F32)
    for c in range(1, N_EXP):
        total = total + parts_ref[c].astype(F32)
    out_ref[...] = (mixed_ref[...] + total).astype(BF)


def serve_kernel(at_ref, kv_ref, c0_ref, c1_ref, c2_ref, c3_ref, *rest):
    coarse_ref, out_ref, scr = rest[-3:]
    y = at_ref[0, 0]
    for k, c_ref in enumerate((c0_ref, c1_ref, c2_ref, c3_ref)):
        scr[around(y, k)] = c_ref[...]
    coarse = jnp.concatenate([scr[c] for c in range(N_EXP)], axis=1)
    coarse_ref[...] = coarse
    req = kv_ref[:, ROWS : ROWS + PSLOTS, :].reshape(N_SEQ * PSLOTS, ROWS)
    chosen = hot(req.astype(F32) == iota(req.shape, 1).astype(F32))
    out_ref[...] = dot(chosen, coarse).astype(BF)


def fine_kernel(rows_ref, pidx_ref, fine_ref, oct_ref, table_ref, gain_ref, didxt_ref, *rest):
    sum_ref, out_ref = rest[-2:]
    pick = hot(pidx_ref[...] == iota((FINE, N_SEQ * PSLOTS), 1))
    parents = dot(pick, rows_ref[...])
    octs = dot(hot(upright(oct_ref[...].astype(F32)) == iota((FINE, 8), 1).astype(F32)), table_ref[...])
    fine_sum = fine_ref[...].astype(F32) + parents + octs
    sum_ref[...] = fine_sum
    normed = rms(fine_sum, gain_ref[...]).astype(BF)
    slot = iota((EXPERTS * SLOTS, FINE), 0)
    place = hot((didxt_ref[0:1, :] == slot) | (didxt_ref[1:2, :] == slot))
    out_ref[...] = dot(place, normed).astype(BF)


def ffn_kernel(has_extra, at_ref, x_ref, extra_ref, gate_ref, u0, u1, u2, u3, d0, d1, d2, d3, out_ref, gb, ub, db, sem):
    y = at_ref[0, 0]
    ups, downs = (u0, u1, u2, u3), (d0, d1, d2, d3)
    copies = []
    for j, k in enumerate((0, 1, 3, 2)):
        places = ((gate_ref.at[around(y, k)], gb), (ups[j].at[0], ub), (downs[j].at[0], db))
        copies += [
            pltpu.make_async_copy(src, dst.at[j], sem.at[3 * j + i])
            for i, (src, dst) in enumerate(places)
        ]
    begun = 0

    def ready(i):
        nonlocal begun
        while begun < min(i + 4, len(copies)):
            copies[begun].start()
            begun += 1
        copies[i].wait()

    x = x_ref[...]
    acc = extra_ref[...].astype(F32) if has_extra else None
    for j in range(N_EXP):
        ready(3 * j)
        g = dot(x, gb[j])
        ready(3 * j + 1)
        u = dot(x, ub[j])
        act = (0.5 * g * (1.0 + jnp.tanh(0.5 * g)) * u).astype(BF)
        ready(3 * j + 2)
        part = dot_nt(act, db[j])
        acc = part if acc is None else acc + part
    out_ref[...] = acc.astype(BF)


def ffn(at, x, extra, gate, ups, downs):
    n = EXPERTS * SLOTS
    has_extra = extra is not None
    vm = pl.BlockSpec(memory_space=pltpu.VMEM)
    hbm = pl.BlockSpec(memory_space=pl.ANY)
    buf = pltpu.VMEM((N_EXP, D, 512), BF)
    return pl.pallas_call(
        functools.partial(ffn_kernel, has_extra),
        in_specs=[pl.BlockSpec(memory_space=pltpu.SMEM), vm, vm if has_extra else hbm] + [hbm] * 9,
        out_specs=vm,
        out_shape=sds((n, D), BF),
        scratch_shapes=[buf, buf, buf, pltpu.SemaphoreType.DMA((12,))],
        compiler_params=pltpu.CompilerParams(vmem_limit_bytes=54 << 20),
        cost_estimate=pl.CostEstimate(
            flops=2 * n * D * 2048 * 3, bytes_accessed=1 << 20, transcendentals=0
        ),
    )(at, x, extra if has_extra else x, gate, *ups, *downs)


def combine_kernel(ret_ref, didx_ref, gates_ref, sum_ref, out_ref):
    ret = ret_ref[...]
    total = sum_ref[...]
    for k in range(2):
        pick = hot(didx_ref[:, k : k + 1] == iota((FINE, EXPERTS * SLOTS), 1))
        total = total + upright(gates_ref[k : k + 1, :]) * dot(pick, ret)
    out_ref[...] = total.astype(BF)


def turn(v, k):
    return lax.ppermute(v, "exp", [(i, (i + k) % N_EXP) for i in range(N_EXP)])


def per_device(
    coarse_in,
    norm1_gain,
    qkv_weight,
    head_scale,
    out_weight,
    norm2_gain,
    mlp_in,
    mlp_out,
    fine_in,
    parent_device,
    parent_row,
    octant,
    octant_table,
    norm3_gain,
    expert_ids,
    expert_gates,
    gate_weight,
    up_weight,
    down_weight,
):
    s = lax.axis_index("seq")
    y = lax.axis_index("exp")
    at = jnp.stack([y, s % 4]).astype(jnp.int32).reshape(1, 2)
    feats = [coarse_in] + [turn(coarse_in, k) for k in (1, 2, 3)]
    wo = lax.all_gather(out_weight, "exp", axis=0, tiled=True)
    gate = lax.all_gather(gate_weight, "exp", axis=0, tiled=True)

    pidx, didx, didxt, req = call(
        route_kernel,
        [
            sds((FINE, 1), jnp.int32),
            sds((FINE, 2), jnp.int32),
            sds((2, FINE), jnp.int32),
            sds((N_SEQ, PSLOTS, ROWS), BF),
        ],
        parent_device.reshape(1, FINE),
        parent_row.reshape(1, FINE),
        expert_ids.T,
    )
    head_block = sds((ROWS, 2 * HD), BF)
    x, *qs, kv = call(
        qkv_kernel,
        [sds((ROWS, D), BF)] + [head_block] * 4 + [sds((N_SEQ, ROWS + PSLOTS, 2 * HD), BF)],
        at,
        *feats,
        norm1_gain.reshape(1, D),
        qkv_weight,
        req,
        smem=(0,),
        scratch_shapes=[pltpu.VMEM((N_EXP, ROWS, 256), BF), pltpu.VMEM((HEADS, ROWS, 2 * HD), BF)],
    )
    qs = [qs[0]] + [
        lax.ppermute(qs[k], "seq", [(i, i ^ k) for i in range(N_SEQ)]) for k in (1, 2, 3)
    ]
    kv = lax.all_to_all(kv, "seq", 0, 0, tiled=True)
    scale = lax.dynamic_slice(head_scale, (s % 4,), (1,)) * (math.log2(math.e) / math.sqrt(HD))
    att = call(
        attn_kernel,
        sds((16, ROWS // 2, 2 * HD), BF),
        scale.reshape(1, 1),
        at,
        *qs,
        kv,
        smem=(0, 1),
        spare=16,
    )
    att = lax.all_to_all(att, ("seq", "exp"), 0, 0, axis_index_groups=SIXTEENS, tiled=True)
    ur, ul = turn(up_weight, 1), turn(up_weight, 3)
    dr, dl = turn(down_weight, 1), turn(down_weight, 3)
    u2, d2 = turn(ur, 1), turn(dl, 3)
    mixed, part = block(
        at, att, x, norm2_gain.reshape(1, D), wo, mlp_in, mlp_out, dr, dl
    )
    parts = lax.all_to_all(part, "exp", 0, 0, tiled=True)
    piece = call(coarse_kernel, sds((ROWS, 256), BF), parts, mixed)
    pieces = [piece] + [turn(piece, k) for k in (1, 2, 3)]
    coarse_new, served = call(
        serve_kernel,
        [sds((ROWS, D), BF), sds((N_SEQ * PSLOTS, D), BF)],
        at,
        kv,
        *pieces,
        smem=(0,),
        scratch_shapes=[pltpu.VMEM((N_EXP, ROWS, 256), BF)],
    )
    served = lax.all_to_all(served, "seq", 0, 0, tiled=True)
    fine_sum, outgoing = call(
        fine_kernel,
        [sds((FINE, D), F32), sds((EXPERTS * SLOTS, D), BF)],
        served,
        pidx,
        fine_in,
        octant.reshape(1, FINE),
        octant_table,
        norm3_gain.reshape(1, D),
        didxt,
        ready=(ur, ul),
    )
    mine = lax.all_to_all(outgoing, "seq", 0, 0, tiled=True)
    other = lax.ppermute(mine, "seq", SWAP)
    ups = [up_weight, ur, ul, u2]
    downs = [down_weight, dr, dl, d2]
    for_other = ffn(at, other, None, gate, ups, downs)
    from_other = lax.ppermute(for_other, "seq", SWAP)
    result = ffn(at, mine, from_other, gate, ups, downs)
    returned = lax.all_to_all(result, "seq", 0, 0, tiled=True)
    fine_out = call(
        combine_kernel, sds((FINE, D), BF), returned, didx, expert_gates.T, fine_sum
    )
    return (coarse_new, fine_out)


def solution(mesh):
    return jax.shard_map(
        per_device,
        mesh=mesh,
        in_specs=(
            P("seq", "exp"),
            P(),
            P(None, None, "exp"),
            P("exp"),
            P("exp", None),
            P(),
            P(None, "exp"),
            P("exp", None),
            P(("seq", "exp"), None),
            P(("seq", "exp"), None),
            P(("seq", "exp")),
            P(("seq", "exp")),
            P(),
            P(),
            P(("seq", "exp"), None),
            P(("seq", "exp"), None),
            P("seq", None, "exp"),
            P("seq", None, "exp"),
            P("seq", None, "exp"),
        ),
        out_specs=(P("seq", None), P(("seq", "exp"), None)),
        check_vma=False,
    )
```

time: 259 us -> 232 us (0.90)
  blocking collectives: 84.2 us -> 37.2 us
  starting transfers between devices: 27.9 us -> 53.2 us
  Pallas kernels: 50.7 us -> 41.7 us
  waiting for transfers between devices: 66.3 us -> 71.7 us
  other arithmetic: 2.95 us -> 0.08 us
    ppermute x1 -> x16, waiting for transfers between devices: 2.73 us -> 48.6 us  [the longest x12 36 us: turn(): return lax.ppermute(v, 'exp', [(i, (i + k) % N_EXP) for i in range(N_EXP)])]
    all_gather x3 -> x0, blocking collectives: 36.1 us -> none  [the longest x1 12.3 us: per_device(): normed2 = lax.all_gather(normed2, 'exp', axis=0, tiled=True)]
    ppermute x1 -> x16, starting transfers between devices: 0.14 us -> 20.7 us  [the longest x12 16.9 us: turn(): return lax.ppermute(v, 'exp', [(i, (i + k) % N_EXP) for i in range(N_EXP)])]
    all_to_all x1, waiting for transfers between devices: 16.1 us -> 0.01 us  [per_device(): served = lax.all_to_all(served, 'seq', 0, 0, tiled=True)]
    all_to_all x1, waiting for transfers between devices: 17.1 us -> 1.88 us  [per_device(): kv = lax.all_to_all(kv, 'seq', 0, 0, tiled=True)]
    all_to_all x4 -> x2, blocking collectives: 48.2 us -> 37.2 us  [the longest x1 24.5 us: per_device(): returned = lax.all_to_all(result, 'seq', 0, 0, tiled=True)]
    pallas_call x11 -> x10, Pallas kernels: 50.7 us -> 41.7 us  [the longest x2 24.8 us: ffn(): pl.pallas_call(functools.partial(ffn_kernel, has_extra), in_specs=[pl.Blo...]
    all_to_all x2, waiting for transfers between devices: 25.7 us -> 19.9 us  [the longest x1 14.2 us: per_device(): mine = lax.all_to_all(outgoing, 'seq', 0, 0, tiled=True)]
  transfers between devices with their start and end apart: 9 -> 23, of which waited for: 6 -> 12; matrix products, arithmetic and copies ran while one was open for 2% -> 0% of each run, Pallas kernels for 10% -> 7%
where the time goes in v2:
time: 232 us; the launch traced here: 231 us
  waiting for transfers between devices  71.7 us (31%)
  starting transfers between devices  53.2 us (23%)
  Pallas kernels  41.7 us (18%)
  blocking collectives  37.2 us (16%)
  between operations  14.9 us (6%)
  local copies, waits for them, and re-layouts  12.5 us (5%)
    ppermute x12, waiting for transfers between devices, turn(): return lax.ppermute(v, 'exp', [(i, (i + k) % N_EXP) for i in range(N_EXP)])  36 us
    pallas_call x2, Pallas kernels, ffn(): pl.pallas_call(functools.partial(ffn_kernel, has_extra), in_specs=[pl.Blo...  24.8 us
    all_to_all x1, blocking collectives, per_device(): returned = lax.all_to_all(result, 'seq', 0, 0, tiled=True)  24.5 us
    ppermute x12, starting transfers between devices, turn(): return lax.ppermute(v, 'exp', [(i, (i + k) % N_EXP) for i in range(N_EXP)])  16.9 us
    all_to_all x1, waiting for transfers between devices, per_device(): mine = lax.all_to_all(outgoing, 'seq', 0, 0, tiled=True)  14.2 us
    all_to_all x1, blocking collectives, per_device(): parts = lax.all_to_all(part, 'exp', 0, 0, tiled=True)  12.8 us
    unnamed x54, local copies, waits for them, and re-layouts  11.9 us
    pallas_call x7, Pallas kernels, call(): pl.pallas_call(kernel, out_shape=out_shape, in_specs=space + [pl.BlockSpe...  11.8 us
  transfers between devices with their start and end apart: 23, of which 12 were waited for; matrix products, arithmetic and copies ran while one was open for 0% of the time, Pallas kernels for 7%

profile of v2, /device:TPU:1, one launch (start us, length us, event | category | flops | bytes accessed | tf_op | source)
XLA Modules:
  0.0 231.4 jit_solution(2233870825455060606)
XLA Ops:
  8.7 2.2 collective-permute-start
  10.9 2.6 %collective-permute-start.1 = (bf16[128,256]{1,0:T(8,128)(2,1)}, bf16[128,256]{1,0:T(8,128)(2,1)S(1)}, u32[]{:S(2)}, u32[]{:S(2)}) collective-permute-start(bf16[128,256]{1,0:T(8,128)(2,1)} %f0_ref.1), channel_id=1, source_target_pairs={{0,2},{1,3},{2,0},{3,1},{4,6},{5,7},{6,4},{7,5},{8,10},{9,11},{10,... | collective-permute-start | bytes 196616 | tf_op jit(solution)/shard_map/ppermute | solution.py:287
  18.7 3.0 %shard_map.195 = (bf16[128,1024]{1,0:T(8,128)(2,1)S(1)}, bf16[128,128]{1,0:T(8,128)(2,1)S(1)}, bf16[128,128]{1,0:T(8,128)(2,1)S(1)}, bf16[128,128]{1,0:T(8,128)(...) custom-call(s32[1,2]{1,0:T(1,128)S(1)} %add_bitcast_fusion.at_ref, ...), custom_call_target="tpu_custom_call" | custom-call | bytes 1 | tf_op jit(solution)/shard_map/pallas_call | solution.py:39
  22.4 9.9 %all-to-all-start = ((bf16[32,144,128]{2,1,0:T(8,128)(2,1)}), bf16[32,144,128]{2,1,0:T(8,128)(2,1)S(1)}, u32[]{:S(2)}, u32[]{:S(2)}) async-start(bf16[32,144,128]{2,1,0:T(8,128)(2,1)} %get-tuple-element.19), calls=%async_computation | async-start | bytes 2359296 | tf_op jit(solution)/shard_map/all_to_all | solution.py:345
  32.5 2.6 %collective-permute-start.7 = (bf16[1,1024,512]{2,1,0:T(8,128)(2,1)}, bf16[1,1024,512]{2,1,0:T(8,128)(2,1)}, u32[]{:S(2)}, u32[]{:S(2)}) collective-permute-start(bf16[1,1024,512]{2,1,0:T(8,128)(2,1)} %d0.3), channel_id=1, source_target_pairs={{0,3},{1,0},{2,1},{3,2},{4,7},{5,4},{6,5},{7,6},{8,11},{9,8},{10,9... | collective-permute-start | bytes 3145736 | tf_op jit(solution)/shard_map/ppermute | solution.py:287
  35.9 1.5 collective-permute-start.4
  38.8 5.6 %collective-permute-done.4.q2_ref = bf16[128,128]{1,0:T(8,128)(2,1)S(1)} collective-permute-done((bf16[128,128]{1,0:T(8,128)(2,1)S(1)}, bf16[128,128]{1,0:T(8,128)(2,1)S(1)}, u32[]{:S(2)}, u32[]{:S(2)}) %collective-permute-start.4) | collective-permute-done | bytes 32800 | tf_op jit(solution)/shard_map/ppermute | solution.py:343
  44.4 4.5 %collective-permute-done.5.q3_ref = bf16[128,128]{1,0:T(8,128)(2,1)S(1)} collective-permute-done((bf16[128,128]{1,0:T(8,128)(2,1)S(1)}, bf16[128,128]{1,0:T(8,128)(2,1)S(1)}, u32[]{:S(2)}, u32[]{:S(2)}) %collective-permute-start.5) | collective-permute-done | bytes 32800 | tf_op jit(solution)/shard_map/ppermute | solution.py:343
  48.9 1.9 all-to-all-done.kv_ref
  50.8 4.6 %shard_map.196 = bf16[16,64,128]{2,1,0:T(8,128)(2,1)} custom-call(f32[1,1]{1,0:T(1,128)} %bitcast.7.scale_ref, s32[1,2]{1,0:T(1,128)S(1)} %add_bitcast_fusion.at_ref, bf16[128,128]{1,0:T(8,128)(2,1)S(1)} %get-tuple-element.20.q0_ref, bf16[128,128]{1,0:T(8,128)(2,1)S(1)} %collective-permute-done.3.q1_ref, bf16[128,128]{1,0:T(8,128)(2,1)S(1)} %collective-permute-done.4.q2_ref, ...), custom_call_target="tpu_custom_call" | custom-call | bytes 1 | tf_op jit(solution)/shard_map/pallas_call | solution.py:39
  55.4 4.1 %all-to-all-start.1 = ((bf16[16,64,128]{2,1,0:T(8,128)(2,1)}), bf16[16,64,128]{2,1,0:T(8,128)(2,1)S(1)}, u32[]{:S(2)}, u32[]{:S(2)}) async-start(bf16[16,64,128]{2,1,0:T(8,128)(2,1)} %shard_map.196), calls=%async_computation.1 | async-start | bytes 524288 | tf_op jit(solution)/shard_map/all_to_all | solution.py:357
  59.5 6.4 %collective-permute-done.6.rest_0_.d1 = bf16[1,1024,512]{2,1,0:T(8,128)(2,1)S(1)} collective-permute-done((bf16[1,1024,512]{2,1,0:T(8,128)(2,1)}, bf16[1,1024,512]{2,1,0:T(8,128)(2,1)S(1)}, u32[]{:S(2)}, u32[]{:S(2)}) %collective-permute-start.6) | collective-permute-done | bytes 1048608 | tf_op jit(solution)/shard_map/ppermute | solution.py:287
  65.9 5.8 %all-to-all-done.1.att_ref = bf16[16,64,128]{2,1,0:T(8,128)(2,1)S(1)} async-done(((bf16[16,64,128]{2,1,0:T(8,128)(2,1)}), bf16[16,64,128]{2,1,0:T(8,128)(2,1)S(1)}, u32[]{:S(2)}, u32[]{:S(2)}) %all-to-all-start.1) | async-done | bytes 262176 | tf_op jit(solution)/shard_map/all_to_all | solution.py:357
  72.4 5.1 %shard_map.197 = (f32[128,256]{1,0:T(8,128)}, bf16[4,128,256]{2,1,0:T(8,128)(2,1)}) custom-call(s32[1,2]{1,0:T(1,128)} %copy-done.12, bf16[16,64,128]{2,1,0:T(8,128)(2,1)} %copy-done.21, bf16[128,1024]{1,0:T(8,128)(2,1)} %copy-done.8, f32[1,1024]{1,0:T(1,128)} %bitcast.33, bf16[1024,1024]{1,0:T(8,128)(2,1)} %all-gather.3.cloned.1.call-done.wo_ref, ...), custom_call_target="tpu_custom_call" | custom-call | flops 1 | bytes 1 | tf_op jit(solution)/shard_map/pallas_call | solution.py:178
  77.5 12.8 %all_to_all.48.parts_ref = bf16[4,128,256]{2,1,0:T(8,128)(2,1)S(1)} all-to-all(bf16[4,128,256]{2,1,0:T(8,128)(2,1)} %get-tuple-element.25), channel_id=1, replica_groups=mesh['seq'=32,'exp'=4] {'exp'}, dimensions={0} | all-to-all | bytes 524288 | tf_op jit(solution)/shard_map/all_to_all | solution.py:364
  91.6 1.8 collective-permute-start.9
  94.8 1.9 collective-permute-start.12
  97.6 1.6 collective-permute-done.9.c2_ref
  99.2 1.4 collective-permute-done.10.c3_ref
  100.7 1.3 shard_map.199
  102.9 10.3 %all-to-all-start.3 = ((bf16[32,16,1024]{2,1,0:T(8,128)(2,1)}), bf16[32,16,1024]{2,1,0:T(8,128)(2,1)S(1)}, u32[]{:S(2)}, u32[]{:S(2)}) async-start(bf16[32,16,1024]{2,1,0:T(8,128)(2,1)} %bitcast.21), calls=%async_computation.3 | async-start | bytes 2097152 | tf_op jit(solution)/shard_map/all_to_all | solution.py:376
  113.3 16.9 %collective-permute-done.11.rest_0_.u1 = bf16[1,1024,512]{2,1,0:T(8,128)(2,1)S(1)} collective-permute-done((bf16[1,1024,512]{2,1,0:T(8,128)(2,1)}, bf16[1,1024,512]{2,1,0:T(8,128)(2,1)S(1)}, u32[]{:S(2)}, u32[]{:S(2)}) %collective-permute-start.11) | collective-permute-done | bytes 1048608 | tf_op jit(solution)/shard_map/ppermute | solution.py:287
  134.3 7.9 %all-to-all-start.4 = ((bf16[32,16,1024]{2,1,0:T(8,128)(2,1)}), bf16[32,16,1024]{2,1,0:T(8,128)(2,1)S(1)}, u32[]{:S(2)}, u32[]{:S(2)}) async-start(bf16[32,16,1024]{2,1,0:T(8,128)(2,1)} %bitcast.22), calls=%async_computation.4 | async-start | bytes 2097152 | tf_op jit(solution)/shard_map/all_to_all | solution.py:389
  142.5 2.4 %collective-permute-start.15 = (bf16[1,1024,512]{2,1,0:T(8,128)(2,1)}, bf16[1,1024,512]{2,1,0:T(8,128)(2,1)}, u32[]{:S(2)}, u32[]{:S(2)}) collective-permute-start(bf16[1,1024,512]{2,1,0:T(8,128)(2,1)} %collective-permute-done.7.rest_1_.d2), channel_id=1, source_target_pairs={{0,3},{1,0},{2,1},{3,2},{4,7},{5,4},{6,5},{7,6},{8,11},{9,8},{10,9... | collective-permute-start | bytes 3145736 | tf_op jit(solution)/shard_map/ppermute | solution.py:287
  145.0 14.2 %all-to-all-done.4 = bf16[32,16,1024]{2,1,0:T(8,128)(2,1)S(1)} async-done(((bf16[32,16,1024]{2,1,0:T(8,128)(2,1)}), bf16[32,16,1024]{2,1,0:T(8,128)(2,1)S(1)}, u32[]{:S(2)}, u32[]{:S(2)}) %all-to-all-start.4) | async-done | bytes 1048608 | tf_op jit(solution)/shard_map/all_to_all | solution.py:389
  159.2 8.8 %collective-permute-done.14.u3 = bf16[1,1024,512]{2,1,0:T(8,128)(2,1)S(1)} collective-permute-done((bf16[1,1024,512]{2,1,0:T(8,128)(2,1)S(1)}, bf16[1,1024,512]{2,1,0:T(8,128)(2,1)S(1)}, u32[]{:S(2)}, u32[]{:S(2)}) %collective-permute-start.14) | collective-permute-done | bytes 1048608 | tf_op jit(solution)/shard_map/ppermute | solution.py:287
  169.0 12.2 %shard_map.201 = bf16[512,1024]{1,0:T(8,128)(2,1)} custom-call(s32[1,2]{1,0:T(1,128)} %copy-done.12, bf16[512,1024]{1,0:T(8,128)(2,1)} %collective-permute-done.13.x_ref.extra_ref, bf16[512,1024]{1,0:T(8,128)(2,1)} %collective-permute-done.13.x_ref.extra_ref, bf16[4,1024,512]{2,1,0:T(8,128)(2,1)} %all-gather.5.cloned.1.call-done.gate_ref, ...), custom_call_target="tpu_custom_call" | custom-call | flops 6442450944 | bytes 1048576 | tf_op jit(solution)/shard_map/pallas_call | solution.py:264
  181.2 1.3 collective-permute-start.16
  182.6 2.5 %collective-permute-done.16.extra_ref = bf16[512,1024]{1,0:T(8,128)(2,1)S(1)} collective-permute-done((bf16[512,1024]{1,0:T(8,128)(2,1)}, bf16[512,1024]{1,0:T(8,128)(2,1)S(1)}, u32[]{:S(2)}, u32[]{:S(2)}) %collective-permute-start.16) | collective-permute-done | bytes 1048608 | tf_op jit(solution)/shard_map/ppermute | solution.py:394
  186.0 12.7 %shard_map.202 = bf16[512,1024]{1,0:T(8,128)(2,1)} custom-call(s32[1,2]{1,0:T(1,128)} %copy-done.12, bf16[512,1024]{1,0:T(8,128)(2,1)} %bitcast.31, bf16[512,1024]{1,0:T(8,128)(2,1)} %copy-done.25, bf16[4,1024,512]{2,1,0:T(8,128)(2,1)} %all-gather.5.cloned.1.call-done.gate_ref, bf16[1,1024,512]{2,1,0:T(8,128)(2,1)} %u0.3, bf16[1,1024,512]{2,1,0:T(8,128)(2,1)} %copy-done.1, ...), custom_call_target="tpu_custom_call" | custom-call | flops 6442450944 | bytes 1048576 | tf_op jit(solution)/shard_map/pallas_call | solution.py:264
  198.7 24.5 %all_to_all.49 = bf16[32,16,1024]{2,1,0:T(8,128)(2,1)S(1)} all-to-all(bf16[32,16,1024]{2,1,0:T(8,128)(2,1)} %bitcast.32), channel_id=1, replica_groups=mesh['seq'=32,'exp'=4] {'seq'}, dimensions={0} | all-to-all | bytes 2097152 | tf_op jit(solution)/shard_map/all_to_all | solution.py:396
  223.2 1.3 shard_map.203
  (84 shorter events, 20.8 us)
Async XLA Ops:
  7.2 64.5 %all-gather.3.cloned.1.call-start = ((), (), s32[]{:S(2)}) async-start(), calls=%async_computation.6 | async-start | bytes 2621440 | tf_op jit(solution)/shard_map/all_gather | solution.py:315
  7.9 160.1 %all-gather.5.cloned.1.call-start = ((), (), s32[]{:S(2)}) async-start(), calls=%async_computation.7 | async-start | bytes 5242880 | tf_op jit(solution)/shard_map/all_gather | solution.py:316
  8.7 8.5 %collective-permute-start = (bf16[128,256]{1,0:T(8,128)(2,1)}, bf16[128,256]{1,0:T(8,128)(2,1)S(1)}, u32[]{:S(2)}, u32[]{:S(2)}) collective-permute-start(bf16[128,256]{1,0:T(8,128)(2,1)} %f0_ref.1), channel_id=1, source_target_pairs={{0,1},{1,2},{2,3},{3,0},{4,5},{5,6},{6,7},{7,4},{8,9},{9,10},{10,1... | collective-permute-start | bytes 196616 | tf_op jit(solution)/shard_map/ppermute | solution.py:287
  10.9 6.3 %collective-permute-start.1 = (bf16[128,256]{1,0:T(8,128)(2,1)}, bf16[128,256]{1,0:T(8,128)(2,1)S(1)}, u32[]{:S(2)}, u32[]{:S(2)}) collective-permute-start(bf16[128,256]{1,0:T(8,128)(2,1)} %f0_ref.1), channel_id=1, source_target_pairs={{0,2},{1,3},{2,0},{3,1},{4,6},{5,7},{6,4},{7,5},{8,10},{9,11},{10,... | collective-permute-start | bytes 196616 | tf_op jit(solution)/shard_map/ppermute | solution.py:287
  13.5 3.7 %collective-permute-start.2 = (bf16[128,256]{1,0:T(8,128)(2,1)}, bf16[128,256]{1,0:T(8,128)(2,1)S(1)}, u32[]{:S(2)}, u32[]{:S(2)}) collective-permute-start(bf16[128,256]{1,0:T(8,128)(2,1)} %f0_ref.1), channel_id=1, source_target_pairs={{0,3},{1,0},{2,1},{3,2},{4,7},{5,4},{6,5},{7,6},{8,11},{9,8},{10,9... | collective-permute-start | bytes 196616 | tf_op jit(solution)/shard_map/ppermute | solution.py:287
  17.1 33.6 %copy-start.12 = (s32[1,2]{1,0:T(1,128)}, s32[1,2]{1,0:T(1,128)S(1)}, u32[]{:S(2)}) copy-start(s32[1,2]{1,0:T(1,128)S(1)} %add_bitcast_fusion.at_ref) | copy-start | bytes 28
  18.7 18.9 %copy-start.26 = (f32[4]{0:T(128)S(1)}, f32[4]{0:T(128)}, u32[]{:S(2)}) copy-start(f32[4]{0:T(128)} %param.22) | copy-start | bytes 52
  22.4 28.3 %all-to-all-start = ((bf16[32,144,128]{2,1,0:T(8,128)(2,1)}), bf16[32,144,128]{2,1,0:T(8,128)(2,1)S(1)}, u32[]{:S(2)}, u32[]{:S(2)}) async-start(bf16[32,144,128]{2,1,0:T(8,128)(2,1)} %get-tuple-element.19), calls=%async_computation | async-start | bytes 2359296 | tf_op jit(solution)/shard_map/all_to_all | solution.py:345
  32.4 33.5 %collective-permute-start.6 = (bf16[1,1024,512]{2,1,0:T(8,128)(2,1)}, bf16[1,1024,512]{2,1,0:T(8,128)(2,1)S(1)}, u32[]{:S(2)}, u32[]{:S(2)}) collective-permute-start(bf16[1,1024,512]{2,1,0:T(8,128)(2,1)} %d0.3), channel_id=1, source_target_pairs={{0,1},{1,2},{2,3},{3,0},{4,5},{5,6},{6,7},{7,4},{8,9},{9,10},{10,1... | collective-permute-start | bytes 3145736 | tf_op jit(solution)/shard_map/ppermute | solution.py:287
  32.5 33.4 %collective-permute-start.7 = (bf16[1,1024,512]{2,1,0:T(8,128)(2,1)}, bf16[1,1024,512]{2,1,0:T(8,128)(2,1)}, u32[]{:S(2)}, u32[]{:S(2)}) collective-permute-start(bf16[1,1024,512]{2,1,0:T(8,128)(2,1)} %d0.3), channel_id=1, source_target_pairs={{0,3},{1,0},{2,1},{3,2},{4,7},{5,4},{6,5},{7,6},{8,11},{9,8},{10,9... | collective-permute-start | bytes 3145736 | tf_op jit(solution)/shard_map/ppermute | solution.py:287
  35.1 3.7 %collective-permute-start.3 = (bf16[128,128]{1,0:T(8,128)(2,1)S(1)}, bf16[128,128]{1,0:T(8,128)(2,1)S(1)}, u32[]{:S(2)}, u32[]{:S(2)}) collective-permute-start(bf16[128,128]{1,0:T(8,128)(2,1)S(1)} %get-tuple-element.21), channel_id=1, source_target_pairs={{0,4},{4,0},{8,12},{12,8},{16,20},{20,16},{24,28},{28,24},{32,36},... | collective-permute-start | bytes 98312 | tf_op jit(solution)/shard_map/ppermute | solution.py:343
  35.9 8.5 %collective-permute-start.4 = (bf16[128,128]{1,0:T(8,128)(2,1)S(1)}, bf16[128,128]{1,0:T(8,128)(2,1)S(1)}, u32[]{:S(2)}, u32[]{:S(2)}) collective-permute-start(bf16[128,128]{1,0:T(8,128)(2,1)S(1)} %get-tuple-element.22), channel_id=1, source_target_pairs={{0,8},{4,12},{8,0},{12,4},{16,24},{20,28},{24,16},{28,20},{32,40},... | collective-permute-start | bytes 98312 | tf_op jit(solution)/shard_map/ppermute | solution.py:343
  37.4 11.4 %collective-permute-start.5 = (bf16[128,128]{1,0:T(8,128)(2,1)S(1)}, bf16[128,128]{1,0:T(8,128)(2,1)S(1)}, u32[]{:S(2)}, u32[]{:S(2)}) collective-permute-start(bf16[128,128]{1,0:T(8,128)(2,1)S(1)} %get-tuple-element.23), channel_id=1, source_target_pairs={{0,12},{4,8},{8,4},{12,0},{16,28},{20,24},{24,20},{28,16},{32,44},... | collective-permute-start | bytes 98312 | tf_op jit(solution)/shard_map/ppermute | solution.py:343
  55.4 16.3 %all-to-all-start.1 = ((bf16[16,64,128]{2,1,0:T(8,128)(2,1)}), bf16[16,64,128]{2,1,0:T(8,128)(2,1)S(1)}, u32[]{:S(2)}, u32[]{:S(2)}) async-start(bf16[16,64,128]{2,1,0:T(8,128)(2,1)} %shard_map.196), calls=%async_computation.1 | async-start | bytes 524288 | tf_op jit(solution)/shard_map/all_to_all | solution.py:357
  72.4 28.3 %copy-start.13 = (s32[1,2]{1,0:T(1,128)S(1)}, s32[1,2]{1,0:T(1,128)}, u32[]{:S(2)}) copy-start(s32[1,2]{1,0:T(1,128)} %copy-done.12) | copy-start | bytes 28
  90.3 40.0 %copy-start.18 = (s32[160]{0:T(256)S(1)}, s32[160]{0:T(256)}, u32[]{:S(2)}) copy-start(s32[160]{0:T(256)} %param.30) | copy-start | bytes 1924
  91.2 39.0 %copy-start.11 = (bf16[8,1024]{1,0:T(8,128)(2,1)S(1)}, bf16[8,1024]{1,0:T(8,128)(2,1)}, u32[]{:S(2)}) copy-start(bf16[8,1024]{1,0:T(8,128)(2,1)} %table_ref.1) | copy-start | bytes 49156
  91.2 39.1 %copy-start.15 = (f32[1024]{0:T(1024)S(1)}, f32[1024]{0:T(1024)}, u32[]{:S(2)}) copy-start(f32[1024]{0:T(1024)} %param.32) | copy-start | bytes 12292
  91.2 6.4 %collective-permute-start.8 = (bf16[128,256]{1,0:T(8,128)(2,1)S(1)}, bf16[128,256]{1,0:T(8,128)(2,1)S(1)}, u32[]{:S(2)}, u32[]{:S(2)}) collective-permute-start(bf16[128,256]{1,0:T(8,128)(2,1)S(1)} %shard_map.198.c0_ref), channel_id=1, source_target_pairs={{0,1},{1,2},{2,3},{3,0},{4,5},{5,6},{6,7},{7,4},{8,9},{9,10},{10,1... | collective-permute-start | bytes 196616 | tf_op jit(solution)/shard_map/ppermute | solution.py:287
  91.6 7.6 %collective-permute-start.9 = (bf16[128,256]{1,0:T(8,128)(2,1)S(1)}, bf16[128,256]{1,0:T(8,128)(2,1)S(1)}, u32[]{:S(2)}, u32[]{:S(2)}) collective-permute-start(bf16[128,256]{1,0:T(8,128)(2,1)S(1)} %shard_map.198.c0_ref), channel_id=1, source_target_pairs={{0,2},{1,3},{2,0},{3,1},{4,6},{5,7},{6,4},{7,5},{8,10},{9,11},{10,... | collective-permute-start | bytes 196616 | tf_op jit(solution)/shard_map/ppermute | solution.py:287
  93.4 7.3 %collective-permute-start.10 = (bf16[128,256]{1,0:T(8,128)(2,1)S(1)}, bf16[128,256]{1,0:T(8,128)(2,1)S(1)}, u32[]{:S(2)}, u32[]{:S(2)}) collective-permute-start(bf16[128,256]{1,0:T(8,128)(2,1)S(1)} %shard_map.198.c0_ref), channel_id=1, source_target_pairs={{0,3},{1,0},{2,1},{3,2},{4,7},{5,4},{6,5},{7,6},{8,11},{9,8},{10,9... | collective-permute-start | bytes 196616 | tf_op jit(solution)/shard_map/ppermute | solution.py:287
  94.1 36.1 %collective-permute-start.11 = (bf16[1,1024,512]{2,1,0:T(8,128)(2,1)}, bf16[1,1024,512]{2,1,0:T(8,128)(2,1)S(1)}, u32[]{:S(2)}, u32[]{:S(2)}) collective-permute-start(bf16[1,1024,512]{2,1,0:T(8,128)(2,1)} %u0.3), channel_id=1, source_target_pairs={{0,1},{1,2},{2,3},{3,0},{4,5},{5,6},{6,7},{7,4},{8,9},{9,10},{10,1... | collective-permute-start | bytes 3145736 | tf_op jit(solution)/shard_map/ppermute | solution.py:287
  94.8 35.4 %collective-permute-start.12 = (bf16[1,1024,512]{2,1,0:T(8,128)(2,1)}, bf16[1,1024,512]{2,1,0:T(8,128)(2,1)S(1)}, u32[]{:S(2)}, u32[]{:S(2)}) collective-permute-start(bf16[1,1024,512]{2,1,0:T(8,128)(2,1)} %u0.3), channel_id=1, source_target_pairs={{0,3},{1,0},{2,1},{3,2},{4,7},{5,4},{6,5},{7,6},{8,11},{9,8},{10,9... | collective-permute-start | bytes 3145736 | tf_op jit(solution)/shard_map/ppermute | solution.py:287
  102.9 27.3 %all-to-all-start.3 = ((bf16[32,16,1024]{2,1,0:T(8,128)(2,1)}), bf16[32,16,1024]{2,1,0:T(8,128)(2,1)S(1)}, u32[]{:S(2)}, u32[]{:S(2)}) async-start(bf16[32,16,1024]{2,1,0:T(8,128)(2,1)} %bitcast.21), calls=%async_computation.3 | async-start | bytes 2097152 | tf_op jit(solution)/shard_map/all_to_all | solution.py:376
  134.3 24.8 %all-to-all-start.4 = ((bf16[32,16,1024]{2,1,0:T(8,128)(2,1)}), bf16[32,16,1024]{2,1,0:T(8,128)(2,1)S(1)}, u32[]{:S(2)}, u32[]{:S(2)}) async-start(bf16[32,16,1024]{2,1,0:T(8,128)(2,1)} %bitcast.22), calls=%async_computation.4 | async-start | bytes 2097152 | tf_op jit(solution)/shard_map/all_to_all | solution.py:389
  142.2 25.8 %collective-permute-start.14 = (bf16[1,1024,512]{2,1,0:T(8,128)(2,1)S(1)}, bf16[1,1024,512]{2,1,0:T(8,128)(2,1)S(1)}, u32[]{:S(2)}, u32[]{:S(2)}) collective-permute-start(bf16[1,1024,512]{2,1,0:T(8,128)(2,1)S(1)} %collective-permute-done.11.rest_0_.u1), channel_id=1, source_target_pairs={{0,1},{1,2},{2,3},{3,0},{4,5},{5,6},{6,7},{7,4},{8,9},{9,10},{10,1... | collective-permute-start | bytes 3145736 | tf_op jit(solution)/shard_map/ppermute | solution.py:287
  142.5 25.5 %collective-permute-start.15 = (bf16[1,1024,512]{2,1,0:T(8,128)(2,1)}, bf16[1,1024,512]{2,1,0:T(8,128)(2,1)}, u32[]{:S(2)}, u32[]{:S(2)}) collective-permute-start(bf16[1,1024,512]{2,1,0:T(8,128)(2,1)} %collective-permute-done.7.rest_1_.d2), channel_id=1, source_target_pairs={{0,3},{1,0},{2,1},{3,2},{4,7},{5,4},{6,5},{7,6},{8,11},{9,8},{10,9... | collective-permute-start | bytes 3145736 | tf_op jit(solution)/shard_map/ppermute | solution.py:287
  159.1 22.1 %copy-start.22 = (bf16[32,16,1024]{2,1,0:T(8,128)(2,1)}, bf16[32,16,1024]{2,1,0:T(8,128)(2,1)S(1)}, u32[]{:S(2)}) copy-start(bf16[32,16,1024]{2,1,0:T(8,128)(2,1)S(1)} %all-to-all-done.4) | copy-start | bytes 3145732
  159.1 8.9 %collective-permute-start.13 = (bf16[512,1024]{1,0:T(8,128)(2,1)S(1)}, bf16[512,1024]{1,0:T(8,128)(2,1)}, u32[]{:S(2)}, u32[]{:S(2)}) collective-permute-start(bf16[512,1024]{1,0:T(8,128)(2,1)S(1)} %bitcast.30), channel_id=1, source_target_pairs={{0,4},{4,0},{8,12},{12,8},{16,20},{20,16},{24,28},{28,24},{32,36},... | collective-permute-start | bytes 3145736 | tf_op jit(solution)/shard_map/ppermute | solution.py:390
  181.2 3.8 %collective-permute-start.16 = (bf16[512,1024]{1,0:T(8,128)(2,1)}, bf16[512,1024]{1,0:T(8,128)(2,1)S(1)}, u32[]{:S(2)}, u32[]{:S(2)}) collective-permute-start(bf16[512,1024]{1,0:T(8,128)(2,1)} %shard_map.201), channel_id=1, source_target_pairs={{0,4},{4,0},{8,12},{12,8},{16,20},{20,16},{24,28},{28,24},{32,36},... | collective-permute-start | bytes 3145736 | tf_op jit(solution)/shard_map/ppermute | solution.py:394
  198.7 24.5 %copy-start.6 = (f32[160,1024]{1,0:T(8,128)S(1)}, f32[160,1024]{1,0:T(8,128)}, u32[]{:S(2)}) copy-start(f32[160,1024]{1,0:T(8,128)} %copy-done.5) | copy-start | bytes 1966084
  198.7 24.5 %copy-start.16 = (f32[160,2]{0,1:T(2,128)S(1)}, f32[160,2]{0,1:T(2,128)}, u32[]{:S(2)}) copy-start(f32[160,2]{0,1:T(2,128)} %param.34) | copy-start | bytes 3844
  (18 other events, 43.7 us)
Sparse Core Ops, SparseCore 0:
  9.7 40.6 all-gather.2
  52.1 64.5 all-gather.4

commit v3 on v2

--- a/solution.py
+++ b/solution.py
@@ -30,18 +30,20 @@
     return math.prod(x.shape) * x.dtype.itemsize
 
 
-def call(kernel, out_shape, *args, smem=(), flops=0, spare=6, ready=(), **kw):
+def call(kernel, out_shape, *args, smem=(), far=(), limit=60, flops=0, ready=(), **kw):
     space = [
         pl.BlockSpec(memory_space=pltpu.SMEM if i in smem else pltpu.VMEM) for i in range(len(args))
     ]
     outs = jax.tree.map(lambda _: pl.BlockSpec(memory_space=pltpu.VMEM), out_shape)
+    for i in far:
+        outs[i] = pl.BlockSpec(memory_space=pltpu.HBM)
     moved = sum(nbytes(a) for a in args) + sum(nbytes(o) for o in jax.tree.leaves(out_shape))
     return pl.pallas_call(
         kernel,
         out_shape=out_shape,
         in_specs=space + [pl.BlockSpec(memory_space=pl.ANY)] * len(ready),
         out_specs=outs,
-        compiler_params=pltpu.CompilerParams(vmem_limit_bytes=2 * moved + (spare << 20)),
+        compiler_params=pltpu.CompilerParams(vmem_limit_bytes=limit << 20),
         cost_estimate=pl.CostEstimate(flops=flops, bytes_accessed=1, transcendentals=0),
         **kw,
     )(*args, *ready)
@@ -121,7 +123,8 @@
         q_ref[...] = qs[me ^ k]
 
 
-def attn_kernel(scale_ref, at_ref, q0_ref, q1_ref, q2_ref, q3_ref, kv_ref, out_ref):
+def attn_kernel(scale_ref, at_ref, q0_ref, q1_ref, q2_ref, q3_ref, kv_ref, out_ref, req_ref):
+    req_ref[...] = kv_ref[:, ROWS : ROWS + PSLOTS, :].reshape(N_SEQ * PSLOTS, ROWS)
     kv = kv_ref[:, 0:ROWS, :].reshape(N_SEQ * ROWS, 2 * HD)
     vones = jnp.where(iota(kv.shape, 1) < HD, jnp.ones_like(kv), kv)
     c = scale_ref[0, 0]
@@ -197,81 +200,185 @@
     out_ref[...] = (mixed_ref[...] + total).astype(BF)
 
 
-def serve_kernel(at_ref, kv_ref, c0_ref, c1_ref, c2_ref, c3_ref, *rest):
-    coarse_ref, out_ref, scr = rest[-3:]
+def copy_out(out_ref, scr, sem, make):
+    step = scr.shape[0] // 4
+    copies = []
+    for i in range(4):
+        part = slice(i * step, (i + 1) * step)
+        scr[part] = make(part)
+        copies.append(pltpu.make_async_copy(scr.at[part], out_ref.at[part], sem.at[i]))
+        copies[-1].start()
+    for c in copies:
+        c.wait()
+
+
+def serve_kernel(at_ref, req_ref, c0_ref, c1_ref, c2_ref, c3_ref, coarse_ref, out_ref, cs, scr, sem):
     y = at_ref[0, 0]
     for k, c_ref in enumerate((c0_ref, c1_ref, c2_ref, c3_ref)):
-        scr[around(y, k)] = c_ref[...]
-    coarse = jnp.concatenate([scr[c] for c in range(N_EXP)], axis=1)
+        cs[around(y, k)] = c_ref[...]
+    coarse = jnp.concatenate([cs[c] for c in range(N_EXP)], axis=1)
     coarse_ref[...] = coarse
-    req = kv_ref[:, ROWS : ROWS + PSLOTS, :].reshape(N_SEQ * PSLOTS, ROWS)
-    chosen = hot(req.astype(F32) == iota(req.shape, 1).astype(F32))
-    out_ref[...] = dot(chosen, coarse).astype(BF)
+
+    def make(part):
+        req = req_ref[part].astype(F32)
+        return dot(hot(req == iota(req.shape, 1).astype(F32)), coarse).astype(BF)
+
+    copy_out(out_ref, scr, sem, make)
 
 
 def fine_kernel(rows_ref, pidx_ref, fine_ref, oct_ref, table_ref, gain_ref, didxt_ref, *rest):
-    sum_ref, out_ref = rest[-2:]
+    sum_ref, out_ref, scr, sem = rest[-4:]
     pick = hot(pidx_ref[...] == iota((FINE, N_SEQ * PSLOTS), 1))
     parents = dot(pick, rows_ref[...])
     octs = dot(hot(upright(oct_ref[...].astype(F32)) == iota((FINE, 8), 1).astype(F32)), table_ref[...])
     fine_sum = fine_ref[...].astype(F32) + parents + octs
     sum_ref[...] = fine_sum
     normed = rms(fine_sum, gain_ref[...]).astype(BF)
-    slot = iota((EXPERTS * SLOTS, FINE), 0)
-    place = hot((didxt_ref[0:1, :] == slot) | (didxt_ref[1:2, :] == slot))
-    out_ref[...] = dot(place, normed).astype(BF)
-
-
-def ffn_kernel(has_extra, at_ref, x_ref, extra_ref, gate_ref, u0, u1, u2, u3, d0, d1, d2, d3, out_ref, gb, ub, db, sem):
+
+    def make(part):
+        slot = part.start + iota((part.stop - part.start, FINE), 0)
+        place = hot((didxt_ref[0:1, :] == slot) | (didxt_ref[1:2, :] == slot))
+        return dot(place, normed).astype(BF)
+
+    copy_out(out_ref, scr, sem, make)
+
+
+def stage_kernel(at_ref, gate_ref, u0_ref, d0_ref, d1_ref, d2_ref, g_ref, u_ref, d_ref, token_ref, sem):
+    token_ref[...] = jnp.zeros_like(token_ref)
     y = at_ref[0, 0]
-    ups, downs = (u0, u1, u2, u3), (d0, d1, d2, d3)
     copies = []
     for j, k in enumerate((0, 1, 3, 2)):
-        places = ((gate_ref.at[around(y, k)], gb), (ups[j].at[0], ub), (downs[j].at[0], db))
-        copies += [
-            pltpu.make_async_copy(src, dst.at[j], sem.at[3 * j + i])
-            for i, (src, dst) in enumerate(places)
-        ]
-    begun = 0
-
-    def ready(i):
-        nonlocal begun
-        while begun < min(i + 4, len(copies)):
-            copies[begun].start()
-            begun += 1
-        copies[i].wait()
-
+        copies.append((gate_ref.at[around(y, k)], g_ref.at[j]))
+    copies.append((u0_ref.at[0], u_ref))
+    for j, d in enumerate((d0_ref, d1_ref, d2_ref)):
+        copies.append((d.at[0], d_ref.at[j]))
+    copies = [pltpu.make_async_copy(src, dst, sem.at[i]) for i, (src, dst) in enumerate(copies)]
+    for c in copies:
+        c.start()
+    for c in copies:
+        c.wait()
+
+
+HBM = pl.BlockSpec(memory_space=pltpu.HBM)
+INNER = pl.BlockSpec(memory_space=pltpu.VMEM)
+SCALAR = pl.BlockSpec(memory_space=pltpu.SMEM)
+
+
+COST = pl.CostEstimate(flops=1, bytes_accessed=1, transcendentals=0)
+
+
+def stage(at, gate, up, downs):
+    return pl.pallas_call(
+        stage_kernel,
+        in_specs=[SCALAR] + [HBM] * 5,
+        out_specs=[INNER] * 4,
+        out_shape=[
+            sds((4, D, 512), BF),
+            sds((D, 512), BF),
+            sds((3, D, 512), BF),
+            sds((8, 128), F32),
+        ],
+        scratch_shapes=[pltpu.SemaphoreType.DMA((8,))],
+        compiler_params=pltpu.CompilerParams(vmem_limit_bytes=53 << 20),
+        cost_estimate=COST,
+    )(at, gate, up, *downs)
+
+
+def swiglu(x, gate, up, down):
+    g = dot(x, gate)
+    u = dot(x, up)
+    return dot_nt((0.5 * g * (1.0 + jnp.tanh(0.5 * g)) * u).astype(BF), down)
+
+
+def first_kernel(x_ref, g_ref, u_ref, d_ref, u1_ref, u2_ref, *rest):
+    out_ref, ups, sem = rest[-3:]
+    copies = [
+        pltpu.make_async_copy(r.at[0], ups.at[j], sem.at[j]) for j, r in enumerate((u1_ref, u2_ref))
+    ]
+    for c in copies:
+        c.start()
     x = x_ref[...]
-    acc = extra_ref[...].astype(F32) if has_extra else None
-    for j in range(N_EXP):
-        ready(3 * j)
-        g = dot(x, gb[j])
-        ready(3 * j + 1)
-        u = dot(x, ub[j])
-        act = (0.5 * g * (1.0 + jnp.tanh(0.5 * g)) * u).astype(BF)
-        ready(3 * j + 2)
-        part = dot_nt(act, db[j])
-        acc = part if acc is None else acc + part
-    out_ref[...] = acc.astype(BF)
-
-
-def ffn(at, x, extra, gate, ups, downs):
+    acc = swiglu(x, g_ref[0], u_ref[...], d_ref[0])
+    for j in (1, 2):
+        copies[j - 1].wait()
+        acc = acc + swiglu(x, g_ref[j], ups[j - 1], d_ref[j])
+    out_ref[...] = acc
+
+
+def first(x, staged, ur, ul, *ready):
     n = EXPERTS * SLOTS
-    has_extra = extra is not None
-    vm = pl.BlockSpec(memory_space=pltpu.VMEM)
-    hbm = pl.BlockSpec(memory_space=pl.ANY)
-    buf = pltpu.VMEM((N_EXP, D, 512), BF)
-    return pl.pallas_call(
-        functools.partial(ffn_kernel, has_extra),
-        in_specs=[pl.BlockSpec(memory_space=pltpu.SMEM), vm, vm if has_extra else hbm] + [hbm] * 9,
-        out_specs=vm,
+    return pl.pallas_call(
+        first_kernel,
+        in_specs=[INNER] * 4 + [HBM] * (2 + len(ready)),
+        out_specs=[INNER] * 2,
+        out_shape=[sds((n, D), F32), sds((2, D, 512), BF)],
+        scratch_shapes=[pltpu.SemaphoreType.DMA((2,))],
+        compiler_params=pltpu.CompilerParams(vmem_limit_bytes=30 << 20),
+        cost_estimate=COST,
+    )(x, *staged, ur, ul, *ready)
+
+
+def second_kernel(x0_ref, x1_ref, x2_ref, x3_ref, g_ref, u_ref, d_ref, ups_ref, out_ref, x_out):
+    x = jnp.concatenate([r[...] for r in (x0_ref, x1_ref, x2_ref, x3_ref)], axis=0)
+    x_out[...] = x
+    acc = swiglu(x, g_ref[0], u_ref[...], d_ref[0])
+    for j in (1, 2):
+        acc = acc + swiglu(x, g_ref[j], ups_ref[j - 1], d_ref[j])
+    out_ref[...] = acc
+
+
+def second(xs, staged, ups):
+    n = EXPERTS * SLOTS
+    return pl.pallas_call(
+        second_kernel,
+        in_specs=[INNER] * 8,
+        out_specs=[INNER] * 2,
+        out_shape=[sds((n, D), F32), sds((n, D), BF)],
+        compiler_params=pltpu.CompilerParams(vmem_limit_bytes=30 << 20),
+        cost_estimate=COST,
+    )(*xs, *staged, ups)
+
+
+def last_kernel(x_ref, acc_ref, g_ref, u_ref, d_ref, out_ref, u_out, d_out, sem):
+    copies = [
+        pltpu.make_async_copy(u_ref.at[0], u_out, sem.at[0]),
+        pltpu.make_async_copy(d_ref.at[0], d_out, sem.at[1]),
+    ]
+    for c in copies:
+        c.start()
+    for c in copies:
+        c.wait()
+    out_ref[...] = (acc_ref[...] + swiglu(x_ref[...], g_ref[3], u_out[...], d_out[...])).astype(BF)
+
+
+def last(x, acc, gate, up, down):
+    n = EXPERTS * SLOTS
+    return pl.pallas_call(
+        last_kernel,
+        in_specs=[INNER] * 3 + [HBM] * 2,
+        out_specs=[INNER] * 3,
+        out_shape=[sds((n, D), BF), sds((D, 512), BF), sds((D, 512), BF)],
+        scratch_shapes=[pltpu.SemaphoreType.DMA((2,))],
+        compiler_params=pltpu.CompilerParams(vmem_limit_bytes=30 << 20),
+        cost_estimate=COST,
+    )(x, acc, gate, up, down)
+
+
+def final_kernel(x_ref, acc_ref, extra_ref, g_ref, u_ref, d_ref, out_ref):
+    acc = acc_ref[...] + swiglu(x_ref[...], g_ref[3], u_ref[...], d_ref[...])
+    out_ref[...] = (acc + extra_ref[...].astype(F32)).astype(BF)
+
+
+def final(x, acc, extra, gate, up, down):
+    n = EXPERTS * SLOTS
+    return pl.pallas_call(
+        final_kernel,
+        in_specs=[INNER] * 6,
+        out_specs=INNER,
         out_shape=sds((n, D), BF),
-        scratch_shapes=[buf, buf, buf, pltpu.SemaphoreType.DMA((12,))],
-        compiler_params=pltpu.CompilerParams(vmem_limit_bytes=54 << 20),
-        cost_estimate=pl.CostEstimate(
-            flops=2 * n * D * 2048 * 3, bytes_accessed=1 << 20, transcendentals=0
-        ),
-    )(at, x, extra if has_extra else x, gate, *ups, *downs)
+        compiler_params=pltpu.CompilerParams(vmem_limit_bytes=30 << 20),
+        cost_estimate=COST,
+    )(x, acc, extra, gate, up, down)
 
 
 def combine_kernel(ret_ref, didx_ref, gates_ref, sum_ref, out_ref):
@@ -344,15 +451,14 @@
     ]
     kv = lax.all_to_all(kv, "seq", 0, 0, tiled=True)
     scale = lax.dynamic_slice(head_scale, (s % 4,), (1,)) * (math.log2(math.e) / math.sqrt(HD))
-    att = call(
+    att, req = call(
         attn_kernel,
-        sds((16, ROWS // 2, 2 * HD), BF),
+        [sds((16, ROWS // 2, 2 * HD), BF), sds((N_SEQ * PSLOTS, ROWS), BF)],
         scale.reshape(1, 1),
         at,
         *qs,
         kv,
         smem=(0, 1),
-        spare=16,
     )
     att = lax.all_to_all(att, ("seq", "exp"), 0, 0, axis_index_groups=SIXTEENS, tiled=True)
     ur, ul = turn(up_weight, 1), turn(up_weight, 3)
@@ -368,12 +474,18 @@
         serve_kernel,
         [sds((ROWS, D), BF), sds((N_SEQ * PSLOTS, D), BF)],
         at,
-        kv,
+        req,
         *pieces,
         smem=(0,),
-        scratch_shapes=[pltpu.VMEM((N_EXP, ROWS, 256), BF)],
+        far=(1,),
+        scratch_shapes=[
+            pltpu.VMEM((N_EXP, ROWS, 256), BF),
+            pltpu.VMEM((N_SEQ * PSLOTS, D), BF),
+            pltpu.SemaphoreType.DMA((4,)),
+        ],
     )
     served = lax.all_to_all(served, "seq", 0, 0, tiled=True)
+    *staged, token = stage(at, gate, up_weight, (down_weight, dr, dl))
     fine_sum, outgoing = call(
         fine_kernel,
         [sds((FINE, D), F32), sds((EXPERTS * SLOTS, D), BF)],
@@ -384,15 +496,22 @@
         octant_table,
         norm3_gain.reshape(1, D),
         didxt,
-        ready=(ur, ul),
+        ready=(ur, ul, token),
+        limit=52,
+        far=(1,),
+        scratch_shapes=[
+            pltpu.VMEM((EXPERTS * SLOTS, D), BF),
+            pltpu.SemaphoreType.DMA((4,)),
+        ],
     )
     mine = lax.all_to_all(outgoing, "seq", 0, 0, tiled=True)
-    other = lax.ppermute(mine, "seq", SWAP)
-    ups = [up_weight, ur, ul, u2]
-    downs = [down_weight, dr, dl, d2]
-    for_other = ffn(at, other, None, gate, ups, downs)
+    mine = mine.reshape(EXPERTS * SLOTS, D)
+    others = [lax.ppermute(mine[i * 128 : i * 128 + 128], "seq", SWAP) for i in range(4)]
+    acc_mine, ups = first(mine, staged, ur, ul)
+    acc_other, other = second(others, staged, ups)
+    for_other, u3, d3 = last(other, acc_other, staged[0], u2, d2)
     from_other = lax.ppermute(for_other, "seq", SWAP)
-    result = ffn(at, mine, from_other, gate, ups, downs)
+    result = final(mine, acc_mine, from_other, staged[0], u3, d3)
     returned = lax.all_to_all(result, "seq", 0, 0, tiled=True)
     fine_out = call(
         combine_kernel, sds((FINE, D), BF), returned, didx, expert_gates.T, fine_sum

time: 232 us -> 217 us (0.935)
  waiting for transfers between devices: 71.7 us -> 53.9 us
  Pallas kernels: 41.7 us -> 50.2 us
  local copies, waits for them, and re-layouts: 12.5 us -> 8.7 us
  blocking collectives: 37.2 us -> 34.3 us
    ppermute x12, waiting for transfers between devices: 36 us -> 15.8 us  [turn(): return lax.ppermute(v, 'exp', [(i, (i + k) % N_EXP) for i in range(N_EXP)])]
    pallas_call x7, Pallas kernels: 11.8 us -> 21.8 us  [call(): pl.pallas_call(kernel, out_shape=out_shape, in_specs=space + [pl.BlockSpe...]
    unnamed x54 -> x64, local copies, waits for them, and re-layouts: 11.9 us -> 8.05 us
    all_to_all x1, blocking collectives: 24.5 us -> 20.8 us  [per_device(): returned = lax.all_to_all(result, 'seq', 0, 0, tiled=True)]
    pallas_call x2 -> x5, Pallas kernels: 24.8 us -> 23.4 us  [the longest x1 7.3 us: stage(): pl.pallas_call(stage_kernel, in_specs=[SCALAR] + [HBM] * 5, out_specs=[IN...]
  transfers between devices with their start and end apart: 23 -> 26, of which waited for: 12 -> 13; matrix products, arithmetic and copies ran while one was open for 0% -> 1% of each run, Pallas kernels for 7% -> 18%
where the time goes in v3:
time: 217 us; the launch traced here: 216 us
  waiting for transfers between devices  53.9 us (25%)
  starting transfers between devices  52.8 us (24%)
  Pallas kernels  50.2 us (23%)
  blocking collectives  34.3 us (16%)
  between operations  15.1 us (7%)
  local copies, waits for them, and re-layouts  8.7 us (4%)
    pallas_call x7, Pallas kernels, call(): pl.pallas_call(kernel, out_shape=out_shape, in_specs=space + [pl.BlockSpe...  21.8 us
    all_to_all x1, blocking collectives, per_device(): returned = lax.all_to_all(result, 'seq', 0, 0, tiled=True)  20.8 us
    ppermute x12, starting transfers between devices, turn(): return lax.ppermute(v, 'exp', [(i, (i + k) % N_EXP) for i in range(N_EXP)])  17.1 us
    ppermute x12, waiting for transfers between devices, turn(): return lax.ppermute(v, 'exp', [(i, (i + k) % N_EXP) for i in range(N_EXP)])  15.8 us
    all_to_all x1, waiting for transfers between devices, per_device(): mine = lax.all_to_all(outgoing, 'seq', 0, 0, tiled=True)  14.2 us
    all_to_all x1, blocking collectives, per_device(): parts = lax.all_to_all(part, 'exp', 0, 0, tiled=True)  13.5 us
    all_to_all x1, starting transfers between devices, per_device(): served = lax.all_to_all(served, 'seq', 0, 0, tiled=True)  10.5 us
    ppermute x3, waiting for transfers between devices, per_device(): lax.ppermute(qs[k], 'seq', [(i, i ^ k) for i in range(N_SEQ)])  9.91 us
  transfers between devices with their start and end apart: 26, of which 13 were waited for; matrix products, arithmetic and copies ran while one was open for 1% of the time, Pallas kernels for 18%

profile of v3, /device:TPU:1, one launch (start us, length us, event | category | flops | bytes accessed | tf_op | source)
XLA Modules:
  0.0 215.7 jit_solution(4666931356803072490)
XLA Ops:
  8.6 3.8 %collective-permute-start.1 = (bf16[128,256]{1,0:T(8,128)(2,1)}, bf16[128,256]{1,0:T(8,128)(2,1)S(1)}, u32[]{:S(2)}, u32[]{:S(2)}) collective-permute-start(bf16[128,256]{1,0:T(8,128)(2,1)} %f0_ref.1), channel_id=1, source_target_pairs={{0,2},{1,3},{2,0},{3,1},{4,6},{5,7},{6,4},{7,5},{8,10},{9,11},{10,... | collective-permute-start | bytes 196616 | tf_op jit(solution)/shard_map/ppermute | solution.py:394
  12.9 2.3 %collective-permute-start.2 = (bf16[128,256]{1,0:T(8,128)(2,1)}, bf16[128,256]{1,0:T(8,128)(2,1)S(1)}, u32[]{:S(2)}, u32[]{:S(2)}) collective-permute-start(bf16[128,256]{1,0:T(8,128)(2,1)} %f0_ref.1), channel_id=1, source_target_pairs={{0,3},{1,0},{2,1},{3,2},{4,7},{5,4},{6,5},{7,6},{8,11},{9,8},{10,9... | collective-permute-start | bytes 196616 | tf_op jit(solution)/shard_map/ppermute | solution.py:394
  18.3 4.1 %shard_map.195 = (bf16[128,1024]{1,0:T(8,128)(2,1)}, bf16[128,128]{1,0:T(8,128)(2,1)}, bf16[128,128]{1,0:T(8,128)(2,1)}, bf16[128,128]{1,0:T(8,128)(2,1)}, bf16[...) custom-call(s32[1,2]{1,0:T(1,128)} %add_bitcast_fusion.at_ref, bf16[128,256]{1,0:T(8,128)(2,1)} %f0_ref.1, ...), custom_call_target="tpu_custom_call" | custom-call | bytes 1 | tf_op jit(solution)/shard_map/pallas_call | solution.py:41
  22.4 9.7 %all-to-all-start = ((bf16[32,144,128]{2,1,0:T(8,128)(2,1)}), bf16[32,144,128]{2,1,0:T(8,128)(2,1)S(1)}, u32[]{:S(2)}, u32[]{:S(2)}) async-start(bf16[32,144,128]{2,1,0:T(8,128)(2,1)} %get-tuple-element.36), calls=%async_computation | async-start | bytes 2359296 | tf_op jit(solution)/shard_map/all_to_all | solution.py:452
  32.2 3.0 %collective-permute-start.7 = (bf16[1,1024,512]{2,1,0:T(8,128)(2,1)}, bf16[1,1024,512]{2,1,0:T(8,128)(2,1)S(1)}, u32[]{:S(2)}, u32[]{:S(2)}) collective-permute-start(bf16[1,1024,512]{2,1,0:T(8,128)(2,1)} %d0_ref.1), channel_id=1, source_target_pairs={{0,3},{1,0},{2,1},{3,2},{4,7},{5,4},{6,5},{7,6},{8,11},{9,8},{10,9... | collective-permute-start | bytes 3145736 | tf_op jit(solution)/shard_map/ppermute | solution.py:394
  38.7 5.4 %collective-permute-done.4.q2_ref = bf16[128,128]{1,0:T(8,128)(2,1)S(1)} collective-permute-done((bf16[128,128]{1,0:T(8,128)(2,1)S(1)}, bf16[128,128]{1,0:T(8,128)(2,1)S(1)}, u32[]{:S(2)}, u32[]{:S(2)}) %collective-permute-start.4) | collective-permute-done | bytes 32800 | tf_op jit(solution)/shard_map/ppermute | solution.py:450
  44.1 4.5 %collective-permute-done.5.q3_ref = bf16[128,128]{1,0:T(8,128)(2,1)S(1)} collective-permute-done((bf16[128,128]{1,0:T(8,128)(2,1)S(1)}, bf16[128,128]{1,0:T(8,128)(2,1)S(1)}, u32[]{:S(2)}, u32[]{:S(2)}) %collective-permute-start.5) | collective-permute-done | bytes 32800 | tf_op jit(solution)/shard_map/ppermute | solution.py:450
  51.5 5.4 %shard_map.196 = (bf16[16,64,128]{2,1,0:T(8,128)(2,1)}, bf16[512,128]{1,0:T(8,128)(2,1)}) custom-call(f32[1,1]{1,0:T(1,128)} %bitcast.3.scale_ref, s32[1,2]{1,0:T(1,128)} %add_bitcast_fusion.at_ref, bf16[128,128]{1,0:T(8,128)(2,1)} %get-tuple-element.32.q0_ref, bf16[128,128]{1,0:T(8,128)(2,1)} %copy-done.25, bf16[128,128]{1,0:T(8,128)(2,1)} %copy-done.26, ...), custom_call_target="tpu_custom_call" | custom-call | bytes 1 | tf_op jit(solution)/shard_map/pallas_call | solution.py:41
  57.0 4.7 %all-to-all-start.1 = ((bf16[16,64,128]{2,1,0:T(8,128)(2,1)}), bf16[16,64,128]{2,1,0:T(8,128)(2,1)S(1)}, u32[]{:S(2)}, u32[]{:S(2)}) async-start(bf16[16,64,128]{2,1,0:T(8,128)(2,1)} %get-tuple-element.38), calls=%async_computation.1 | async-start | bytes 524288 | tf_op jit(solution)/shard_map/all_to_all | solution.py:463
  61.7 4.3 %collective-permute-done.6.rest_0_.d1_ref = bf16[1,1024,512]{2,1,0:T(8,128)(2,1)S(1)} collective-permute-done((bf16[1,1024,512]{2,1,0:T(8,128)(2,1)}, bf16[1,1024,512]{2,1,0:T(8,128)(2,1)S(1)}, u32[]{:S(2)}, u32[]{:S(2)}) %collective-permute-start.6) | collective-permute-done | bytes 1048608 | tf_op jit(solution)/shard_map/ppermute | solution.py:394
  66.0 5.3 %all-to-all-done.1.att_ref = bf16[16,64,128]{2,1,0:T(8,128)(2,1)S(1)} async-done(((bf16[16,64,128]{2,1,0:T(8,128)(2,1)}), bf16[16,64,128]{2,1,0:T(8,128)(2,1)S(1)}, u32[]{:S(2)}, u32[]{:S(2)}) %all-to-all-start.1) | async-done | bytes 262176 | tf_op jit(solution)/shard_map/all_to_all | solution.py:463
  72.0 5.1 %shard_map.197 = (f32[128,256]{1,0:T(8,128)}, bf16[4,128,256]{2,1,0:T(8,128)(2,1)}) custom-call(s32[1,2]{1,0:T(1,128)} %add_bitcast_fusion.at_ref, bf16[16,64,128]{2,1,0:T(8,128)(2,1)} %copy-done.18, bf16[128,1024]{1,0:T(8,128)(2,1)} %get-tuple-element.39.x_ref, f32[1,1024]{1,0:T(1,128)} %bitcast.36, bf16[1024,1024]{1,0:T(8,128)(2,1)} %all-gather.3.cloned.1.call-done.wo_ref, ...), custom_call_target="tpu_custom_call" | custom-call | flops 1 | bytes 1 | tf_op jit(solution)/shard_map/pallas_call | solution.py:181
  77.1 13.5 %all_to_all.48.parts_ref = bf16[4,128,256]{2,1,0:T(8,128)(2,1)} all-to-all(bf16[4,128,256]{2,1,0:T(8,128)(2,1)} %get-tuple-element.40), channel_id=1, replica_groups=mesh['seq'=32,'exp'=4] {'exp'}, dimensions={0} | all-to-all | bytes 524288 | tf_op jit(solution)/shard_map/all_to_all | solution.py:470
  97.3 2.0 collective-permute-done.9.c2_ref
  99.3 1.9 collective-permute-done.8.c1_ref
  101.9 3.0 %shard_map.199 = (bf16[128,1024]{1,0:T(8,128)(2,1)}, bf16[512,1024]{1,0:T(8,128)(2,1)}) custom-call(s32[1,2]{1,0:T(1,128)} %add_bitcast_fusion.at_ref, bf16[512,128]{1,0:T(8,128)(2,1)} %get-tuple-element.37.req_ref, bf16[128,256]{1,0:T(8,128)(2,1)} %shard_map.198.c0_ref, bf16[128,256]{1,0:T(8,128)(2,1)} %copy-done.24, bf16[128,256]{1,0:T(8,128)(2,1)} %copy-done.23, ...), custom_call_target="tpu_custom_call" | custom-call | bytes 1 | tf_op jit(solution)/shard_map/pallas_call | solution.py:41
  104.9 10.5 %all-to-all-start.3 = ((bf16[32,16,1024]{2,1,0:T(8,128)(2,1)}), bf16[32,16,1024]{2,1,0:T(8,128)(2,1)}, u32[]{:S(2)}, u32[]{:S(2)}) async-start(bf16[32,16,1024]{2,1,0:T(8,128)(2,1)} %bitcast.29), calls=%async_computation.3 | async-start | bytes 2097152 | tf_op jit(solution)/shard_map/all_to_all | solution.py:487
  115.5 7.3 %shard_map.200 = (bf16[4,1024,512]{2,1,0:T(8,128)(2,1)}, bf16[1024,512]{1,0:T(8,128)(2,1)}, bf16[3,1024,512]{2,1,0:T(8,128)(2,1)}, f32[8,128]{1,0:T(8,128)S(1)}) custom-call(s32[1,2]{1,0:T(1,128)S(1)} %copy-done.11, bf16[4,1024,512]{2,1,0:T(8,128)(2,1)} %all-gather.5.cloned.1.call-done.gate_ref, bf16[1,1024,512]{2,1,0:T(8,128)(2,1)} %u0_ref.1, ...), custom_call_target="tpu_custom_call" | custom-call | flops 1 | bytes 1 | tf_op jit(solution)/shard_map/pallas_call | solution.py:271
  122.8 7.2 %collective-permute-done.11.rest_0_.u1_ref = bf16[1,1024,512]{2,1,0:T(8,128)(2,1)S(1)} collective-permute-done((bf16[1,1024,512]{2,1,0:T(8,128)(2,1)}, bf16[1,1024,512]{2,1,0:T(8,128)(2,1)S(1)}, u32[]{:S(2)}, u32[]{:S(2)}) %collective-permute-start.11) | collective-permute-done | bytes 1048608 | tf_op jit(solution)/shard_map/ppermute | solution.py:394
  130.0 2.3 %all-to-all-done.3 = bf16[32,16,1024]{2,1,0:T(8,128)(2,1)} async-done(((bf16[32,16,1024]{2,1,0:T(8,128)(2,1)}), bf16[32,16,1024]{2,1,0:T(8,128)(2,1)}, u32[]{:S(2)}, u32[]{:S(2)}) %all-to-all-start.3) | async-done | bytes 1048608 | tf_op jit(solution)/shard_map/all_to_all | solution.py:487
  132.4 3.0 %shard_map.201 = (f32[160,1024]{1,0:T(8,128)S(1)}, bf16[512,1024]{1,0:T(8,128)(2,1)}) custom-call(bf16[512,1024]{1,0:T(8,128)(2,1)} %bitcast.10.rows_ref, s32[160,1]{1,0:T(8,128)S(1)} %copy-done.9, bf16[160,1024]{1,0:T(8,128)(2,1)S(1)} %copy-done.8, s32[1,160]{1,0:T(1,128)S(1)} %bitcast.27, bf16[8,1024]{1,0:T(8,128)(2,1)S(1)} %copy-done.10, ...), custom_call_target="tpu_custom_call" | custom-call | bytes 1 | tf_op jit(solution)/shard_map/pallas_call | solution.py:41
  136.3 7.3 %all-to-all-start.4 = ((bf16[32,16,1024]{2,1,0:T(8,128)(2,1)}), bf16[32,16,1024]{2,1,0:T(8,128)(2,1)S(1)}, u32[]{:S(2)}, u32[]{:S(2)}) async-start(bf16[32,16,1024]{2,1,0:T(8,128)(2,1)} %bitcast.30), calls=%async_computation.4 | async-start | bytes 2097152 | tf_op jit(solution)/shard_map/all_to_all | solution.py:507
  143.6 2.7 %collective-permute-start.18 = (bf16[1,1024,512]{2,1,0:T(8,128)(2,1)}, bf16[1,1024,512]{2,1,0:T(8,128)(2,1)}, u32[]{:S(2)}, u32[]{:S(2)}) collective-permute-start(bf16[1,1024,512]{2,1,0:T(8,128)(2,1)} %copy-done.16), channel_id=1, source_target_pairs={{0,3},{1,0},{2,1},{3,2},{4,7},{5,4},{6,5},{7,6},{8,11},{9,8},{10,9... | collective-permute-start | bytes 3145736 | tf_op jit(solution)/shard_map/ppermute | solution.py:394
  146.3 14.2 %all-to-all-done.4 = bf16[32,16,1024]{2,1,0:T(8,128)(2,1)S(1)} async-done(((bf16[32,16,1024]{2,1,0:T(8,128)(2,1)}), bf16[32,16,1024]{2,1,0:T(8,128)(2,1)S(1)}, u32[]{:S(2)}, u32[]{:S(2)}) %all-to-all-start.4) | async-done | bytes 1048608 | tf_op jit(solution)/shard_map/all_to_all | solution.py:507
  162.3 2.2 %copy-done = bf16[4,1024,512]{2,1,0:T(8,128)(2,1)S(1)} copy-done((bf16[4,1024,512]{2,1,0:T(8,128)(2,1)S(1)}, bf16[4,1024,512]{2,1,0:T(8,128)(2,1)}, u32[]{:S(2)}) %copy-start) | copy-done | bytes 4194328
  164.5 1.9 copy-done.1
  166.4 5.7 %shard_map.202 = (f32[512,1024]{1,0:T(8,128)S(1)}, bf16[2,1024,512]{2,1,0:T(8,128)(2,1)S(1)}) custom-call(bf16[512,1024]{1,0:T(8,128)(2,1)S(1)} %bitcast.23, bf16[4,1024,512]{2,1,0:T(8,128)(2,1)S(1)} %copy-done, bf16[1024,512]{1,0:T(8,128)(2,1)S(1)} %copy-done.6, bf16[3,1024,512]{2,1,0:T(8,128)(2,1)S(1)} %copy-done.1, bf16[1,1024,512]{2,1,0:T(8,128)(2,1)S(1)} %copy-done.3, ...), custom_call_target="tpu_custom_call" | custom-call | flops 1 | bytes 1 | tf_op jit(solution)/shard_map/pallas_call | solution.py:310
  172.1 5.2 %shard_map.203 = (f32[512,1024]{1,0:T(8,128)S(1)}, bf16[512,1024]{1,0:T(8,128)(2,1)S(1)}) custom-call(bf16[128,1024]{1,0:T(8,128)(2,1)S(1)} %collective-permute-done.13.x0_ref, bf16[128,1024]{1,0:T(8,128)(2,1)S(1)} %collective-permute-done.14.x1_ref, bf16[128,1024]{1,0:T(8,128)(2,1)S(1)} %collective-permute-done.15.x2_ref, ...), custom_call_target="tpu_custom_call" | custom-call | flops 1 | bytes 1 | tf_op jit(solution)/shard_map/pallas_call | solution.py:332
  177.3 3.4 %shard_map.204 = (bf16[512,1024]{1,0:T(8,128)(2,1)S(1)}, bf16[1024,512]{1,0:T(8,128)(2,1)S(1)}, bf16[1024,512]{1,0:T(8,128)(2,1)S(1)}) custom-call(bf16[512,1024]{1,0:T(8,128)(2,1)S(1)} %get-tuple-element.53.x_ref, f32[512,1024]{1,0:T(8,128)S(1)} %get-tuple-element.54.acc_ref, bf16[4,1024,512]{2,1,0:T(8,128)(2,1)S(1)} %copy-done, ...), custom_call_target="tpu_custom_call" | custom-call | flops 1 | bytes 1 | tf_op jit(solution)/shard_map/pallas_call | solution.py:356
  181.2 2.3 %collective-permute-done.19.extra_ref = bf16[512,1024]{1,0:T(8,128)(2,1)S(1)} collective-permute-done((bf16[512,1024]{1,0:T(8,128)(2,1)S(1)}, bf16[512,1024]{1,0:T(8,128)(2,1)S(1)}, u32[]{:S(2)}, u32[]{:S(2)}) %collective-permute-start.19) | collective-permute-done | bytes 1048608 | tf_op jit(solution)/shard_map/ppermute | solution.py:513
  185.3 20.8 %all_to_all.49 = bf16[32,16,1024]{2,1,0:T(8,128)(2,1)} all-to-all(bf16[32,16,1024]{2,1,0:T(8,128)(2,1)S(1)} %bitcast.25), channel_id=1, replica_groups=mesh['seq'=32,'exp'=4] {'seq'}, dimensions={0} | all-to-all | bytes 2097152 | tf_op jit(solution)/shard_map/all_to_all | solution.py:515
  206.1 2.8 %shard_map.206 = bf16[160,1024]{1,0:T(8,128)(2,1)} custom-call(bf16[512,1024]{1,0:T(8,128)(2,1)} %bitcast.28, s32[160,2]{1,0:T(8,128)} %get-tuple-element.58.didx_ref, f32[2,160]{1,0:T(2,128)} %bitcast.37, f32[160,1024]{1,0:T(8,128)} %copy-done.7), custom_call_target="tpu_custom_call" | custom-call | bytes 1 | tf_op jit(solution)/shard_map/pallas_call | solution.py:41
  (104 shorter events, 24.1 us)
Async XLA Ops:
  7.2 64.1 %all-gather.3.cloned.1.call-start = ((), (), s32[]{:S(2)}) async-start(), calls=%async_computation.6 | async-start | bytes 2621440 | tf_op jit(solution)/shard_map/all_gather | solution.py:422
  7.9 107.6 %all-gather.5.cloned.1.call-start = ((), (), s32[]{:S(2)}) async-start(), calls=%async_computation.7 | async-start | bytes 5242880 | tf_op jit(solution)/shard_map/all_gather | solution.py:423
  8.6 9.0 %collective-permute-start.1 = (bf16[128,256]{1,0:T(8,128)(2,1)}, bf16[128,256]{1,0:T(8,128)(2,1)S(1)}, u32[]{:S(2)}, u32[]{:S(2)}) collective-permute-start(bf16[128,256]{1,0:T(8,128)(2,1)} %f0_ref.1), channel_id=1, source_target_pairs={{0,2},{1,3},{2,0},{3,1},{4,6},{5,7},{6,4},{7,5},{8,10},{9,11},{10,... | collective-permute-start | bytes 196616 | tf_op jit(solution)/shard_map/ppermute | solution.py:394
  12.5 5.2 %collective-permute-start = (bf16[128,256]{1,0:T(8,128)(2,1)}, bf16[128,256]{1,0:T(8,128)(2,1)S(1)}, u32[]{:S(2)}, u32[]{:S(2)}) collective-permute-start(bf16[128,256]{1,0:T(8,128)(2,1)} %f0_ref.1), channel_id=1, source_target_pairs={{0,1},{1,2},{2,3},{3,0},{4,5},{5,6},{6,7},{7,4},{8,9},{9,10},{10,1... | collective-permute-start | bytes 196616 | tf_op jit(solution)/shard_map/ppermute | solution.py:394
  12.9 4.8 %collective-permute-start.2 = (bf16[128,256]{1,0:T(8,128)(2,1)}, bf16[128,256]{1,0:T(8,128)(2,1)S(1)}, u32[]{:S(2)}, u32[]{:S(2)}) collective-permute-start(bf16[128,256]{1,0:T(8,128)(2,1)} %f0_ref.1), channel_id=1, source_target_pairs={{0,3},{1,0},{2,1},{3,2},{4,7},{5,4},{6,5},{7,6},{8,11},{9,8},{10,9... | collective-permute-start | bytes 196616 | tf_op jit(solution)/shard_map/ppermute | solution.py:394
  18.3 19.1 %copy-start.31 = (f32[4]{0:T(128)S(1)}, f32[4]{0:T(128)}, u32[]{:S(2)}) copy-start(f32[4]{0:T(128)} %param.22) | copy-start | bytes 52
  22.4 28.0 %all-to-all-start = ((bf16[32,144,128]{2,1,0:T(8,128)(2,1)}), bf16[32,144,128]{2,1,0:T(8,128)(2,1)S(1)}, u32[]{:S(2)}, u32[]{:S(2)}) async-start(bf16[32,144,128]{2,1,0:T(8,128)(2,1)} %get-tuple-element.36), calls=%async_computation | async-start | bytes 2359296 | tf_op jit(solution)/shard_map/all_to_all | solution.py:452
  32.1 33.9 %collective-permute-start.6 = (bf16[1,1024,512]{2,1,0:T(8,128)(2,1)}, bf16[1,1024,512]{2,1,0:T(8,128)(2,1)S(1)}, u32[]{:S(2)}, u32[]{:S(2)}) collective-permute-start(bf16[1,1024,512]{2,1,0:T(8,128)(2,1)} %d0_ref.1), channel_id=1, source_target_pairs={{0,1},{1,2},{2,3},{3,0},{4,5},{5,6},{6,7},{7,4},{8,9},{9,10},{10,1... | collective-permute-start | bytes 3145736 | tf_op jit(solution)/shard_map/ppermute | solution.py:394
  32.2 33.8 %collective-permute-start.7 = (bf16[1,1024,512]{2,1,0:T(8,128)(2,1)}, bf16[1,1024,512]{2,1,0:T(8,128)(2,1)S(1)}, u32[]{:S(2)}, u32[]{:S(2)}) collective-permute-start(bf16[1,1024,512]{2,1,0:T(8,128)(2,1)} %d0_ref.1), channel_id=1, source_target_pairs={{0,3},{1,0},{2,1},{3,2},{4,7},{5,4},{6,5},{7,6},{8,11},{9,8},{10,9... | collective-permute-start | bytes 3145736 | tf_op jit(solution)/shard_map/ppermute | solution.py:394
  35.2 3.5 %collective-permute-start.3 = (bf16[128,128]{1,0:T(8,128)(2,1)S(1)}, bf16[128,128]{1,0:T(8,128)(2,1)S(1)}, u32[]{:S(2)}, u32[]{:S(2)}) collective-permute-start(bf16[128,128]{1,0:T(8,128)(2,1)S(1)} %copy-done.30), channel_id=1, source_target_pairs={{0,4},{4,0},{8,12},{12,8},{16,20},{20,16},{24,28},{28,24},{32,36},... | collective-permute-start | bytes 98312 | tf_op jit(solution)/shard_map/ppermute | solution.py:450
  35.7 8.4 %collective-permute-start.4 = (bf16[128,128]{1,0:T(8,128)(2,1)S(1)}, bf16[128,128]{1,0:T(8,128)(2,1)S(1)}, u32[]{:S(2)}, u32[]{:S(2)}) collective-permute-start(bf16[128,128]{1,0:T(8,128)(2,1)S(1)} %copy-done.29), channel_id=1, source_target_pairs={{0,8},{4,12},{8,0},{12,4},{16,24},{20,28},{24,16},{28,20},{32,40},... | collective-permute-start | bytes 98312 | tf_op jit(solution)/shard_map/ppermute | solution.py:450
  37.2 11.4 %collective-permute-start.5 = (bf16[128,128]{1,0:T(8,128)(2,1)S(1)}, bf16[128,128]{1,0:T(8,128)(2,1)S(1)}, u32[]{:S(2)}, u32[]{:S(2)}) collective-permute-start(bf16[128,128]{1,0:T(8,128)(2,1)S(1)} %copy-done.28), channel_id=1, source_target_pairs={{0,12},{4,8},{8,4},{12,0},{16,28},{20,24},{24,20},{28,16},{32,44},... | collective-permute-start | bytes 98312 | tf_op jit(solution)/shard_map/ppermute | solution.py:450
  57.0 14.3 %all-to-all-start.1 = ((bf16[16,64,128]{2,1,0:T(8,128)(2,1)}), bf16[16,64,128]{2,1,0:T(8,128)(2,1)S(1)}, u32[]{:S(2)}, u32[]{:S(2)}) async-start(bf16[16,64,128]{2,1,0:T(8,128)(2,1)} %get-tuple-element.38), calls=%async_computation.1 | async-start | bytes 524288 | tf_op jit(solution)/shard_map/all_to_all | solution.py:463
  77.0 38.4 %copy-start.11 = (s32[1,2]{1,0:T(1,128)S(1)}, s32[1,2]{1,0:T(1,128)}, u32[]{:S(2)}) copy-start(s32[1,2]{1,0:T(1,128)} %add_bitcast_fusion.at_ref) | copy-start | bytes 28
  92.2 5.1 %collective-permute-start.10 = (bf16[128,256]{1,0:T(8,128)(2,1)}, bf16[128,256]{1,0:T(8,128)(2,1)S(1)}, u32[]{:S(2)}, u32[]{:S(2)}) collective-permute-start(bf16[128,256]{1,0:T(8,128)(2,1)} %shard_map.198.c0_ref), channel_id=1, source_target_pairs={{0,3},{1,0},{2,1},{3,2},{4,7},{5,4},{6,5},{7,6},{8,11},{9,8},{10,9... | collective-permute-start | bytes 196616 | tf_op jit(solution)/shard_map/ppermute | solution.py:394
  93.1 6.3 %collective-permute-start.9 = (bf16[128,256]{1,0:T(8,128)(2,1)}, bf16[128,256]{1,0:T(8,128)(2,1)S(1)}, u32[]{:S(2)}, u32[]{:S(2)}) collective-permute-start(bf16[128,256]{1,0:T(8,128)(2,1)} %shard_map.198.c0_ref), channel_id=1, source_target_pairs={{0,2},{1,3},{2,0},{3,1},{4,6},{5,7},{6,4},{7,5},{8,10},{9,11},{10,... | collective-permute-start | bytes 196616 | tf_op jit(solution)/shard_map/ppermute | solution.py:394
  94.3 7.0 %collective-permute-start.8 = (bf16[128,256]{1,0:T(8,128)(2,1)}, bf16[128,256]{1,0:T(8,128)(2,1)S(1)}, u32[]{:S(2)}, u32[]{:S(2)}) collective-permute-start(bf16[128,256]{1,0:T(8,128)(2,1)} %shard_map.198.c0_ref), channel_id=1, source_target_pairs={{0,1},{1,2},{2,3},{3,0},{4,5},{5,6},{6,7},{7,4},{8,9},{9,10},{10,1... | collective-permute-start | bytes 196616 | tf_op jit(solution)/shard_map/ppermute | solution.py:394
  94.3 35.8 %collective-permute-start.11 = (bf16[1,1024,512]{2,1,0:T(8,128)(2,1)}, bf16[1,1024,512]{2,1,0:T(8,128)(2,1)S(1)}, u32[]{:S(2)}, u32[]{:S(2)}) collective-permute-start(bf16[1,1024,512]{2,1,0:T(8,128)(2,1)} %u0_ref.1), channel_id=1, source_target_pairs={{0,1},{1,2},{2,3},{3,0},{4,5},{5,6},{6,7},{7,4},{8,9},{9,10},{10,1... | collective-permute-start | bytes 3145736 | tf_op jit(solution)/shard_map/ppermute | solution.py:394
  95.7 34.3 %collective-permute-start.12 = (bf16[1,1024,512]{2,1,0:T(8,128)(2,1)}, bf16[1,1024,512]{2,1,0:T(8,128)(2,1)S(1)}, u32[]{:S(2)}, u32[]{:S(2)}) collective-permute-start(bf16[1,1024,512]{2,1,0:T(8,128)(2,1)} %u0_ref.1), channel_id=1, source_target_pairs={{0,3},{1,0},{2,1},{3,2},{4,7},{5,4},{6,5},{7,6},{8,11},{9,8},{10,9... | collective-permute-start | bytes 3145736 | tf_op jit(solution)/shard_map/ppermute | solution.py:394
  104.9 27.5 %all-to-all-start.3 = ((bf16[32,16,1024]{2,1,0:T(8,128)(2,1)}), bf16[32,16,1024]{2,1,0:T(8,128)(2,1)}, u32[]{:S(2)}, u32[]{:S(2)}) async-start(bf16[32,16,1024]{2,1,0:T(8,128)(2,1)} %bitcast.29), calls=%async_computation.3 | async-start | bytes 2097152 | tf_op jit(solution)/shard_map/all_to_all | solution.py:487
  115.4 17.0 %copy-start.8 = (bf16[160,1024]{1,0:T(8,128)(2,1)S(1)}, bf16[160,1024]{1,0:T(8,128)(2,1)}, u32[]{:S(2)}) copy-start(bf16[160,1024]{1,0:T(8,128)(2,1)} %fine_ref.1) | copy-start | bytes 983044
  115.4 17.0 %copy-start.9 = (s32[160,1]{1,0:T(8,128)S(1)}, s32[160,1]{1,0:T(8,128)}, u32[]{:S(2)}) copy-start(s32[160,1]{1,0:T(8,128)} %get-tuple-element.44.pidx_ref) | copy-start | bytes 1924
  115.4 17.0 %copy-start.10 = (bf16[8,1024]{1,0:T(8,128)(2,1)S(1)}, bf16[8,1024]{1,0:T(8,128)(2,1)}, u32[]{:S(2)}) copy-start(bf16[8,1024]{1,0:T(8,128)(2,1)} %table_ref.1) | copy-start | bytes 49156
  136.3 26.0 %copy-start.5 = (bf16[1,1024,512]{2,1,0:T(8,128)(2,1)S(1)}, bf16[1,1024,512]{2,1,0:T(8,128)(2,1)}, u32[]{:S(2)}) copy-start(bf16[1,1024,512]{2,1,0:T(8,128)(2,1)} %copy-done.4) | copy-start | bytes 3145732
  136.3 24.2 %all-to-all-start.4 = ((bf16[32,16,1024]{2,1,0:T(8,128)(2,1)}), bf16[32,16,1024]{2,1,0:T(8,128)(2,1)S(1)}, u32[]{:S(2)}, u32[]{:S(2)}) async-start(bf16[32,16,1024]{2,1,0:T(8,128)(2,1)} %bitcast.30), calls=%async_computation.4 | async-start | bytes 2097152 | tf_op jit(solution)/shard_map/all_to_all | solution.py:507
  143.5 33.7 %collective-permute-start.17 = (bf16[1,1024,512]{2,1,0:T(8,128)(2,1)S(1)}, bf16[1,1024,512]{2,1,0:T(8,128)(2,1)}, u32[]{:S(2)}, u32[]{:S(2)}) collective-permute-start(bf16[1,1024,512]{2,1,0:T(8,128)(2,1)S(1)} %copy-done.3), channel_id=1, source_target_pairs={{0,1},{1,2},{2,3},{3,0},{4,5},{5,6},{6,7},{7,4},{8,9},{9,10},{10,1... | collective-permute-start | bytes 3145736 | tf_op jit(solution)/shard_map/ppermute | solution.py:394
  143.6 33.7 %collective-permute-start.18 = (bf16[1,1024,512]{2,1,0:T(8,128)(2,1)}, bf16[1,1024,512]{2,1,0:T(8,128)(2,1)}, u32[]{:S(2)}, u32[]{:S(2)}) collective-permute-start(bf16[1,1024,512]{2,1,0:T(8,128)(2,1)} %copy-done.16), channel_id=1, source_target_pairs={{0,3},{1,0},{2,1},{3,2},{4,7},{5,4},{6,5},{7,6},{8,11},{9,8},{10,9... | collective-permute-start | bytes 3145736 | tf_op jit(solution)/shard_map/ppermute | solution.py:394
  160.5 1.6 collective-permute-start.15
  160.7 11.3 %collective-permute-start.16 = (bf16[128,1024]{1,0:T(8,128)(2,1)S(1)}, bf16[128,1024]{1,0:T(8,128)(2,1)S(1)}, u32[]{:S(2)}, u32[]{:S(2)}) collective-permute-start(bf16[128,1024]{1,0:T(8,128)(2,1)S(1)} %bitcast.33), channel_id=1, source_target_pairs={{0,4},{4,0},{8,12},{12,8},{16,20},{20,16},{24,28},{28,24},{32,36},... | collective-permute-start | bytes 786440 | tf_op jit(solution)/shard_map/ppermute | solution.py:509
  161.1 11.0 %collective-permute-start.14 = (bf16[128,1024]{1,0:T(8,128)(2,1)S(1)}, bf16[128,1024]{1,0:T(8,128)(2,1)S(1)}, u32[]{:S(2)}, u32[]{:S(2)}) collective-permute-start(bf16[128,1024]{1,0:T(8,128)(2,1)S(1)} %bitcast.32), channel_id=1, source_target_pairs={{0,4},{4,0},{8,12},{12,8},{16,20},{20,16},{24,28},{28,24},{32,36},... | collective-permute-start | bytes 786440 | tf_op jit(solution)/shard_map/ppermute | solution.py:509
  162.1 10.0 %collective-permute-start.13 = (bf16[128,1024]{1,0:T(8,128)(2,1)S(1)}, bf16[128,1024]{1,0:T(8,128)(2,1)S(1)}, u32[]{:S(2)}, u32[]{:S(2)}) collective-permute-start(bf16[128,1024]{1,0:T(8,128)(2,1)S(1)} %bitcast.31), channel_id=1, source_target_pairs={{0,4},{4,0},{8,12},{12,8},{16,20},{20,16},{24,28},{28,24},{32,36},... | collective-permute-start | bytes 786440 | tf_op jit(solution)/shard_map/ppermute | solution.py:509
  180.7 2.7 %collective-permute-start.19 = (bf16[512,1024]{1,0:T(8,128)(2,1)S(1)}, bf16[512,1024]{1,0:T(8,128)(2,1)S(1)}, u32[]{:S(2)}, u32[]{:S(2)}) collective-permute-start(bf16[512,1024]{1,0:T(8,128)(2,1)S(1)} %get-tuple-element.55), channel_id=1, source_target_pairs={{0,4},{4,0},{8,12},{12,8},{16,20},{20,16},{24,28},{28,24},{32,36},... | collective-permute-start | bytes 3145736 | tf_op jit(solution)/shard_map/ppermute | solution.py:513
  (26 other events, 151.3 us)
Sparse Core Ops, SparseCore 0:
  9.7 40.8 all-gather.2
  52.2 61.6 all-gather.4

commit v4 on v3

--- a/solution.py
+++ b/solution.py
@@ -142,7 +142,7 @@
 
 
 def block_kernel(at_ref, att_ref, x_ref, gain_ref, wo_ref, win_ref, wout_ref, *rest):
-    mixed_ref, part_ref, scr, wbuf, sem = rest[-5:]
+    mixed_ref, p0_ref, p1_ref, p2_ref, p3_ref, scr, pieces, wbuf, sem = rest[-9:]
     copies = [
         pltpu.make_async_copy(src, dst, sem.at[i])
         for i, (src, dst) in enumerate(
@@ -172,7 +172,9 @@
     copies[2].wait()
     part = dot(inner, wbuf[2]).astype(BF)
     for c in range(N_EXP):
-        part_ref[c] = part[:, c * 256 : (c + 1) * 256]
+        pieces[c] = part[:, c * 256 : (c + 1) * 256]
+    for k, p_ref in enumerate((p0_ref, p1_ref, p2_ref, p3_ref)):
+        p_ref[...] = pieces[lax.rem(at_ref[0, 0] + k, N_EXP)]
 
 
 def block(at, att, x, gain, wo, win, wout, *ready):
@@ -181,10 +183,11 @@
     return pl.pallas_call(
         block_kernel,
         in_specs=[pl.BlockSpec(memory_space=pltpu.SMEM), vm, vm, vm] + [hbm] * (3 + len(ready)),
-        out_specs=[vm, vm],
-        out_shape=[sds((ROWS, 256), F32), sds((N_EXP, ROWS, 256), BF)],
+        out_specs=[vm] * 5,
+        out_shape=[sds((ROWS, 256), F32)] + [sds((ROWS, 256), BF)] * 4,
         scratch_shapes=[
             pltpu.VMEM((N_EXP, ROWS, 256), F32),
+            pltpu.VMEM((N_EXP, ROWS, 256), BF),
             pltpu.VMEM((3, D, D), BF),
             pltpu.SemaphoreType.DMA((3,)),
         ],
@@ -193,10 +196,10 @@
     )(at, att, x, gain, wo, win, wout, *ready)
 
 
-def coarse_kernel(parts_ref, mixed_ref, out_ref):
-    total = parts_ref[0].astype(F32)
-    for c in range(1, N_EXP):
-        total = total + parts_ref[c].astype(F32)
+def coarse_kernel(p0_ref, p1_ref, p2_ref, p3_ref, mixed_ref, out_ref):
+    total = p0_ref[...].astype(F32)
+    for p_ref in (p1_ref, p2_ref, p3_ref):
+        total = total + p_ref[...].astype(F32)
     out_ref[...] = (mixed_ref[...] + total).astype(BF)
 
 
@@ -346,9 +349,13 @@
     ]
     for c in copies:
         c.start()
-    for c in copies:
-        c.wait()
-    out_ref[...] = (acc_ref[...] + swiglu(x_ref[...], g_ref[3], u_out[...], d_out[...])).astype(BF)
+    x = x_ref[...]
+    g = dot(x, g_ref[3])
+    copies[0].wait()
+    u = dot(x, u_out[...])
+    act = (0.5 * g * (1.0 + jnp.tanh(0.5 * g)) * u).astype(BF)
+    copies[1].wait()
+    out_ref[...] = (acc_ref[...] + dot_nt(act, d_out[...])).astype(BF)
 
 
 def last(x, acc, gate, up, down):
@@ -459,16 +466,17 @@
         *qs,
         kv,
         smem=(0, 1),
+        limit=24,
     )
     att = lax.all_to_all(att, ("seq", "exp"), 0, 0, axis_index_groups=SIXTEENS, tiled=True)
     ur, ul = turn(up_weight, 1), turn(up_weight, 3)
     dr, dl = turn(down_weight, 1), turn(down_weight, 3)
     u2, d2 = turn(ur, 1), turn(dl, 3)
-    mixed, part = block(
+    mixed, *parts = block(
         at, att, x, norm2_gain.reshape(1, D), wo, mlp_in, mlp_out, dr, dl
     )
-    parts = lax.all_to_all(part, "exp", 0, 0, tiled=True)
-    piece = call(coarse_kernel, sds((ROWS, 256), BF), parts, mixed)
+    parts = [parts[0]] + [turn(parts[k], k) for k in (1, 2, 3)]
+    piece = call(coarse_kernel, sds((ROWS, 256), BF), *parts, mixed, limit=8)
     pieces = [piece] + [turn(piece, k) for k in (1, 2, 3)]
     coarse_new, served = call(
         serve_kernel,
@@ -497,7 +505,7 @@
         norm3_gain.reshape(1, D),
         didxt,
         ready=(ur, ul, token),
-        limit=52,
+        limit=60,
         far=(1,),
         scratch_shapes=[
             pltpu.VMEM((EXPERTS * SLOTS, D), BF),
@@ -514,7 +522,7 @@
     result = final(mine, acc_mine, from_other, staged[0], u3, d3)
     returned = lax.all_to_all(result, "seq", 0, 0, tiled=True)
     fine_out = call(
-        combine_kernel, sds((FINE, D), BF), returned, didx, expert_gates.T, fine_sum
+        combine_kernel, sds((FINE, D), BF), returned, didx, expert_gates.T, fine_sum, limit=12
     )
     return (coarse_new, fine_out)
 

time: 217 us -> 215 us (level)
  blocking collectives: 34.3 us -> 20.8 us
  waiting for transfers between devices: 53.9 us -> 64.4 us
  Pallas kernels: 50.2 us -> 46.9 us
  starting transfers between devices: 52.8 us -> 55.6 us
    all_to_all x1 -> x0, blocking collectives: 13.5 us -> none  [per_device(): parts = lax.all_to_all(part, 'exp', 0, 0, tiled=True)]
    all_gather x1, waiting for transfers between devices: 0.02 us -> 7 us  [per_device(): gate = lax.all_gather(gate_weight, 'exp', axis=0, tiled=True)]
    ppermute x12 -> x15, waiting for transfers between devices: 15.8 us -> 21.9 us  [turn(): return lax.ppermute(v, 'exp', [(i, (i + k) % N_EXP) for i in range(N_EXP)])]
    pallas_call x7, Pallas kernels: 21.8 us -> 18.9 us  [call(): pl.pallas_call(kernel, out_shape=out_shape, in_specs=space + [pl.BlockSpe...]
    ppermute x12 -> x15, starting transfers between devices: 17.1 us -> 19.9 us  [turn(): return lax.ppermute(v, 'exp', [(i, (i + k) % N_EXP) for i in range(N_EXP)])]
    all_to_all x1, waiting for transfers between devices: 2.31 us -> 0.01 us  [per_device(): served = lax.all_to_all(served, 'seq', 0, 0, tiled=True)]
  transfers between devices with their start and end apart: 26 -> 29, of which waited for: 13 -> 16; matrix products, arithmetic and copies ran while one was open for 1% -> 1% of each run, Pallas kernels for 18% -> 17%
where the time goes in v4:
time: 215 us; the launch traced here: 214 us
  waiting for transfers between devices  64.4 us (30%)
  starting transfers between devices  55.6 us (26%)
  Pallas kernels  46.9 us (22%)
  blocking collectives  20.8 us (10%)
  between operations  15 us (7%)
  local copies, waits for them, and re-layouts  10.5 us (5%)
    ppermute x15, waiting for transfers between devices, turn(): return lax.ppermute(v, 'exp', [(i, (i + k) % N_EXP) for i in range(N_EXP)])  21.9 us
    all_to_all x1, blocking collectives, per_device(): returned = lax.all_to_all(result, 'seq', 0, 0, tiled=True)  20.8 us
    ppermute x15, starting transfers between devices, turn(): return lax.ppermute(v, 'exp', [(i, (i + k) % N_EXP) for i in range(N_EXP)])  19.9 us
    pallas_call x7, Pallas kernels, call(): pl.pallas_call(kernel, out_shape=out_shape, in_specs=space + [pl.BlockSpe...  18.9 us
    all_to_all x1, waiting for transfers between devices, per_device(): mine = lax.all_to_all(outgoing, 'seq', 0, 0, tiled=True)  14.2 us
    unnamed x64, local copies, waits for them, and re-layouts  9.85 us
    ppermute x3, waiting for transfers between devices, per_device(): lax.ppermute(qs[k], 'seq', [(i, i ^ k) for i in range(N_SEQ)])  9.84 us
    all_to_all x1, starting transfers between devices, per_device(): kv = lax.all_to_all(kv, 'seq', 0, 0, tiled=True)  9.69 us
  transfers between devices with their start and end apart: 29, of which 16 were waited for; matrix products, arithmetic and copies ran while one was open for 1% of the time, Pallas kernels for 17%

profile of v4, /device:TPU:1, one launch (start us, length us, event | category | flops | bytes accessed | tf_op | source)
XLA Modules:
  0.0 213.8 jit_solution(6397778874847277601)
XLA Ops:
  8.6 3.8 %collective-permute-start.1 = (bf16[128,256]{1,0:T(8,128)(2,1)}, bf16[128,256]{1,0:T(8,128)(2,1)S(1)}, u32[]{:S(2)}, u32[]{:S(2)}) collective-permute-start(bf16[128,256]{1,0:T(8,128)(2,1)} %f0_ref.1), channel_id=1, source_target_pairs={{0,2},{1,3},{2,0},{3,1},{4,6},{5,7},{6,4},{7,5},{8,10},{9,11},{10,... | collective-permute-start | bytes 196616 | tf_op jit(solution)/shard_map/ppermute | solution.py:401
  12.9 2.3 %collective-permute-start.2 = (bf16[128,256]{1,0:T(8,128)(2,1)}, bf16[128,256]{1,0:T(8,128)(2,1)S(1)}, u32[]{:S(2)}, u32[]{:S(2)}) collective-permute-start(bf16[128,256]{1,0:T(8,128)(2,1)} %f0_ref.1), channel_id=1, source_target_pairs={{0,3},{1,0},{2,1},{3,2},{4,7},{5,4},{6,5},{7,6},{8,11},{9,8},{10,9... | collective-permute-start | bytes 196616 | tf_op jit(solution)/shard_map/ppermute | solution.py:401
  18.2 4.2 %shard_map.195 = (bf16[128,1024]{1,0:T(8,128)(2,1)}, bf16[128,128]{1,0:T(8,128)(2,1)}, bf16[128,128]{1,0:T(8,128)(2,1)}, bf16[128,128]{1,0:T(8,128)(2,1)}, bf16[...) custom-call(s32[1,2]{1,0:T(1,128)} %add_bitcast_fusion.at_ref, bf16[128,256]{1,0:T(8,128)(2,1)} %f0_ref.1, ...), custom_call_target="tpu_custom_call" | custom-call | bytes 1 | tf_op jit(solution)/shard_map/pallas_call | solution.py:41
  22.4 9.7 %all-to-all-start = ((bf16[32,144,128]{2,1,0:T(8,128)(2,1)}), bf16[32,144,128]{2,1,0:T(8,128)(2,1)S(1)}, u32[]{:S(2)}, u32[]{:S(2)}) async-start(bf16[32,144,128]{2,1,0:T(8,128)(2,1)} %get-tuple-element.39), calls=%async_computation | async-start | bytes 2359296 | tf_op jit(solution)/shard_map/all_to_all | solution.py:459
  32.2 3.1 %collective-permute-start.7 = (bf16[1,1024,512]{2,1,0:T(8,128)(2,1)S(1)}, bf16[1,1024,512]{2,1,0:T(8,128)(2,1)S(1)}, u32[]{:S(2)}, u32[]{:S(2)}) collective-permute-start(bf16[1,1024,512]{2,1,0:T(8,128)(2,1)S(1)} %copy-done.19), channel_id=1, source_target_pairs={{0,3},{1,0},{2,1},{3,2},{4,7},{5,4},{6,5},{7,6},{8,11},{9,8},{10,9... | collective-permute-start | bytes 3145736 | tf_op jit(solution)/shard_map/ppermute | solution.py:401
  38.7 5.4 %collective-permute-done.4.q2_ref = bf16[128,128]{1,0:T(8,128)(2,1)S(1)} collective-permute-done((bf16[128,128]{1,0:T(8,128)(2,1)S(1)}, bf16[128,128]{1,0:T(8,128)(2,1)S(1)}, u32[]{:S(2)}, u32[]{:S(2)}) %collective-permute-start.4) | collective-permute-done | bytes 32800 | tf_op jit(solution)/shard_map/ppermute | solution.py:457
  44.1 4.5 %collective-permute-done.5.q3_ref = bf16[128,128]{1,0:T(8,128)(2,1)S(1)} collective-permute-done((bf16[128,128]{1,0:T(8,128)(2,1)S(1)}, bf16[128,128]{1,0:T(8,128)(2,1)S(1)}, u32[]{:S(2)}, u32[]{:S(2)}) %collective-permute-start.5) | collective-permute-done | bytes 32800 | tf_op jit(solution)/shard_map/ppermute | solution.py:457
  48.6 1.9 all-to-all-done.kv_ref
  50.5 4.6 %shard_map.196 = (bf16[16,64,128]{2,1,0:T(8,128)(2,1)}, bf16[512,128]{1,0:T(8,128)(2,1)S(1)}) custom-call(f32[1,1]{1,0:T(1,128)} %bitcast.3.scale_ref, s32[1,2]{1,0:T(1,128)S(1)} %copy-done.14, bf16[128,128]{1,0:T(8,128)(2,1)S(1)} %copy-done.13, bf16[128,128]{1,0:T(8,128)(2,1)S(1)} %collective-permute-done.3.q1_ref, ...), custom_call_target="tpu_custom_call" | custom-call | bytes 1 | tf_op jit(solution)/shard_map/pallas_call | solution.py:41
  55.7 4.8 %all-to-all-start.1 = ((bf16[16,64,128]{2,1,0:T(8,128)(2,1)}), bf16[16,64,128]{2,1,0:T(8,128)(2,1)S(1)}, u32[]{:S(2)}, u32[]{:S(2)}) async-start(bf16[16,64,128]{2,1,0:T(8,128)(2,1)} %get-tuple-element.41), calls=%async_computation.1 | async-start | bytes 524288 | tf_op jit(solution)/shard_map/all_to_all | solution.py:471
  60.5 5.6 %collective-permute-done.6.rest_0_.d1_ref = bf16[1,1024,512]{2,1,0:T(8,128)(2,1)} collective-permute-done((bf16[1,1024,512]{2,1,0:T(8,128)(2,1)S(1)}, bf16[1,1024,512]{2,1,0:T(8,128)(2,1)}, u32[]{:S(2)}, u32[]{:S(2)}) %collective-permute-start.6) | collective-permute-done | bytes 1048608 | tf_op jit(solution)/shard_map/ppermute | solution.py:401
  66.1 5.0 %all-to-all-done.1.att_ref = bf16[16,64,128]{2,1,0:T(8,128)(2,1)S(1)} async-done(((bf16[16,64,128]{2,1,0:T(8,128)(2,1)}), bf16[16,64,128]{2,1,0:T(8,128)(2,1)S(1)}, u32[]{:S(2)}, u32[]{:S(2)}) %all-to-all-start.1) | async-done | bytes 262176 | tf_op jit(solution)/shard_map/all_to_all | solution.py:471
  71.8 5.2 %shard_map.197 = (f32[128,256]{1,0:T(8,128)}, bf16[128,256]{1,0:T(8,128)(2,1)}, bf16[128,256]{1,0:T(8,128)(2,1)}, bf16[128,256]{1,0:T(8,128)(2,1)}, bf16[128,256]{1,0:T(8,128)(2,1)}) custom-call(s32[1,2]{1,0:T(1,128)} %add_bitcast_fusion.at_ref, bf16[16,64,128]{2,1,0:T(8,128)(2,1)} %copy-done.21, bf16[128,1024]{1,0:T(8,128)(2,1)} %get-tuple-element.42.x_ref, ...), custom_call_target="tpu_custom_call" | custom-call | flops 1 | bytes 1 | tf_op jit(solution)/shard_map/pallas_call | solution.py:183
  80.0 3.9 %collective-permute-done.8.p1_ref = bf16[128,256]{1,0:T(8,128)(2,1)S(1)} collective-permute-done((bf16[128,256]{1,0:T(8,128)(2,1)}, bf16[128,256]{1,0:T(8,128)(2,1)S(1)}, u32[]{:S(2)}, u32[]{:S(2)}) %collective-permute-start.8) | collective-permute-done | bytes 65568 | tf_op jit(solution)/shard_map/ppermute | solution.py:401
  83.9 2.1 collective-permute-done.9.p2_ref
  93.8 2.4 %collective-permute-done.12.c2_ref = bf16[128,256]{1,0:T(8,128)(2,1)S(1)} collective-permute-done((bf16[128,256]{1,0:T(8,128)(2,1)S(1)}, bf16[128,256]{1,0:T(8,128)(2,1)S(1)}, u32[]{:S(2)}, u32[]{:S(2)}) %collective-permute-start.12) | collective-permute-done | bytes 65568 | tf_op jit(solution)/shard_map/ppermute | solution.py:401
  98.3 3.0 %shard_map.199 = (bf16[128,1024]{1,0:T(8,128)(2,1)}, bf16[512,1024]{1,0:T(8,128)(2,1)}) custom-call(s32[1,2]{1,0:T(1,128)} %add_bitcast_fusion.at_ref, bf16[512,128]{1,0:T(8,128)(2,1)} %copy-done.10, bf16[128,256]{1,0:T(8,128)(2,1)} %copy-done.8, bf16[128,256]{1,0:T(8,128)(2,1)} %copy-done.27, bf16[128,256]{1,0:T(8,128)(2,1)} %copy-done.26, ...), custom_call_target="tpu_custom_call" | custom-call | bytes 1 | tf_op jit(solution)/shard_map/pallas_call | solution.py:41
  101.3 9.6 %all-to-all-start.2 = ((bf16[32,16,1024]{2,1,0:T(8,128)(2,1)}), bf16[32,16,1024]{2,1,0:T(8,128)(2,1)}, u32[]{:S(2)}, u32[]{:S(2)}) async-start(bf16[32,16,1024]{2,1,0:T(8,128)(2,1)} %bitcast.28), calls=%async_computation.2 | async-start | bytes 2097152 | tf_op jit(solution)/shard_map/all_to_all | solution.py:495
  110.9 7.0 %all-gather.5.cloned.1.call-done.gate_ref = bf16[4,1024,512]{2,1,0:T(8,128)(2,1)} async-done(((bf16[1,1024,512]{2,1,0:T(8,128)(2,1)}), bf16[4,1024,512]{2,1,0:T(8,128)(2,1)}) %all-gather.5.cloned.1.call-update) | async-done | bytes 4194320 | tf_op jit(solution)/shard_map/all_gather | solution.py:430
  117.9 7.3 %shard_map.200 = (bf16[4,1024,512]{2,1,0:T(8,128)(2,1)}, bf16[1024,512]{1,0:T(8,128)(2,1)}, bf16[3,1024,512]{2,1,0:T(8,128)(2,1)}, f32[8,128]{1,0:T(8,128)S(1)}) custom-call(s32[1,2]{1,0:T(1,128)S(1)} %copy-done.15, bf16[4,1024,512]{2,1,0:T(8,128)(2,1)} %all-gather.5.cloned.1.call-done.gate_ref, bf16[1,1024,512]{2,1,0:T(8,128)(2,1)} %u0_ref.1, ...), custom_call_target="tpu_custom_call" | custom-call | flops 1 | bytes 1 | tf_op jit(solution)/shard_map/pallas_call | solution.py:274
  125.2 5.0 %collective-permute-done.14.rest_0_.u1_ref = bf16[1,1024,512]{2,1,0:T(8,128)(2,1)S(1)} collective-permute-done((bf16[1,1024,512]{2,1,0:T(8,128)(2,1)S(1)}, bf16[1,1024,512]{2,1,0:T(8,128)(2,1)S(1)}, u32[]{:S(2)}, u32[]{:S(2)}) %collective-permute-start.14) | collective-permute-done | bytes 1048608 | tf_op jit(solution)/shard_map/ppermute | solution.py:401
  131.6 4.0 %shard_map.201 = (f32[160,1024]{1,0:T(8,128)}, bf16[512,1024]{1,0:T(8,128)(2,1)}) custom-call(bf16[512,1024]{1,0:T(8,128)(2,1)} %bitcast.10.rows_ref, s32[160,1]{1,0:T(8,128)} %get-tuple-element.50.pidx_ref, bf16[160,1024]{1,0:T(8,128)(2,1)} %fine_ref.1, s32[1,160]{1,0:T(1,128)} %bitcast.38, bf16[8,1024]{1,0:T(8,128)(2,1)} %table_ref.1, f32[1,1024]{1,0:T(1,128)} %bitcast.36, ...), custom_call_target="tpu_custom_call" | custom-call | bytes 1 | tf_op jit(solution)/shard_map/pallas_call | solution.py:41
  135.6 8.0 %all-to-all-start.3 = ((bf16[32,16,1024]{2,1,0:T(8,128)(2,1)}), bf16[32,16,1024]{2,1,0:T(8,128)(2,1)S(1)}, u32[]{:S(2)}, u32[]{:S(2)}) async-start(bf16[32,16,1024]{2,1,0:T(8,128)(2,1)} %bitcast.29), calls=%async_computation.3 | async-start | bytes 2097152 | tf_op jit(solution)/shard_map/all_to_all | solution.py:515
  143.8 2.7 %collective-permute-start.21 = (bf16[1,1024,512]{2,1,0:T(8,128)(2,1)}, bf16[1,1024,512]{2,1,0:T(8,128)(2,1)}, u32[]{:S(2)}, u32[]{:S(2)}) collective-permute-start(bf16[1,1024,512]{2,1,0:T(8,128)(2,1)} %copy-done.18), channel_id=1, source_target_pairs={{0,3},{1,0},{2,1},{3,2},{4,7},{5,4},{6,5},{7,6},{8,11},{9,8},{10,9... | collective-permute-start | bytes 3145736 | tf_op jit(solution)/shard_map/ppermute | solution.py:401
  146.4 14.2 %all-to-all-done.3 = bf16[32,16,1024]{2,1,0:T(8,128)(2,1)S(1)} async-done(((bf16[32,16,1024]{2,1,0:T(8,128)(2,1)}), bf16[32,16,1024]{2,1,0:T(8,128)(2,1)S(1)}, u32[]{:S(2)}, u32[]{:S(2)}) %all-to-all-start.3) | async-done | bytes 1048608 | tf_op jit(solution)/shard_map/all_to_all | solution.py:515
  162.4 2.2 %copy-done = bf16[4,1024,512]{2,1,0:T(8,128)(2,1)S(1)} copy-done((bf16[4,1024,512]{2,1,0:T(8,128)(2,1)S(1)}, bf16[4,1024,512]{2,1,0:T(8,128)(2,1)}, u32[]{:S(2)}) %copy-start) | copy-done | bytes 4194328
  164.6 1.9 copy-done.1
  166.5 5.7 %shard_map.202 = (f32[512,1024]{1,0:T(8,128)S(1)}, bf16[2,1024,512]{2,1,0:T(8,128)(2,1)S(1)}) custom-call(bf16[512,1024]{1,0:T(8,128)(2,1)S(1)} %bitcast.23, bf16[4,1024,512]{2,1,0:T(8,128)(2,1)S(1)} %copy-done, bf16[1024,512]{1,0:T(8,128)(2,1)S(1)} %copy-done.6, bf16[3,1024,512]{2,1,0:T(8,128)(2,1)S(1)} %copy-done.1, bf16[1,1024,512]{2,1,0:T(8,128)(2,1)S(1)} %copy-done.3, ...), custom_call_target="tpu_custom_call" | custom-call | flops 1 | bytes 1 | tf_op jit(solution)/shard_map/pallas_call | solution.py:313
  172.3 5.2 %shard_map.203 = (f32[512,1024]{1,0:T(8,128)S(1)}, bf16[512,1024]{1,0:T(8,128)(2,1)S(1)}) custom-call(bf16[128,1024]{1,0:T(8,128)(2,1)S(1)} %collective-permute-done.16.x0_ref, bf16[128,1024]{1,0:T(8,128)(2,1)S(1)} %collective-permute-done.17.x1_ref, bf16[128,1024]{1,0:T(8,128)(2,1)S(1)} %collective-permute-done.18.x2_ref, ...), custom_call_target="tpu_custom_call" | custom-call | flops 1 | bytes 1 | tf_op jit(solution)/shard_map/pallas_call | solution.py:335
  177.5 2.7 %shard_map.204 = (bf16[512,1024]{1,0:T(8,128)(2,1)S(1)}, bf16[1024,512]{1,0:T(8,128)(2,1)S(1)}, bf16[1024,512]{1,0:T(8,128)(2,1)S(1)}) custom-call(bf16[512,1024]{1,0:T(8,128)(2,1)S(1)} %get-tuple-element.59.x_ref, f32[512,1024]{1,0:T(8,128)S(1)} %get-tuple-element.60.acc_ref, bf16[4,1024,512]{2,1,0:T(8,128)(2,1)S(1)} %copy-done, ...), custom_call_target="tpu_custom_call" | custom-call | flops 1 | bytes 1 | tf_op jit(solution)/shard_map/pallas_call | solution.py:363
  180.6 2.3 %collective-permute-done.22.extra_ref = bf16[512,1024]{1,0:T(8,128)(2,1)S(1)} collective-permute-done((bf16[512,1024]{1,0:T(8,128)(2,1)S(1)}, bf16[512,1024]{1,0:T(8,128)(2,1)S(1)}, u32[]{:S(2)}, u32[]{:S(2)}) %collective-permute-start.22) | collective-permute-done | bytes 1048608 | tf_op jit(solution)/shard_map/ppermute | solution.py:521
  184.8 20.8 %all_to_all.43 = bf16[32,16,1024]{2,1,0:T(8,128)(2,1)S(1)} all-to-all(bf16[32,16,1024]{2,1,0:T(8,128)(2,1)S(1)} %bitcast.26), channel_id=1, replica_groups=mesh['seq'=32,'exp'=4] {'seq'}, dimensions={0} | all-to-all | bytes 2097152 | tf_op jit(solution)/shard_map/all_to_all | solution.py:523
  (109 shorter events, 28.9 us)
Async XLA Ops:
  7.2 63.9 %all-gather.3.cloned.1.call-start = ((), (), s32[]{:S(2)}) async-start(), calls=%async_computation.5 | async-start | bytes 2621440 | tf_op jit(solution)/shard_map/all_gather | solution.py:429
  7.9 110.0 %all-gather.5.cloned.1.call-start = ((), (), s32[]{:S(2)}) async-start(), calls=%async_computation.6 | async-start | bytes 5242880 | tf_op jit(solution)/shard_map/all_gather | solution.py:430
  8.6 8.9 %collective-permute-start.1 = (bf16[128,256]{1,0:T(8,128)(2,1)}, bf16[128,256]{1,0:T(8,128)(2,1)S(1)}, u32[]{:S(2)}, u32[]{:S(2)}) collective-permute-start(bf16[128,256]{1,0:T(8,128)(2,1)} %f0_ref.1), channel_id=1, source_target_pairs={{0,2},{1,3},{2,0},{3,1},{4,6},{5,7},{6,4},{7,5},{8,10},{9,11},{10,... | collective-permute-start | bytes 196616 | tf_op jit(solution)/shard_map/ppermute | solution.py:401
  12.5 5.1 %collective-permute-start = (bf16[128,256]{1,0:T(8,128)(2,1)}, bf16[128,256]{1,0:T(8,128)(2,1)S(1)}, u32[]{:S(2)}, u32[]{:S(2)}) collective-permute-start(bf16[128,256]{1,0:T(8,128)(2,1)} %f0_ref.1), channel_id=1, source_target_pairs={{0,1},{1,2},{2,3},{3,0},{4,5},{5,6},{6,7},{7,4},{8,9},{9,10},{10,1... | collective-permute-start | bytes 196616 | tf_op jit(solution)/shard_map/ppermute | solution.py:401
  12.9 4.7 %collective-permute-start.2 = (bf16[128,256]{1,0:T(8,128)(2,1)}, bf16[128,256]{1,0:T(8,128)(2,1)S(1)}, u32[]{:S(2)}, u32[]{:S(2)}) collective-permute-start(bf16[128,256]{1,0:T(8,128)(2,1)} %f0_ref.1), channel_id=1, source_target_pairs={{0,3},{1,0},{2,1},{3,2},{4,7},{5,4},{6,5},{7,6},{8,11},{9,8},{10,9... | collective-permute-start | bytes 196616 | tf_op jit(solution)/shard_map/ppermute | solution.py:401
  18.2 32.3 %copy-start.14 = (s32[1,2]{1,0:T(1,128)S(1)}, s32[1,2]{1,0:T(1,128)}, u32[]{:S(2)}) copy-start(s32[1,2]{1,0:T(1,128)} %add_bitcast_fusion.at_ref) | copy-start | bytes 28
  22.4 28.1 %copy-start.13 = (bf16[128,128]{1,0:T(8,128)(2,1)S(1)}, bf16[128,128]{1,0:T(8,128)(2,1)}, u32[]{:S(2)}) copy-start(bf16[128,128]{1,0:T(8,128)(2,1)} %get-tuple-element.35.q0_ref) | copy-start | bytes 98308
  22.4 28.1 %all-to-all-start = ((bf16[32,144,128]{2,1,0:T(8,128)(2,1)}), bf16[32,144,128]{2,1,0:T(8,128)(2,1)S(1)}, u32[]{:S(2)}, u32[]{:S(2)}) async-start(bf16[32,144,128]{2,1,0:T(8,128)(2,1)} %get-tuple-element.39), calls=%async_computation | async-start | bytes 2359296 | tf_op jit(solution)/shard_map/all_to_all | solution.py:459
  32.1 34.0 %collective-permute-start.6 = (bf16[1,1024,512]{2,1,0:T(8,128)(2,1)S(1)}, bf16[1,1024,512]{2,1,0:T(8,128)(2,1)}, u32[]{:S(2)}, u32[]{:S(2)}) collective-permute-start(bf16[1,1024,512]{2,1,0:T(8,128)(2,1)S(1)} %copy-done.19), channel_id=1, source_target_pairs={{0,1},{1,2},{2,3},{3,0},{4,5},{5,6},{6,7},{7,4},{8,9},{9,10},{10,1... | collective-permute-start | bytes 3145736 | tf_op jit(solution)/shard_map/ppermute | solution.py:401
  32.2 33.9 %collective-permute-start.7 = (bf16[1,1024,512]{2,1,0:T(8,128)(2,1)S(1)}, bf16[1,1024,512]{2,1,0:T(8,128)(2,1)S(1)}, u32[]{:S(2)}, u32[]{:S(2)}) collective-permute-start(bf16[1,1024,512]{2,1,0:T(8,128)(2,1)S(1)} %copy-done.19), channel_id=1, source_target_pairs={{0,3},{1,0},{2,1},{3,2},{4,7},{5,4},{6,5},{7,6},{8,11},{9,8},{10,9... | collective-permute-start | bytes 3145736 | tf_op jit(solution)/shard_map/ppermute | solution.py:401
  35.3 3.5 %collective-permute-start.3 = (bf16[128,128]{1,0:T(8,128)(2,1)S(1)}, bf16[128,128]{1,0:T(8,128)(2,1)S(1)}, u32[]{:S(2)}, u32[]{:S(2)}) collective-permute-start(bf16[128,128]{1,0:T(8,128)(2,1)S(1)} %copy-done.30), channel_id=1, source_target_pairs={{0,4},{4,0},{8,12},{12,8},{16,20},{20,16},{24,28},{28,24},{32,36},... | collective-permute-start | bytes 98312 | tf_op jit(solution)/shard_map/ppermute | solution.py:457
  35.8 8.3 %collective-permute-start.4 = (bf16[128,128]{1,0:T(8,128)(2,1)S(1)}, bf16[128,128]{1,0:T(8,128)(2,1)S(1)}, u32[]{:S(2)}, u32[]{:S(2)}) collective-permute-start(bf16[128,128]{1,0:T(8,128)(2,1)S(1)} %copy-done.29), channel_id=1, source_target_pairs={{0,8},{4,12},{8,0},{12,4},{16,24},{20,28},{24,16},{28,20},{32,40},... | collective-permute-start | bytes 98312 | tf_op jit(solution)/shard_map/ppermute | solution.py:457
  37.3 11.3 %collective-permute-start.5 = (bf16[128,128]{1,0:T(8,128)(2,1)S(1)}, bf16[128,128]{1,0:T(8,128)(2,1)S(1)}, u32[]{:S(2)}, u32[]{:S(2)}) collective-permute-start(bf16[128,128]{1,0:T(8,128)(2,1)S(1)} %copy-done.28), channel_id=1, source_target_pairs={{0,12},{4,8},{8,4},{12,0},{16,28},{20,24},{24,20},{28,16},{32,44},... | collective-permute-start | bytes 98312 | tf_op jit(solution)/shard_map/ppermute | solution.py:457
  55.7 15.4 %all-to-all-start.1 = ((bf16[16,64,128]{2,1,0:T(8,128)(2,1)}), bf16[16,64,128]{2,1,0:T(8,128)(2,1)S(1)}, u32[]{:S(2)}, u32[]{:S(2)}) async-start(bf16[16,64,128]{2,1,0:T(8,128)(2,1)} %get-tuple-element.41), calls=%async_computation.1 | async-start | bytes 524288 | tf_op jit(solution)/shard_map/all_to_all | solution.py:471
  77.0 40.8 %copy-start.15 = (s32[1,2]{1,0:T(1,128)S(1)}, s32[1,2]{1,0:T(1,128)}, u32[]{:S(2)}) copy-start(s32[1,2]{1,0:T(1,128)} %add_bitcast_fusion.at_ref) | copy-start | bytes 28
  77.1 6.9 %collective-permute-start.8 = (bf16[128,256]{1,0:T(8,128)(2,1)}, bf16[128,256]{1,0:T(8,128)(2,1)S(1)}, u32[]{:S(2)}, u32[]{:S(2)}) collective-permute-start(bf16[128,256]{1,0:T(8,128)(2,1)} %get-tuple-element.44), channel_id=1, source_target_pairs={{0,1},{1,2},{2,3},{3,0},{4,5},{5,6},{6,7},{7,4},{8,9},{9,10},{10,1... | collective-permute-start | bytes 196616 | tf_op jit(solution)/shard_map/ppermute | solution.py:401
  77.5 8.5 %collective-permute-start.9 = (bf16[128,256]{1,0:T(8,128)(2,1)}, bf16[128,256]{1,0:T(8,128)(2,1)S(1)}, u32[]{:S(2)}, u32[]{:S(2)}) collective-permute-start(bf16[128,256]{1,0:T(8,128)(2,1)} %get-tuple-element.45), channel_id=1, source_target_pairs={{0,2},{1,3},{2,0},{3,1},{4,6},{5,7},{6,4},{7,5},{8,10},{9,11},{10,... | collective-permute-start | bytes 196616 | tf_op jit(solution)/shard_map/ppermute | solution.py:401
  79.2 7.8 %collective-permute-start.10 = (bf16[128,256]{1,0:T(8,128)(2,1)}, bf16[128,256]{1,0:T(8,128)(2,1)S(1)}, u32[]{:S(2)}, u32[]{:S(2)}) collective-permute-start(bf16[128,256]{1,0:T(8,128)(2,1)} %get-tuple-element.46), channel_id=1, source_target_pairs={{0,3},{1,0},{2,1},{3,2},{4,7},{5,4},{6,5},{7,6},{8,11},{9,8},{10,9... | collective-permute-start | bytes 196616 | tf_op jit(solution)/shard_map/ppermute | solution.py:401
  88.9 5.0 %collective-permute-start.13 = (bf16[128,256]{1,0:T(8,128)(2,1)S(1)}, bf16[128,256]{1,0:T(8,128)(2,1)S(1)}, u32[]{:S(2)}, u32[]{:S(2)}) collective-permute-start(bf16[128,256]{1,0:T(8,128)(2,1)S(1)} %shard_map.198.c0_ref), channel_id=1, source_target_pairs={{0,3},{1,0},{2,1},{3,2},{4,7},{5,4},{6,5},{7,6},{8,11},{9,8},{10,9... | collective-permute-start | bytes 196616 | tf_op jit(solution)/shard_map/ppermute | solution.py:401
  89.9 6.3 %collective-permute-start.12 = (bf16[128,256]{1,0:T(8,128)(2,1)S(1)}, bf16[128,256]{1,0:T(8,128)(2,1)S(1)}, u32[]{:S(2)}, u32[]{:S(2)}) collective-permute-start(bf16[128,256]{1,0:T(8,128)(2,1)S(1)} %shard_map.198.c0_ref), channel_id=1, source_target_pairs={{0,2},{1,3},{2,0},{3,1},{4,6},{5,7},{6,4},{7,5},{8,10},{9,11},{10,... | collective-permute-start | bytes 196616 | tf_op jit(solution)/shard_map/ppermute | solution.py:401
  90.4 7.3 %collective-permute-start.11 = (bf16[128,256]{1,0:T(8,128)(2,1)S(1)}, bf16[128,256]{1,0:T(8,128)(2,1)S(1)}, u32[]{:S(2)}, u32[]{:S(2)}) collective-permute-start(bf16[128,256]{1,0:T(8,128)(2,1)S(1)} %shard_map.198.c0_ref), channel_id=1, source_target_pairs={{0,1},{1,2},{2,3},{3,0},{4,5},{5,6},{6,7},{7,4},{8,9},{9,10},{10,1... | collective-permute-start | bytes 196616 | tf_op jit(solution)/shard_map/ppermute | solution.py:401
  90.8 39.4 %collective-permute-start.14 = (bf16[1,1024,512]{2,1,0:T(8,128)(2,1)S(1)}, bf16[1,1024,512]{2,1,0:T(8,128)(2,1)S(1)}, u32[]{:S(2)}, u32[]{:S(2)}) collective-permute-start(bf16[1,1024,512]{2,1,0:T(8,128)(2,1)S(1)} %copy-done.20), channel_id=1, source_target_pairs={{0,1},{1,2},{2,3},{3,0},{4,5},{5,6},{6,7},{7,4},{8,9},{9,10},{10,1... | collective-permute-start | bytes 3145736 | tf_op jit(solution)/shard_map/ppermute | solution.py:401
  92.5 37.7 %collective-permute-start.15 = (bf16[1,1024,512]{2,1,0:T(8,128)(2,1)S(1)}, bf16[1,1024,512]{2,1,0:T(8,128)(2,1)S(1)}, u32[]{:S(2)}, u32[]{:S(2)}) collective-permute-start(bf16[1,1024,512]{2,1,0:T(8,128)(2,1)S(1)} %copy-done.20), channel_id=1, source_target_pairs={{0,3},{1,0},{2,1},{3,2},{4,7},{5,4},{6,5},{7,6},{8,11},{9,8},{10,9... | collective-permute-start | bytes 3145736 | tf_op jit(solution)/shard_map/ppermute | solution.py:401
  101.3 28.9 %all-to-all-start.2 = ((bf16[32,16,1024]{2,1,0:T(8,128)(2,1)}), bf16[32,16,1024]{2,1,0:T(8,128)(2,1)}, u32[]{:S(2)}, u32[]{:S(2)}) async-start(bf16[32,16,1024]{2,1,0:T(8,128)(2,1)} %bitcast.28), calls=%async_computation.2 | async-start | bytes 2097152 | tf_op jit(solution)/shard_map/all_to_all | solution.py:495
  135.6 25.0 %all-to-all-start.3 = ((bf16[32,16,1024]{2,1,0:T(8,128)(2,1)}), bf16[32,16,1024]{2,1,0:T(8,128)(2,1)S(1)}, u32[]{:S(2)}, u32[]{:S(2)}) async-start(bf16[32,16,1024]{2,1,0:T(8,128)(2,1)} %bitcast.29), calls=%async_computation.3 | async-start | bytes 2097152 | tf_op jit(solution)/shard_map/all_to_all | solution.py:515
  143.7 33.8 %collective-permute-start.20 = (bf16[1,1024,512]{2,1,0:T(8,128)(2,1)S(1)}, bf16[1,1024,512]{2,1,0:T(8,128)(2,1)}, u32[]{:S(2)}, u32[]{:S(2)}) collective-permute-start(bf16[1,1024,512]{2,1,0:T(8,128)(2,1)S(1)} %copy-done.3), channel_id=1, source_target_pairs={{0,1},{1,2},{2,3},{3,0},{4,5},{5,6},{6,7},{7,4},{8,9},{9,10},{10,1... | collective-permute-start | bytes 3145736 | tf_op jit(solution)/shard_map/ppermute | solution.py:401
  143.8 33.7 %collective-permute-start.21 = (bf16[1,1024,512]{2,1,0:T(8,128)(2,1)}, bf16[1,1024,512]{2,1,0:T(8,128)(2,1)}, u32[]{:S(2)}, u32[]{:S(2)}) collective-permute-start(bf16[1,1024,512]{2,1,0:T(8,128)(2,1)} %copy-done.18), channel_id=1, source_target_pairs={{0,3},{1,0},{2,1},{3,2},{4,7},{5,4},{6,5},{7,6},{8,11},{9,8},{10,9... | collective-permute-start | bytes 3145736 | tf_op jit(solution)/shard_map/ppermute | solution.py:401
  160.7 1.6 collective-permute-start.18
  160.9 11.4 %collective-permute-start.19 = (bf16[128,1024]{1,0:T(8,128)(2,1)S(1)}, bf16[128,1024]{1,0:T(8,128)(2,1)S(1)}, u32[]{:S(2)}, u32[]{:S(2)}) collective-permute-start(bf16[128,1024]{1,0:T(8,128)(2,1)S(1)} %bitcast.32), channel_id=1, source_target_pairs={{0,4},{4,0},{8,12},{12,8},{16,20},{20,16},{24,28},{28,24},{32,36},... | collective-permute-start | bytes 786440 | tf_op jit(solution)/shard_map/ppermute | solution.py:517
  161.3 11.0 %collective-permute-start.17 = (bf16[128,1024]{1,0:T(8,128)(2,1)S(1)}, bf16[128,1024]{1,0:T(8,128)(2,1)S(1)}, u32[]{:S(2)}, u32[]{:S(2)}) collective-permute-start(bf16[128,1024]{1,0:T(8,128)(2,1)S(1)} %bitcast.31), channel_id=1, source_target_pairs={{0,4},{4,0},{8,12},{12,8},{16,20},{20,16},{24,28},{28,24},{32,36},... | collective-permute-start | bytes 786440 | tf_op jit(solution)/shard_map/ppermute | solution.py:517
  162.3 10.0 %collective-permute-start.16 = (bf16[128,1024]{1,0:T(8,128)(2,1)S(1)}, bf16[128,1024]{1,0:T(8,128)(2,1)S(1)}, u32[]{:S(2)}, u32[]{:S(2)}) collective-permute-start(bf16[128,1024]{1,0:T(8,128)(2,1)S(1)} %bitcast.30), channel_id=1, source_target_pairs={{0,4},{4,0},{8,12},{12,8},{16,20},{20,16},{24,28},{28,24},{32,36},... | collective-permute-start | bytes 786440 | tf_op jit(solution)/shard_map/ppermute | solution.py:517
  180.2 2.7 %collective-permute-start.22 = (bf16[512,1024]{1,0:T(8,128)(2,1)S(1)}, bf16[512,1024]{1,0:T(8,128)(2,1)S(1)}, u32[]{:S(2)}, u32[]{:S(2)}) collective-permute-start(bf16[512,1024]{1,0:T(8,128)(2,1)S(1)} %get-tuple-element.61), channel_id=1, source_target_pairs={{0,4},{4,0},{8,12},{12,8},{16,20},{20,16},{24,28},{28,24},{32,36},... | collective-permute-start | bytes 3145736 | tf_op jit(solution)/shard_map/ppermute | solution.py:521
  (29 other events, 228.9 us)
Sparse Core Ops, SparseCore 0:
  9.7 40.9 all-gather.2
  52.3 65.5 all-gather.4

commit v5 on v4

--- a/solution.py
+++ b/solution.py
@@ -101,8 +101,8 @@
     return lax.rem(y - k + N_EXP, N_EXP)
 
 
-def qkv_kernel(at_ref, f0_ref, f1_ref, f2_ref, f3_ref, gain_ref, w_ref, req_ref, x_ref, q0_ref, q1_ref, q2_ref, q3_ref, kv_ref, xs, qs):
-    y, me = at_ref[0, 0], at_ref[0, 1]
+def qkv_kernel(f0_ref, f1_ref, f2_ref, f3_ref, gain_ref, w_ref, req_ref, x_ref, q0_ref, q1_ref, q2_ref, q3_ref, kv_ref, xs, qs):
+    y, me = lax.axis_index("exp"), lax.rem(lax.axis_index("seq"), HEADS)
     for k, f_ref in enumerate((f0_ref, f1_ref, f2_ref, f3_ref)):
         xs[around(y, k)] = f_ref[...]
     whole = jnp.concatenate([xs[c] for c in range(N_EXP)], axis=1)
@@ -123,12 +123,12 @@
         q_ref[...] = qs[me ^ k]
 
 
-def attn_kernel(scale_ref, at_ref, q0_ref, q1_ref, q2_ref, q3_ref, kv_ref, out_ref, req_ref):
+def attn_kernel(scale_ref, q0_ref, q1_ref, q2_ref, q3_ref, kv_ref, out_ref, req_ref):
     req_ref[...] = kv_ref[:, ROWS : ROWS + PSLOTS, :].reshape(N_SEQ * PSLOTS, ROWS)
     kv = kv_ref[:, 0:ROWS, :].reshape(N_SEQ * ROWS, 2 * HD)
     vones = jnp.where(iota(kv.shape, 1) < HD, jnp.ones_like(kv), kv)
-    c = scale_ref[0, 0]
-    me = at_ref[0, 1]
+    me = lax.rem(lax.axis_index("seq"), HEADS)
+    c = scale_ref[me] * (math.log2(math.e) / math.sqrt(HD))
     for b, q_ref in enumerate((q0_ref, q1_ref, q2_ref, q3_ref)):
         s = dot_nt(q_ref[...], kv)
         top = jnp.max(s, axis=-1, keepdims=True)
@@ -141,7 +141,7 @@
             out_ref[(me ^ b) * N_EXP + z] = packed
 
 
-def block_kernel(at_ref, att_ref, x_ref, gain_ref, wo_ref, win_ref, wout_ref, *rest):
+def block_kernel(att_ref, x_ref, gain_ref, wo_ref, win_ref, wout_ref, *rest):
     mixed_ref, p0_ref, p1_ref, p2_ref, p3_ref, scr, pieces, wbuf, sem = rest[-9:]
     copies = [
         pltpu.make_async_copy(src, dst, sem.at[i])
@@ -165,7 +165,8 @@
     mixed = x_ref[...].astype(F32) + dot(att, wbuf[0])
     for c in range(N_EXP):
         scr[c] = mixed[:, c * 256 : (c + 1) * 256]
-    mixed_ref[...] = scr[at_ref[0, 0]]
+    y = lax.axis_index("exp")
+    mixed_ref[...] = scr[y]
     normed = rms(mixed, gain_ref[...]).astype(BF)
     copies[1].wait()
     inner = jax.nn.gelu(dot(normed, wbuf[1])).astype(BF)
@@ -174,15 +175,15 @@
     for c in range(N_EXP):
         pieces[c] = part[:, c * 256 : (c + 1) * 256]
     for k, p_ref in enumerate((p0_ref, p1_ref, p2_ref, p3_ref)):
-        p_ref[...] = pieces[lax.rem(at_ref[0, 0] + k, N_EXP)]
-
-
-def block(at, att, x, gain, wo, win, wout, *ready):
+        p_ref[...] = pieces[lax.rem(y + k, N_EXP)]
+
+
+def block(att, x, gain, wo, win, wout, *ready):
     vm = pl.BlockSpec(memory_space=pltpu.VMEM)
     hbm = pl.BlockSpec(memory_space=pl.ANY)
     return pl.pallas_call(
         block_kernel,
-        in_specs=[pl.BlockSpec(memory_space=pltpu.SMEM), vm, vm, vm] + [hbm] * (3 + len(ready)),
+        in_specs=[vm, vm, vm] + [hbm] * (3 + len(ready)),
         out_specs=[vm] * 5,
         out_shape=[sds((ROWS, 256), F32)] + [sds((ROWS, 256), BF)] * 4,
         scratch_shapes=[
@@ -193,7 +194,7 @@
         ],
         compiler_params=pltpu.CompilerParams(vmem_limit_bytes=58 << 20),
         cost_estimate=pl.CostEstimate(flops=1, bytes_accessed=1, transcendentals=0),
-    )(at, att, x, gain, wo, win, wout, *ready)
+    )(att, x, gain, wo, win, wout, *ready)
 
 
 def coarse_kernel(p0_ref, p1_ref, p2_ref, p3_ref, mixed_ref, out_ref):
@@ -215,8 +216,8 @@
         c.wait()
 
 
-def serve_kernel(at_ref, req_ref, c0_ref, c1_ref, c2_ref, c3_ref, coarse_ref, out_ref, cs, scr, sem):
-    y = at_ref[0, 0]
+def serve_kernel(req_ref, c0_ref, c1_ref, c2_ref, c3_ref, coarse_ref, out_ref, cs, scr, sem):
+    y = lax.axis_index("exp")
     for k, c_ref in enumerate((c0_ref, c1_ref, c2_ref, c3_ref)):
         cs[around(y, k)] = c_ref[...]
     coarse = jnp.concatenate([cs[c] for c in range(N_EXP)], axis=1)
@@ -246,9 +247,9 @@
     copy_out(out_ref, scr, sem, make)
 
 
-def stage_kernel(at_ref, gate_ref, u0_ref, d0_ref, d1_ref, d2_ref, g_ref, u_ref, d_ref, token_ref, sem):
+def stage_kernel(gate_ref, u0_ref, d0_ref, d1_ref, d2_ref, g_ref, u_ref, d_ref, token_ref, sem):
     token_ref[...] = jnp.zeros_like(token_ref)
-    y = at_ref[0, 0]
+    y = lax.axis_index("exp")
     copies = []
     for j, k in enumerate((0, 1, 3, 2)):
         copies.append((gate_ref.at[around(y, k)], g_ref.at[j]))
@@ -264,16 +265,15 @@
 
 HBM = pl.BlockSpec(memory_space=pltpu.HBM)
 INNER = pl.BlockSpec(memory_space=pltpu.VMEM)
-SCALAR = pl.BlockSpec(memory_space=pltpu.SMEM)
 
 
 COST = pl.CostEstimate(flops=1, bytes_accessed=1, transcendentals=0)
 
 
-def stage(at, gate, up, downs):
+def stage(gate, up, downs):
     return pl.pallas_call(
         stage_kernel,
-        in_specs=[SCALAR] + [HBM] * 5,
+        in_specs=[HBM] * 5,
         out_specs=[INNER] * 4,
         out_shape=[
             sds((4, D, 512), BF),
@@ -284,7 +284,25 @@
         scratch_shapes=[pltpu.SemaphoreType.DMA((8,))],
         compiler_params=pltpu.CompilerParams(vmem_limit_bytes=53 << 20),
         cost_estimate=COST,
-    )(at, gate, up, *downs)
+    )(gate, up, *downs)
+
+
+def relay_kernel(src_ref, ready_ref, out_ref, sem):
+    copy = pltpu.make_async_copy(src_ref, out_ref, sem.at[0])
+    copy.start()
+    copy.wait()
+
+
+def relay(src, ready):
+    return pl.pallas_call(
+        relay_kernel,
+        in_specs=[HBM] * 2,
+        out_specs=INNER,
+        out_shape=sds(src.shape, src.dtype),
+        scratch_shapes=[pltpu.SemaphoreType.DMA((1,))],
+        compiler_params=pltpu.CompilerParams(vmem_limit_bytes=60 << 20),
+        cost_estimate=COST,
+    )(src, ready)
 
 
 def swiglu(x, gate, up, down):
@@ -371,21 +389,24 @@
     )(x, acc, gate, up, down)
 
 
-def final_kernel(x_ref, acc_ref, extra_ref, g_ref, u_ref, d_ref, out_ref):
-    acc = acc_ref[...] + swiglu(x_ref[...], g_ref[3], u_ref[...], d_ref[...])
-    out_ref[...] = (acc + extra_ref[...].astype(F32)).astype(BF)
-
-
-def final(x, acc, extra, gate, up, down):
+def own_kernel(x_ref, acc_ref, g_ref, u_ref, d_ref, out_ref):
+    out_ref[...] = acc_ref[...] + swiglu(x_ref[...], g_ref[3], u_ref[...], d_ref[...])
+
+
+def own(x, acc, gate, up, down):
     n = EXPERTS * SLOTS
     return pl.pallas_call(
-        final_kernel,
-        in_specs=[INNER] * 6,
+        own_kernel,
+        in_specs=[INNER] * 5,
         out_specs=INNER,
-        out_shape=sds((n, D), BF),
+        out_shape=sds((n, D), F32),
         compiler_params=pltpu.CompilerParams(vmem_limit_bytes=30 << 20),
         cost_estimate=COST,
-    )(x, acc, extra, gate, up, down)
+    )(x, acc, gate, up, down)
+
+
+def join_kernel(acc_ref, extra_ref, out_ref):
+    out_ref[...] = (acc_ref[...] + extra_ref[...].astype(F32)).astype(BF)
 
 
 def combine_kernel(ret_ref, didx_ref, gates_ref, sum_ref, out_ref):
@@ -422,9 +443,6 @@
     up_weight,
     down_weight,
 ):
-    s = lax.axis_index("seq")
-    y = lax.axis_index("exp")
-    at = jnp.stack([y, s % 4]).astype(jnp.int32).reshape(1, 2)
     feats = [coarse_in] + [turn(coarse_in, k) for k in (1, 2, 3)]
     wo = lax.all_gather(out_weight, "exp", axis=0, tiled=True)
     gate = lax.all_gather(gate_weight, "exp", axis=0, tiled=True)
@@ -445,35 +463,31 @@
     x, *qs, kv = call(
         qkv_kernel,
         [sds((ROWS, D), BF)] + [head_block] * 4 + [sds((N_SEQ, ROWS + PSLOTS, 2 * HD), BF)],
-        at,
         *feats,
         norm1_gain.reshape(1, D),
         qkv_weight,
         req,
-        smem=(0,),
         scratch_shapes=[pltpu.VMEM((N_EXP, ROWS, 256), BF), pltpu.VMEM((HEADS, ROWS, 2 * HD), BF)],
     )
     qs = [qs[0]] + [
         lax.ppermute(qs[k], "seq", [(i, i ^ k) for i in range(N_SEQ)]) for k in (1, 2, 3)
     ]
     kv = lax.all_to_all(kv, "seq", 0, 0, tiled=True)
-    scale = lax.dynamic_slice(head_scale, (s % 4,), (1,)) * (math.log2(math.e) / math.sqrt(HD))
     att, req = call(
         attn_kernel,
         [sds((16, ROWS // 2, 2 * HD), BF), sds((N_SEQ * PSLOTS, ROWS), BF)],
-        scale.reshape(1, 1),
-        at,
+        head_scale,
         *qs,
         kv,
-        smem=(0, 1),
+        smem=(0,),
         limit=24,
     )
     att = lax.all_to_all(att, ("seq", "exp"), 0, 0, axis_index_groups=SIXTEENS, tiled=True)
     ur, ul = turn(up_weight, 1), turn(up_weight, 3)
     dr, dl = turn(down_weight, 1), turn(down_weight, 3)
-    u2, d2 = turn(ur, 1), turn(dl, 3)
+    u2, d2 = turn(ur, 1), turn(relay(dl, ul), 3)
     mixed, *parts = block(
-        at, att, x, norm2_gain.reshape(1, D), wo, mlp_in, mlp_out, dr, dl
+        att, x, norm2_gain.reshape(1, D), wo, mlp_in, mlp_out, dr, dl
     )
     parts = [parts[0]] + [turn(parts[k], k) for k in (1, 2, 3)]
     piece = call(coarse_kernel, sds((ROWS, 256), BF), *parts, mixed, limit=8)
@@ -481,10 +495,8 @@
     coarse_new, served = call(
         serve_kernel,
         [sds((ROWS, D), BF), sds((N_SEQ * PSLOTS, D), BF)],
-        at,
         req,
         *pieces,
-        smem=(0,),
         far=(1,),
         scratch_shapes=[
             pltpu.VMEM((N_EXP, ROWS, 256), BF),
@@ -493,7 +505,7 @@
         ],
     )
     served = lax.all_to_all(served, "seq", 0, 0, tiled=True)
-    *staged, token = stage(at, gate, up_weight, (down_weight, dr, dl))
+    *staged, token = stage(gate, up_weight, (down_weight, dr, dl))
     fine_sum, outgoing = call(
         fine_kernel,
         [sds((FINE, D), F32), sds((EXPERTS * SLOTS, D), BF)],
@@ -504,7 +516,7 @@
         octant_table,
         norm3_gain.reshape(1, D),
         didxt,
-        ready=(ur, ul, token),
+        ready=(token,),
         limit=60,
         far=(1,),
         scratch_shapes=[
@@ -519,7 +531,8 @@
     acc_other, other = second(others, staged, ups)
     for_other, u3, d3 = last(other, acc_other, staged[0], u2, d2)
     from_other = lax.ppermute(for_other, "seq", SWAP)
-    result = final(mine, acc_mine, from_other, staged[0], u3, d3)
+    acc_mine = own(mine, acc_mine, staged[0], u3, d3)
+    result = call(join_kernel, sds((EXPERTS * SLOTS, D), BF), acc_mine, from_other, limit=24)
     returned = lax.all_to_all(result, "seq", 0, 0, tiled=True)
     fine_out = call(
         combine_kernel, sds((FINE, D), BF), returned, didx, expert_gates.T, fine_sum, limit=12

time: 215 us -> 205 us (0.953)
  waiting for transfers between devices: 64.4 us -> 58.1 us
  starting transfers between devices: 55.6 us -> 51.5 us
    all_gather x1, waiting for transfers between devices: 7 us -> 0.01 us  [per_device(): gate = lax.all_gather(gate_weight, 'exp', axis=0, tiled=True)]
    all_to_all x1, waiting for transfers between devices: 0.01 us -> 6.8 us  [per_device(): served = lax.all_to_all(served, 'seq', 0, 0, tiled=True)]
    all_to_all x1, starting transfers between devices: 8.05 us -> 3.96 us  [per_device(): mine = lax.all_to_all(outgoing, 'seq', 0, 0, tiled=True)]
    all_to_all x1, waiting for transfers between devices: 14.2 us -> 10.7 us  [per_device(): mine = lax.all_to_all(outgoing, 'seq', 0, 0, tiled=True)]
    pallas_call x3 -> x4, Pallas kernels: 14.4 us -> 16 us  [the longest x1 6.76 us: stage(): pl.pallas_call(stage_kernel, in_specs=[HBM] * 5, out_specs=[INNER] * 4, o...]
    unnamed x64 -> x56, local copies, waits for them, and re-layouts: 9.85 us -> 11 us
    pallas_call x7 -> x8, Pallas kernels: 18.9 us -> 19.1 us  [call(): pl.pallas_call(kernel, out_shape=out_shape, in_specs=space + [pl.BlockSpe...]
  transfers between devices with their start and end apart: 29 -> 29, of which waited for: 16 -> 16; matrix products, arithmetic and copies ran while one was open for 1% -> 0% of each run, Pallas kernels for 17% -> 22%
where the time goes in v5:
time: 205 us; the launch traced here: 204 us
  waiting for transfers between devices  58.1 us (28%)
  starting transfers between devices  51.5 us (25%)
  Pallas kernels  48.6 us (24%)
  blocking collectives  20.8 us (10%)
  between operations  14.3 us (7%)
  local copies, waits for them, and re-layouts  11.1 us (5%)
    all_to_all x1, blocking collectives, per_device(): returned = lax.all_to_all(result, 'seq', 0, 0, tiled=True)  20.8 us
    ppermute x15, waiting for transfers between devices, turn(): return lax.ppermute(v, 'exp', [(i, (i + k) % N_EXP) for i in range(N_EXP)])  19.9 us
    ppermute x15, starting transfers between devices, turn(): return lax.ppermute(v, 'exp', [(i, (i + k) % N_EXP) for i in range(N_EXP)])  19.9 us
    pallas_call x8, Pallas kernels, call(): pl.pallas_call(kernel, out_shape=out_shape, in_specs=space + [pl.BlockSpe...  19.1 us
    ppermute x3, waiting for transfers between devices, per_device(): lax.ppermute(qs[k], 'seq', [(i, i ^ k) for i in range(N_SEQ)])  11.1 us
    unnamed x56, local copies, waits for them, and re-layouts  11 us
    all_to_all x1, waiting for transfers between devices, per_device(): mine = lax.all_to_all(outgoing, 'seq', 0, 0, tiled=True)  10.7 us
    all_to_all x1, starting transfers between devices, per_device(): kv = lax.all_to_all(kv, 'seq', 0, 0, tiled=True)  10.2 us
  transfers between devices with their start and end apart: 29, of which 16 were waited for; matrix products, arithmetic and copies ran while one was open for 0% of the time, Pallas kernels for 22%

profile of v5, /device:TPU:1, one launch (start us, length us, event | category | flops | bytes accessed | tf_op | source)
XLA Modules:
  0.0 204.5 jit_solution(10611884654126275100)
XLA Ops:
  8.6 3.8 %collective-permute-start.1 = (bf16[128,256]{1,0:T(8,128)(2,1)}, bf16[128,256]{1,0:T(8,128)(2,1)S(1)}, u32[]{:S(2)}, u32[]{:S(2)}) collective-permute-start(bf16[128,256]{1,0:T(8,128)(2,1)} %f0_ref.1), channel_id=1, source_target_pairs={{0,2},{1,3},{2,0},{3,1},{4,6},{5,7},{6,4},{7,5},{8,10},{9,11},{10,... | collective-permute-start | bytes 196616 | tf_op jit(solution)/shard_map/ppermute | solution.py:422
  12.9 2.3 %collective-permute-start.2 = (bf16[128,256]{1,0:T(8,128)(2,1)}, bf16[128,256]{1,0:T(8,128)(2,1)S(1)}, u32[]{:S(2)}, u32[]{:S(2)}) collective-permute-start(bf16[128,256]{1,0:T(8,128)(2,1)} %f0_ref.1), channel_id=1, source_target_pairs={{0,3},{1,0},{2,1},{3,2},{4,7},{5,4},{6,5},{7,6},{8,11},{9,8},{10,9... | collective-permute-start | bytes 196616 | tf_op jit(solution)/shard_map/ppermute | solution.py:422
  17.7 4.2 %shard_map.195 = (bf16[128,1024]{1,0:T(8,128)(2,1)}, bf16[128,128]{1,0:T(8,128)(2,1)}, bf16[128,128]{1,0:T(8,128)(2,1)}, bf16[128,128]{1,0:T(8,128)(2,1)}, bf16[...) custom-call(bf16[128,256]{1,0:T(8,128)(2,1)} %f0_ref.1, bf16[128,256]{1,0:T(8,128)(2,1)} %copy-done.20, ...), custom_call_target="tpu_custom_call" | custom-call | bytes 1 | tf_op jit(solution)/shard_map/pallas_call | solution.py:41
  21.8 10.2 %all-to-all-start = ((bf16[32,144,128]{2,1,0:T(8,128)(2,1)}), bf16[32,144,128]{2,1,0:T(8,128)(2,1)S(1)}, u32[]{:S(2)}, u32[]{:S(2)}) async-start(bf16[32,144,128]{2,1,0:T(8,128)(2,1)} %get-tuple-element.39), calls=%async_computation | async-start | bytes 2359296 | tf_op jit(solution)/shard_map/all_to_all | solution.py:475
  32.2 3.0 %collective-permute-start.7 = (bf16[1,1024,512]{2,1,0:T(8,128)(2,1)S(1)}, bf16[1,1024,512]{2,1,0:T(8,128)(2,1)S(1)}, u32[]{:S(2)}, u32[]{:S(2)}) collective-permute-start(bf16[1,1024,512]{2,1,0:T(8,128)(2,1)S(1)} %copy-done.18), channel_id=1, source_target_pairs={{0,3},{1,0},{2,1},{3,2},{4,7},{5,4},{6,5},{7,6},{8,11},{9,8},{10,9... | collective-permute-start | bytes 3145736 | tf_op jit(solution)/shard_map/ppermute | solution.py:422
  37.5 6.6 %collective-permute-done.4.q2_ref = bf16[128,128]{1,0:T(8,128)(2,1)S(1)} collective-permute-done((bf16[128,128]{1,0:T(8,128)(2,1)S(1)}, bf16[128,128]{1,0:T(8,128)(2,1)S(1)}, u32[]{:S(2)}, u32[]{:S(2)}) %collective-permute-start.4) | collective-permute-done | bytes 32800 | tf_op jit(solution)/shard_map/ppermute | solution.py:473
  44.1 4.5 %collective-permute-done.5.q3_ref = bf16[128,128]{1,0:T(8,128)(2,1)S(1)} collective-permute-done((bf16[128,128]{1,0:T(8,128)(2,1)S(1)}, bf16[128,128]{1,0:T(8,128)(2,1)S(1)}, u32[]{:S(2)}, u32[]{:S(2)}) %collective-permute-start.5) | collective-permute-done | bytes 32800 | tf_op jit(solution)/shard_map/ppermute | solution.py:473
  50.5 4.6 %shard_map.196 = (bf16[16,64,128]{2,1,0:T(8,128)(2,1)}, bf16[512,128]{1,0:T(8,128)(2,1)S(1)}) custom-call(f32[4]{0:T(128)S(1)} %copy-done.14, bf16[128,128]{1,0:T(8,128)(2,1)S(1)} %copy-done.11, bf16[128,128]{1,0:T(8,128)(2,1)S(1)} %collective-permute-done.3.q1_ref, bf16[128,128]{1,0:T(8,128)(2,1)S(1)} %collective-permute-done.4.q2_ref, ...), custom_call_target="tpu_custom_call" | custom-call | bytes 1 | tf_op jit(solution)/shard_map/pallas_call | solution.py:41
  55.7 4.8 %all-to-all-start.1 = ((bf16[16,64,128]{2,1,0:T(8,128)(2,1)}), bf16[16,64,128]{2,1,0:T(8,128)(2,1)S(1)}, u32[]{:S(2)}, u32[]{:S(2)}) async-start(bf16[16,64,128]{2,1,0:T(8,128)(2,1)} %get-tuple-element.41), calls=%async_computation.1 | async-start | bytes 524288 | tf_op jit(solution)/shard_map/all_to_all | solution.py:485
  60.5 5.6 %collective-permute-done.6.rest_0_.d1_ref = bf16[1,1024,512]{2,1,0:T(8,128)(2,1)} collective-permute-done((bf16[1,1024,512]{2,1,0:T(8,128)(2,1)S(1)}, bf16[1,1024,512]{2,1,0:T(8,128)(2,1)}, u32[]{:S(2)}, u32[]{:S(2)}) %collective-permute-start.6) | collective-permute-done | bytes 1048608 | tf_op jit(solution)/shard_map/ppermute | solution.py:422
  66.1 5.0 %all-to-all-done.1.att_ref = bf16[16,64,128]{2,1,0:T(8,128)(2,1)S(1)} async-done(((bf16[16,64,128]{2,1,0:T(8,128)(2,1)}), bf16[16,64,128]{2,1,0:T(8,128)(2,1)S(1)}, u32[]{:S(2)}, u32[]{:S(2)}) %all-to-all-start.1) | async-done | bytes 262176 | tf_op jit(solution)/shard_map/all_to_all | solution.py:485
  71.8 5.1 %shard_map.197 = (f32[128,256]{1,0:T(8,128)}, bf16[128,256]{1,0:T(8,128)(2,1)}, bf16[128,256]{1,0:T(8,128)(2,1)}, bf16[128,256]{1,0:T(8,128)(2,1)}, bf16[128,256]{1,0:T(8,128)(2,1)}) custom-call(bf16[16,64,128]{2,1,0:T(8,128)(2,1)} %copy-done.17, bf16[128,1024]{1,0:T(8,128)(2,1)} %get-tuple-element.42.x_ref, f32[1,1024]{1,0:T(1,128)} %bitcast.31, ...), custom_call_target="tpu_custom_call" | custom-call | flops 1 | bytes 1 | tf_op jit(solution)/shard_map/pallas_call | solution.py:184
  79.9 4.0 %collective-permute-done.8.p1_ref = bf16[128,256]{1,0:T(8,128)(2,1)S(1)} collective-permute-done((bf16[128,256]{1,0:T(8,128)(2,1)}, bf16[128,256]{1,0:T(8,128)(2,1)S(1)}, u32[]{:S(2)}, u32[]{:S(2)}) %collective-permute-start.8) | collective-permute-done | bytes 65568 | tf_op jit(solution)/shard_map/ppermute | solution.py:422
  83.9 2.0 collective-permute-done.9.p2_ref
  90.6 3.1 %collective-permute-done.13.c3_ref = bf16[128,256]{1,0:T(8,128)(2,1)S(1)} collective-permute-done((bf16[128,256]{1,0:T(8,128)(2,1)S(1)}, bf16[128,256]{1,0:T(8,128)(2,1)S(1)}, u32[]{:S(2)}, u32[]{:S(2)}) %collective-permute-start.13) | collective-permute-done | bytes 65568 | tf_op jit(solution)/shard_map/ppermute | solution.py:422
  93.7 2.4 %collective-permute-done.12.c2_ref = bf16[128,256]{1,0:T(8,128)(2,1)S(1)} collective-permute-done((bf16[128,256]{1,0:T(8,128)(2,1)S(1)}, bf16[128,256]{1,0:T(8,128)(2,1)S(1)}, u32[]{:S(2)}, u32[]{:S(2)}) %collective-permute-start.12) | collective-permute-done | bytes 65568 | tf_op jit(solution)/shard_map/ppermute | solution.py:422
  98.2 3.0 %shard_map.199 = (bf16[128,1024]{1,0:T(8,128)(2,1)}, bf16[512,1024]{1,0:T(8,128)(2,1)}) custom-call(bf16[512,128]{1,0:T(8,128)(2,1)} %copy-done.7, bf16[128,256]{1,0:T(8,128)(2,1)} %copy-done.6, bf16[128,256]{1,0:T(8,128)(2,1)} %copy-done.24, bf16[128,256]{1,0:T(8,128)(2,1)} %copy-done.23, bf16[128,256]{1,0:T(8,128)(2,1)} %copy-done.22), custom_call_target="tpu_custom_call" | custom-call | bytes 1 | tf_op jit(solution)/shard_map/pallas_call | solution.py:41
  101.2 9.0 %all-to-all-start.2 = ((bf16[32,16,1024]{2,1,0:T(8,128)(2,1)}), bf16[32,16,1024]{2,1,0:T(8,128)(2,1)S(1)}, u32[]{:S(2)}, u32[]{:S(2)}) async-start(bf16[32,16,1024]{2,1,0:T(8,128)(2,1)} %bitcast.24), calls=%async_computation.2 | async-start | bytes 2097152 | tf_op jit(solution)/shard_map/all_to_all | solution.py:507
  110.9 2.1 %collective-permute-start.15 = (bf16[1,1024,512]{2,1,0:T(8,128)(2,1)}, bf16[1,1024,512]{2,1,0:T(8,128)(2,1)S(1)}, u32[]{:S(2)}, u32[]{:S(2)}) collective-permute-start(bf16[1,1024,512]{2,1,0:T(8,128)(2,1)} %u0_ref.1), channel_id=1, source_target_pairs={{0,3},{1,0},{2,1},{3,2},{4,7},{5,4},{6,5},{7,6},{8,11},{9,8},{10,9... | collective-permute-start | bytes 3145736 | tf_op jit(solution)/shard_map/ppermute | solution.py:422
  113.0 6.8 %shard_map.200 = (bf16[4,1024,512]{2,1,0:T(8,128)(2,1)}, bf16[1024,512]{1,0:T(8,128)(2,1)}, bf16[3,1024,512]{2,1,0:T(8,128)(2,1)}, f32[8,128]{1,0:T(8,128)S(1)}) custom-call(bf16[4,1024,512]{2,1,0:T(8,128)(2,1)} %all-gather.5.cloned.1.call-done.gate_ref, bf16[1,1024,512]{2,1,0:T(8,128)(2,1)} %u0_ref.1, bf16[1,1024,512]{2,1,0:T(8,128)(2,1)} %d0_ref.1, ...), custom_call_target="tpu_custom_call" | custom-call | flops 1 | bytes 1 | tf_op jit(solution)/shard_map/pallas_call | solution.py:274
  120.3 6.8 %all-to-all-done.2 = bf16[32,16,1024]{2,1,0:T(8,128)(2,1)S(1)} async-done(((bf16[32,16,1024]{2,1,0:T(8,128)(2,1)}), bf16[32,16,1024]{2,1,0:T(8,128)(2,1)S(1)}, u32[]{:S(2)}, u32[]{:S(2)}) %all-to-all-start.2) | async-done | bytes 1048608 | tf_op jit(solution)/shard_map/all_to_all | solution.py:507
  128.1 4.0 %shard_map.201 = (f32[160,1024]{1,0:T(8,128)}, bf16[512,1024]{1,0:T(8,128)(2,1)}) custom-call(bf16[512,1024]{1,0:T(8,128)(2,1)} %bitcast.23, s32[160,1]{1,0:T(8,128)} %get-tuple-element.50.pidx_ref, bf16[160,1024]{1,0:T(8,128)(2,1)} %fine_ref.1, s32[1,160]{1,0:T(1,128)} %bitcast.34, bf16[8,1024]{1,0:T(8,128)(2,1)} %table_ref.1, f32[1,1024]{1,0:T(1,128)} %bitcast.32, ...), custom_call_target="tpu_custom_call" | custom-call | bytes 1 | tf_op jit(solution)/shard_map/pallas_call | solution.py:41
  132.2 4.0 %all-to-all-start.3 = ((bf16[32,16,1024]{2,1,0:T(8,128)(2,1)}), bf16[32,16,1024]{2,1,0:T(8,128)(2,1)S(1)}, u32[]{:S(2)}, u32[]{:S(2)}) async-start(bf16[32,16,1024]{2,1,0:T(8,128)(2,1)} %bitcast.25), calls=%async_computation.3 | async-start | bytes 2097152 | tf_op jit(solution)/shard_map/all_to_all | solution.py:527
  137.8 2.2 %shard_map.204 = bf16[1,1024,512]{2,1,0:T(8,128)(2,1)} custom-call(bf16[1,1024,512]{2,1,0:T(8,128)(2,1)} %copy-done.15, bf16[1,1024,512]{2,1,0:T(8,128)(2,1)} %copy-done.2), custom_call_target="tpu_custom_call" | custom-call | flops 1 | bytes 1 | tf_op jit(solution)/shard_map/pallas_call | solution.py:297
  140.1 2.3 %collective-permute-start.21 = (bf16[1,1024,512]{2,1,0:T(8,128)(2,1)}, bf16[1,1024,512]{2,1,0:T(8,128)(2,1)}, u32[]{:S(2)}, u32[]{:S(2)}) collective-permute-start(bf16[1,1024,512]{2,1,0:T(8,128)(2,1)} %shard_map.204), channel_id=1, source_target_pairs={{0,3},{1,0},{2,1},{3,2},{4,7},{5,4},{6,5},{7,6},{8,11},{9,8},{10,9... | collective-permute-start | bytes 3145736 | tf_op jit(solution)/shard_map/ppermute | solution.py:422
  142.3 10.7 %all-to-all-done.3 = bf16[32,16,1024]{2,1,0:T(8,128)(2,1)S(1)} async-done(((bf16[32,16,1024]{2,1,0:T(8,128)(2,1)}), bf16[32,16,1024]{2,1,0:T(8,128)(2,1)S(1)}, u32[]{:S(2)}, u32[]{:S(2)}) %all-to-all-start.3) | async-done | bytes 1048608 | tf_op jit(solution)/shard_map/all_to_all | solution.py:527
  154.9 2.2 %copy-done = bf16[4,1024,512]{2,1,0:T(8,128)(2,1)S(1)} copy-done((bf16[4,1024,512]{2,1,0:T(8,128)(2,1)S(1)}, bf16[4,1024,512]{2,1,0:T(8,128)(2,1)}, u32[]{:S(2)}) %copy-start) | copy-done | bytes 4194328
  157.1 1.9 copy-done.1
  159.0 5.6 %shard_map.202 = (f32[512,1024]{1,0:T(8,128)S(1)}, bf16[2,1024,512]{2,1,0:T(8,128)(2,1)S(1)}) custom-call(bf16[512,1024]{1,0:T(8,128)(2,1)S(1)} %bitcast.18, bf16[4,1024,512]{2,1,0:T(8,128)(2,1)S(1)} %copy-done, bf16[1024,512]{1,0:T(8,128)(2,1)S(1)} %copy-done.4, bf16[3,1024,512]{2,1,0:T(8,128)(2,1)S(1)} %copy-done.1, ...), custom_call_target="tpu_custom_call" | custom-call | flops 1 | bytes 1 | tf_op jit(solution)/shard_map/pallas_call | solution.py:331
  164.6 5.2 %shard_map.203 = (f32[512,1024]{1,0:T(8,128)S(1)}, bf16[512,1024]{1,0:T(8,128)(2,1)S(1)}) custom-call(bf16[128,1024]{1,0:T(8,128)(2,1)S(1)} %collective-permute-done.16.x0_ref, bf16[128,1024]{1,0:T(8,128)(2,1)S(1)} %collective-permute-done.17.x1_ref, bf16[128,1024]{1,0:T(8,128)(2,1)S(1)} %collective-permute-done.18.x2_ref, ...), custom_call_target="tpu_custom_call" | custom-call | flops 1 | bytes 1 | tf_op jit(solution)/shard_map/pallas_call | solution.py:353
  169.8 2.7 %shard_map.205 = (bf16[512,1024]{1,0:T(8,128)(2,1)S(1)}, bf16[1024,512]{1,0:T(8,128)(2,1)S(1)}, bf16[1024,512]{1,0:T(8,128)(2,1)S(1)}) custom-call(bf16[512,1024]{1,0:T(8,128)(2,1)S(1)} %get-tuple-element.59.x_ref, f32[512,1024]{1,0:T(8,128)S(1)} %get-tuple-element.60.acc_ref, bf16[4,1024,512]{2,1,0:T(8,128)(2,1)S(1)} %copy-done, ...), custom_call_target="tpu_custom_call" | custom-call | flops 1 | bytes 1 | tf_op jit(solution)/shard_map/pallas_call | solution.py:381
  175.5 20.8 %all_to_all.43 = bf16[32,16,1024]{2,1,0:T(8,128)(2,1)S(1)} all-to-all(bf16[32,16,1024]{2,1,0:T(8,128)(2,1)S(1)} %bitcast.21), channel_id=1, replica_groups=mesh['seq'=32,'exp'=4] {'seq'}, dimensions={0} | all-to-all | bytes 2097152 | tf_op jit(solution)/shard_map/all_to_all | solution.py:536
  (101 shorter events, 29.7 us)
Async XLA Ops:
  7.2 64.0 %all-gather.3.cloned.1.call-start = ((), (), s32[]{:S(2)}) async-start(), calls=%async_computation.5 | async-start | bytes 2621440 | tf_op jit(solution)/shard_map/all_gather | solution.py:447
  7.9 105.1 %all-gather.5.cloned.1.call-start = ((), (), s32[]{:S(2)}) async-start(), calls=%async_computation.6 | async-start | bytes 5242880 | tf_op jit(solution)/shard_map/all_gather | solution.py:448
  8.6 8.3 %collective-permute-start.1 = (bf16[128,256]{1,0:T(8,128)(2,1)}, bf16[128,256]{1,0:T(8,128)(2,1)S(1)}, u32[]{:S(2)}, u32[]{:S(2)}) collective-permute-start(bf16[128,256]{1,0:T(8,128)(2,1)} %f0_ref.1), channel_id=1, source_target_pairs={{0,2},{1,3},{2,0},{3,1},{4,6},{5,7},{6,4},{7,5},{8,10},{9,11},{10,... | collective-permute-start | bytes 196616 | tf_op jit(solution)/shard_map/ppermute | solution.py:422
  12.5 4.5 %collective-permute-start = (bf16[128,256]{1,0:T(8,128)(2,1)}, bf16[128,256]{1,0:T(8,128)(2,1)S(1)}, u32[]{:S(2)}, u32[]{:S(2)}) collective-permute-start(bf16[128,256]{1,0:T(8,128)(2,1)} %f0_ref.1), channel_id=1, source_target_pairs={{0,1},{1,2},{2,3},{3,0},{4,5},{5,6},{6,7},{7,4},{8,9},{9,10},{10,1... | collective-permute-start | bytes 196616 | tf_op jit(solution)/shard_map/ppermute | solution.py:422
  12.9 4.1 %collective-permute-start.2 = (bf16[128,256]{1,0:T(8,128)(2,1)}, bf16[128,256]{1,0:T(8,128)(2,1)S(1)}, u32[]{:S(2)}, u32[]{:S(2)}) collective-permute-start(bf16[128,256]{1,0:T(8,128)(2,1)} %f0_ref.1), channel_id=1, source_target_pairs={{0,3},{1,0},{2,1},{3,2},{4,7},{5,4},{6,5},{7,6},{8,11},{9,8},{10,9... | collective-permute-start | bytes 196616 | tf_op jit(solution)/shard_map/ppermute | solution.py:422
  17.7 32.8 %copy-start.14 = (f32[4]{0:T(128)S(1)}, f32[4]{0:T(128)}, u32[]{:S(2)}) copy-start(f32[4]{0:T(128)} %scale_ref.1) | copy-start | bytes 52
  21.8 28.6 %copy-start.11 = (bf16[128,128]{1,0:T(8,128)(2,1)S(1)}, bf16[128,128]{1,0:T(8,128)(2,1)}, u32[]{:S(2)}) copy-start(bf16[128,128]{1,0:T(8,128)(2,1)} %get-tuple-element.35.q0_ref) | copy-start | bytes 98308
  21.8 28.6 %all-to-all-start = ((bf16[32,144,128]{2,1,0:T(8,128)(2,1)}), bf16[32,144,128]{2,1,0:T(8,128)(2,1)S(1)}, u32[]{:S(2)}, u32[]{:S(2)}) async-start(bf16[32,144,128]{2,1,0:T(8,128)(2,1)} %get-tuple-element.39), calls=%async_computation | async-start | bytes 2359296 | tf_op jit(solution)/shard_map/all_to_all | solution.py:475
  32.1 34.0 %collective-permute-start.6 = (bf16[1,1024,512]{2,1,0:T(8,128)(2,1)S(1)}, bf16[1,1024,512]{2,1,0:T(8,128)(2,1)}, u32[]{:S(2)}, u32[]{:S(2)}) collective-permute-start(bf16[1,1024,512]{2,1,0:T(8,128)(2,1)S(1)} %copy-done.18), channel_id=1, source_target_pairs={{0,1},{1,2},{2,3},{3,0},{4,5},{5,6},{6,7},{7,4},{8,9},{9,10},{10,1... | collective-permute-start | bytes 3145736 | tf_op jit(solution)/shard_map/ppermute | solution.py:422
  32.2 33.9 %collective-permute-start.7 = (bf16[1,1024,512]{2,1,0:T(8,128)(2,1)S(1)}, bf16[1,1024,512]{2,1,0:T(8,128)(2,1)S(1)}, u32[]{:S(2)}, u32[]{:S(2)}) collective-permute-start(bf16[1,1024,512]{2,1,0:T(8,128)(2,1)S(1)} %copy-done.18), channel_id=1, source_target_pairs={{0,3},{1,0},{2,1},{3,2},{4,7},{5,4},{6,5},{7,6},{8,11},{9,8},{10,9... | collective-permute-start | bytes 3145736 | tf_op jit(solution)/shard_map/ppermute | solution.py:422
  35.2 2.2 %collective-permute-start.3 = (bf16[128,128]{1,0:T(8,128)(2,1)S(1)}, bf16[128,128]{1,0:T(8,128)(2,1)S(1)}, u32[]{:S(2)}, u32[]{:S(2)}) collective-permute-start(bf16[128,128]{1,0:T(8,128)(2,1)S(1)} %copy-done.27), channel_id=1, source_target_pairs={{0,4},{4,0},{8,12},{12,8},{16,20},{20,16},{24,28},{28,24},{32,36},... | collective-permute-start | bytes 98312 | tf_op jit(solution)/shard_map/ppermute | solution.py:473
  35.8 8.4 %collective-permute-start.4 = (bf16[128,128]{1,0:T(8,128)(2,1)S(1)}, bf16[128,128]{1,0:T(8,128)(2,1)S(1)}, u32[]{:S(2)}, u32[]{:S(2)}) collective-permute-start(bf16[128,128]{1,0:T(8,128)(2,1)S(1)} %copy-done.26), channel_id=1, source_target_pairs={{0,8},{4,12},{8,0},{12,4},{16,24},{20,28},{24,16},{28,20},{32,40},... | collective-permute-start | bytes 98312 | tf_op jit(solution)/shard_map/ppermute | solution.py:473
  37.3 11.3 %collective-permute-start.5 = (bf16[128,128]{1,0:T(8,128)(2,1)S(1)}, bf16[128,128]{1,0:T(8,128)(2,1)S(1)}, u32[]{:S(2)}, u32[]{:S(2)}) collective-permute-start(bf16[128,128]{1,0:T(8,128)(2,1)S(1)} %copy-done.25), channel_id=1, source_target_pairs={{0,12},{4,8},{8,4},{12,0},{16,28},{20,24},{24,20},{28,16},{32,44},... | collective-permute-start | bytes 98312 | tf_op jit(solution)/shard_map/ppermute | solution.py:473
  55.7 15.4 %all-to-all-start.1 = ((bf16[16,64,128]{2,1,0:T(8,128)(2,1)}), bf16[16,64,128]{2,1,0:T(8,128)(2,1)S(1)}, u32[]{:S(2)}, u32[]{:S(2)}) async-start(bf16[16,64,128]{2,1,0:T(8,128)(2,1)} %get-tuple-element.41), calls=%async_computation.1 | async-start | bytes 524288 | tf_op jit(solution)/shard_map/all_to_all | solution.py:485
  77.0 6.9 %collective-permute-start.8 = (bf16[128,256]{1,0:T(8,128)(2,1)}, bf16[128,256]{1,0:T(8,128)(2,1)S(1)}, u32[]{:S(2)}, u32[]{:S(2)}) collective-permute-start(bf16[128,256]{1,0:T(8,128)(2,1)} %get-tuple-element.44), channel_id=1, source_target_pairs={{0,1},{1,2},{2,3},{3,0},{4,5},{5,6},{6,7},{7,4},{8,9},{9,10},{10,1... | collective-permute-start | bytes 196616 | tf_op jit(solution)/shard_map/ppermute | solution.py:422
  77.4 8.5 %collective-permute-start.9 = (bf16[128,256]{1,0:T(8,128)(2,1)}, bf16[128,256]{1,0:T(8,128)(2,1)S(1)}, u32[]{:S(2)}, u32[]{:S(2)}) collective-permute-start(bf16[128,256]{1,0:T(8,128)(2,1)} %get-tuple-element.45), channel_id=1, source_target_pairs={{0,2},{1,3},{2,0},{3,1},{4,6},{5,7},{6,4},{7,5},{8,10},{9,11},{10,... | collective-permute-start | bytes 196616 | tf_op jit(solution)/shard_map/ppermute | solution.py:422
  79.1 7.9 %collective-permute-start.10 = (bf16[128,256]{1,0:T(8,128)(2,1)}, bf16[128,256]{1,0:T(8,128)(2,1)S(1)}, u32[]{:S(2)}, u32[]{:S(2)}) collective-permute-start(bf16[128,256]{1,0:T(8,128)(2,1)} %get-tuple-element.46), channel_id=1, source_target_pairs={{0,3},{1,0},{2,1},{3,2},{4,7},{5,4},{6,5},{7,6},{8,11},{9,8},{10,9... | collective-permute-start | bytes 196616 | tf_op jit(solution)/shard_map/ppermute | solution.py:422
  88.8 5.0 %collective-permute-start.13 = (bf16[128,256]{1,0:T(8,128)(2,1)S(1)}, bf16[128,256]{1,0:T(8,128)(2,1)S(1)}, u32[]{:S(2)}, u32[]{:S(2)}) collective-permute-start(bf16[128,256]{1,0:T(8,128)(2,1)S(1)} %shard_map.198.c0_ref), channel_id=1, source_target_pairs={{0,3},{1,0},{2,1},{3,2},{4,7},{5,4},{6,5},{7,6},{8,11},{9,8},{10,9... | collective-permute-start | bytes 196616 | tf_op jit(solution)/shard_map/ppermute | solution.py:422
  89.8 6.3 %collective-permute-start.12 = (bf16[128,256]{1,0:T(8,128)(2,1)S(1)}, bf16[128,256]{1,0:T(8,128)(2,1)S(1)}, u32[]{:S(2)}, u32[]{:S(2)}) collective-permute-start(bf16[128,256]{1,0:T(8,128)(2,1)S(1)} %shard_map.198.c0_ref), channel_id=1, source_target_pairs={{0,2},{1,3},{2,0},{3,1},{4,6},{5,7},{6,4},{7,5},{8,10},{9,11},{10,... | collective-permute-start | bytes 196616 | tf_op jit(solution)/shard_map/ppermute | solution.py:422
  90.3 7.3 %collective-permute-start.11 = (bf16[128,256]{1,0:T(8,128)(2,1)S(1)}, bf16[128,256]{1,0:T(8,128)(2,1)S(1)}, u32[]{:S(2)}, u32[]{:S(2)}) collective-permute-start(bf16[128,256]{1,0:T(8,128)(2,1)S(1)} %shard_map.198.c0_ref), channel_id=1, source_target_pairs={{0,1},{1,2},{2,3},{3,0},{4,5},{5,6},{6,7},{7,4},{8,9},{9,10},{10,1... | collective-permute-start | bytes 196616 | tf_op jit(solution)/shard_map/ppermute | solution.py:422
  101.2 25.9 %all-to-all-start.2 = ((bf16[32,16,1024]{2,1,0:T(8,128)(2,1)}), bf16[32,16,1024]{2,1,0:T(8,128)(2,1)S(1)}, u32[]{:S(2)}, u32[]{:S(2)}) async-start(bf16[32,16,1024]{2,1,0:T(8,128)(2,1)} %bitcast.24), calls=%async_computation.2 | async-start | bytes 2097152 | tf_op jit(solution)/shard_map/all_to_all | solution.py:507
  110.2 26.1 %collective-permute-start.14 = (bf16[1,1024,512]{2,1,0:T(8,128)(2,1)}, bf16[1,1024,512]{2,1,0:T(8,128)(2,1)}, u32[]{:S(2)}, u32[]{:S(2)}) collective-permute-start(bf16[1,1024,512]{2,1,0:T(8,128)(2,1)} %u0_ref.1), channel_id=1, source_target_pairs={{0,1},{1,2},{2,3},{3,0},{4,5},{5,6},{6,7},{7,4},{8,9},{9,10},{10,1... | collective-permute-start | bytes 3145736 | tf_op jit(solution)/shard_map/ppermute | solution.py:422
  110.9 25.9 %collective-permute-start.15 = (bf16[1,1024,512]{2,1,0:T(8,128)(2,1)}, bf16[1,1024,512]{2,1,0:T(8,128)(2,1)S(1)}, u32[]{:S(2)}, u32[]{:S(2)}) collective-permute-start(bf16[1,1024,512]{2,1,0:T(8,128)(2,1)} %u0_ref.1), channel_id=1, source_target_pairs={{0,3},{1,0},{2,1},{3,2},{4,7},{5,4},{6,5},{7,6},{8,11},{9,8},{10,9... | collective-permute-start | bytes 3145736 | tf_op jit(solution)/shard_map/ppermute | solution.py:422
  132.2 20.9 %all-to-all-start.3 = ((bf16[32,16,1024]{2,1,0:T(8,128)(2,1)}), bf16[32,16,1024]{2,1,0:T(8,128)(2,1)S(1)}, u32[]{:S(2)}, u32[]{:S(2)}) async-start(bf16[32,16,1024]{2,1,0:T(8,128)(2,1)} %bitcast.25), calls=%async_computation.3 | async-start | bytes 2097152 | tf_op jit(solution)/shard_map/all_to_all | solution.py:527
  136.3 33.5 %collective-permute-start.20 = (bf16[1,1024,512]{2,1,0:T(8,128)(2,1)}, bf16[1,1024,512]{2,1,0:T(8,128)(2,1)}, u32[]{:S(2)}, u32[]{:S(2)}) collective-permute-start(bf16[1,1024,512]{2,1,0:T(8,128)(2,1)} %collective-permute-done.14.u1_ref), channel_id=1, source_target_pairs={{0,1},{1,2},{2,3},{3,0},{4,5},{5,6},{6,7},{7,4},{8,9},{9,10},{10,1... | collective-permute-start | bytes 3145736 | tf_op jit(solution)/shard_map/ppermute | solution.py:422
  140.1 29.8 %collective-permute-start.21 = (bf16[1,1024,512]{2,1,0:T(8,128)(2,1)}, bf16[1,1024,512]{2,1,0:T(8,128)(2,1)}, u32[]{:S(2)}, u32[]{:S(2)}) collective-permute-start(bf16[1,1024,512]{2,1,0:T(8,128)(2,1)} %shard_map.204), channel_id=1, source_target_pairs={{0,3},{1,0},{2,1},{3,2},{4,7},{5,4},{6,5},{7,6},{8,11},{9,8},{10,9... | collective-permute-start | bytes 3145736 | tf_op jit(solution)/shard_map/ppermute | solution.py:422
  153.1 1.6 collective-permute-start.18
  153.3 11.3 %collective-permute-start.19 = (bf16[128,1024]{1,0:T(8,128)(2,1)S(1)}, bf16[128,1024]{1,0:T(8,128)(2,1)S(1)}, u32[]{:S(2)}, u32[]{:S(2)}) collective-permute-start(bf16[128,1024]{1,0:T(8,128)(2,1)S(1)} %bitcast.28), channel_id=1, source_target_pairs={{0,4},{4,0},{8,12},{12,8},{16,20},{20,16},{24,28},{28,24},{32,36},... | collective-permute-start | bytes 786440 | tf_op jit(solution)/shard_map/ppermute | solution.py:529
  153.7 10.9 %collective-permute-start.17 = (bf16[128,1024]{1,0:T(8,128)(2,1)S(1)}, bf16[128,1024]{1,0:T(8,128)(2,1)S(1)}, u32[]{:S(2)}, u32[]{:S(2)}) collective-permute-start(bf16[128,1024]{1,0:T(8,128)(2,1)S(1)} %bitcast.27), channel_id=1, source_target_pairs={{0,4},{4,0},{8,12},{12,8},{16,20},{20,16},{24,28},{28,24},{32,36},... | collective-permute-start | bytes 786440 | tf_op jit(solution)/shard_map/ppermute | solution.py:529
  154.7 9.9 %collective-permute-start.16 = (bf16[128,1024]{1,0:T(8,128)(2,1)S(1)}, bf16[128,1024]{1,0:T(8,128)(2,1)S(1)}, u32[]{:S(2)}, u32[]{:S(2)}) collective-permute-start(bf16[128,1024]{1,0:T(8,128)(2,1)S(1)} %bitcast.26), channel_id=1, source_target_pairs={{0,4},{4,0},{8,12},{12,8},{16,20},{20,16},{24,28},{28,24},{32,36},... | collective-permute-start | bytes 786440 | tf_op jit(solution)/shard_map/ppermute | solution.py:529
  172.6 2.7 %collective-permute-start.22 = (bf16[512,1024]{1,0:T(8,128)(2,1)S(1)}, bf16[512,1024]{1,0:T(8,128)(2,1)S(1)}, u32[]{:S(2)}, u32[]{:S(2)}) collective-permute-start(bf16[512,1024]{1,0:T(8,128)(2,1)S(1)} %get-tuple-element.63), channel_id=1, source_target_pairs={{0,4},{4,0},{8,12},{12,8},{16,20},{20,16},{24,28},{28,24},{32,36},... | collective-permute-start | bytes 3145736 | tf_op jit(solution)/shard_map/ppermute | solution.py:533
  175.5 20.8 %copy-start.5 = (f32[160,1024]{1,0:T(8,128)S(1)}, f32[160,1024]{1,0:T(8,128)}, u32[]{:S(2)}) copy-start(f32[160,1024]{1,0:T(8,128)} %get-tuple-element.65.sum_ref) | copy-start | bytes 1966084
  (25 other events, 164.0 us)
Sparse Core Ops, SparseCore 0:
  9.7 40.9 all-gather.2
  52.3 56.2 all-gather.4

commit v6 on v5

--- a/solution.py
+++ b/solution.py
@@ -339,8 +339,8 @@
     )(x, *staged, ur, ul, *ready)
 
 
-def second_kernel(x0_ref, x1_ref, x2_ref, x3_ref, g_ref, u_ref, d_ref, ups_ref, out_ref, x_out):
-    x = jnp.concatenate([r[...] for r in (x0_ref, x1_ref, x2_ref, x3_ref)], axis=0)
+def second_kernel(x0_ref, x1_ref, g_ref, u_ref, d_ref, ups_ref, out_ref, x_out):
+    x = jnp.concatenate([r[...] for r in (x0_ref, x1_ref)], axis=0)
     x_out[...] = x
     acc = swiglu(x, g_ref[0], u_ref[...], d_ref[0])
     for j in (1, 2):
@@ -352,7 +352,7 @@
     n = EXPERTS * SLOTS
     return pl.pallas_call(
         second_kernel,
-        in_specs=[INNER] * 8,
+        in_specs=[INNER] * 6,
         out_specs=[INNER] * 2,
         out_shape=[sds((n, D), F32), sds((n, D), BF)],
         compiler_params=pltpu.CompilerParams(vmem_limit_bytes=30 << 20),
@@ -517,7 +517,7 @@
         norm3_gain.reshape(1, D),
         didxt,
         ready=(token,),
-        limit=60,
+        limit=56,
         far=(1,),
         scratch_shapes=[
             pltpu.VMEM((EXPERTS * SLOTS, D), BF),
@@ -526,7 +526,7 @@
     )
     mine = lax.all_to_all(outgoing, "seq", 0, 0, tiled=True)
     mine = mine.reshape(EXPERTS * SLOTS, D)
-    others = [lax.ppermute(mine[i * 128 : i * 128 + 128], "seq", SWAP) for i in range(4)]
+    others = [lax.ppermute(mine[i * 256 : i * 256 + 256], "seq", SWAP) for i in range(2)]
     acc_mine, ups = first(mine, staged, ur, ul)
     acc_other, other = second(others, staged, ups)
     for_other, u3, d3 = last(other, acc_other, staged[0], u2, d2)

time: 205 us -> 205 us (level)
  transfers between devices with their start and end apart: 29 -> 27, of which waited for: 16 -> 15; matrix products, arithmetic and copies ran while one was open for 0% -> 0% of each run, Pallas kernels for 22% -> 22%
where the time goes in v6:
time: 205 us; the launch traced here: 204 us
  waiting for transfers between devices  57.4 us (28%)
  starting transfers between devices  51 us (25%)
  Pallas kernels  48.6 us (24%)
  blocking collectives  21.2 us (10%)
  between operations  14.3 us (7%)
  local copies, waits for them, and re-layouts  11.1 us (5%)
    all_to_all x1, blocking collectives, per_device(): returned = lax.all_to_all(result, 'seq', 0, 0, tiled=True)  21.2 us
    ppermute x15, starting transfers between devices, turn(): return lax.ppermute(v, 'exp', [(i, (i + k) % N_EXP) for i in range(N_EXP)])  19.9 us
    ppermute x15, waiting for transfers between devices, turn(): return lax.ppermute(v, 'exp', [(i, (i + k) % N_EXP) for i in range(N_EXP)])  19.8 us
    pallas_call x8, Pallas kernels, call(): pl.pallas_call(kernel, out_shape=out_shape, in_specs=space + [pl.BlockSpe...  19.1 us
    ppermute x3, waiting for transfers between devices, per_device(): lax.ppermute(qs[k], 'seq', [(i, i ^ k) for i in range(N_SEQ)])  11.1 us
    unnamed x56, local copies, waits for them, and re-layouts  11 us
    all_to_all x1, waiting for transfers between devices, per_device(): mine = lax.all_to_all(outgoing, 'seq', 0, 0, tiled=True)  10.7 us
    all_to_all x1, starting transfers between devices, per_device(): kv = lax.all_to_all(kv, 'seq', 0, 0, tiled=True)  10.2 us
  transfers between devices with their start and end apart: 27, of which 15 were waited for; matrix products, arithmetic and copies ran while one was open for 0% of the time, Pallas kernels for 22%

profile of v6, /device:TPU:1, one launch (start us, length us, event | category | flops | bytes accessed | tf_op | source)
XLA Modules:
  0.0 203.7 jit_solution(16331034702505243470)
XLA Ops:
  8.6 3.8 %collective-permute-start.1 = (bf16[128,256]{1,0:T(8,128)(2,1)}, bf16[128,256]{1,0:T(8,128)(2,1)S(1)}, u32[]{:S(2)}, u32[]{:S(2)}) collective-permute-start(bf16[128,256]{1,0:T(8,128)(2,1)} %f0_ref.1), channel_id=1, source_target_pairs={{0,2},{1,3},{2,0},{3,1},{4,6},{5,7},{6,4},{7,5},{8,10},{9,11},{10,... | collective-permute-start | bytes 196616 | tf_op jit(solution)/shard_map/ppermute | solution.py:422
  12.9 2.3 %collective-permute-start.2 = (bf16[128,256]{1,0:T(8,128)(2,1)}, bf16[128,256]{1,0:T(8,128)(2,1)S(1)}, u32[]{:S(2)}, u32[]{:S(2)}) collective-permute-start(bf16[128,256]{1,0:T(8,128)(2,1)} %f0_ref.1), channel_id=1, source_target_pairs={{0,3},{1,0},{2,1},{3,2},{4,7},{5,4},{6,5},{7,6},{8,11},{9,8},{10,9... | collective-permute-start | bytes 196616 | tf_op jit(solution)/shard_map/ppermute | solution.py:422
  17.7 4.2 %shard_map.195 = (bf16[128,1024]{1,0:T(8,128)(2,1)}, bf16[128,128]{1,0:T(8,128)(2,1)}, bf16[128,128]{1,0:T(8,128)(2,1)}, bf16[128,128]{1,0:T(8,128)(2,1)}, bf16[...) custom-call(bf16[128,256]{1,0:T(8,128)(2,1)} %f0_ref.1, bf16[128,256]{1,0:T(8,128)(2,1)} %copy-done.20, ...), custom_call_target="tpu_custom_call" | custom-call | bytes 1 | tf_op jit(solution)/shard_map/pallas_call | solution.py:41
  21.9 10.2 %all-to-all-start = ((bf16[32,144,128]{2,1,0:T(8,128)(2,1)}), bf16[32,144,128]{2,1,0:T(8,128)(2,1)S(1)}, u32[]{:S(2)}, u32[]{:S(2)}) async-start(bf16[32,144,128]{2,1,0:T(8,128)(2,1)} %get-tuple-element.39), calls=%async_computation | async-start | bytes 2359296 | tf_op jit(solution)/shard_map/all_to_all | solution.py:475
  32.2 3.0 %collective-permute-start.7 = (bf16[1,1024,512]{2,1,0:T(8,128)(2,1)S(1)}, bf16[1,1024,512]{2,1,0:T(8,128)(2,1)S(1)}, u32[]{:S(2)}, u32[]{:S(2)}) collective-permute-start(bf16[1,1024,512]{2,1,0:T(8,128)(2,1)S(1)} %copy-done.18), channel_id=1, source_target_pairs={{0,3},{1,0},{2,1},{3,2},{4,7},{5,4},{6,5},{7,6},{8,11},{9,8},{10,9... | collective-permute-start | bytes 3145736 | tf_op jit(solution)/shard_map/ppermute | solution.py:422
  37.5 6.6 %collective-permute-done.4.q2_ref = bf16[128,128]{1,0:T(8,128)(2,1)S(1)} collective-permute-done((bf16[128,128]{1,0:T(8,128)(2,1)S(1)}, bf16[128,128]{1,0:T(8,128)(2,1)S(1)}, u32[]{:S(2)}, u32[]{:S(2)}) %collective-permute-start.4) | collective-permute-done | bytes 32800 | tf_op jit(solution)/shard_map/ppermute | solution.py:473
  44.1 4.5 %collective-permute-done.5.q3_ref = bf16[128,128]{1,0:T(8,128)(2,1)S(1)} collective-permute-done((bf16[128,128]{1,0:T(8,128)(2,1)S(1)}, bf16[128,128]{1,0:T(8,128)(2,1)S(1)}, u32[]{:S(2)}, u32[]{:S(2)}) %collective-permute-start.5) | collective-permute-done | bytes 32800 | tf_op jit(solution)/shard_map/ppermute | solution.py:473
  50.4 4.6 %shard_map.196 = (bf16[16,64,128]{2,1,0:T(8,128)(2,1)}, bf16[512,128]{1,0:T(8,128)(2,1)S(1)}) custom-call(f32[4]{0:T(128)S(1)} %copy-done.14, bf16[128,128]{1,0:T(8,128)(2,1)S(1)} %copy-done.11, bf16[128,128]{1,0:T(8,128)(2,1)S(1)} %collective-permute-done.3.q1_ref, bf16[128,128]{1,0:T(8,128)(2,1)S(1)} %collective-permute-done.4.q2_ref, ...), custom_call_target="tpu_custom_call" | custom-call | bytes 1 | tf_op jit(solution)/shard_map/pallas_call | solution.py:41
  55.7 4.8 %all-to-all-start.1 = ((bf16[16,64,128]{2,1,0:T(8,128)(2,1)}), bf16[16,64,128]{2,1,0:T(8,128)(2,1)S(1)}, u32[]{:S(2)}, u32[]{:S(2)}) async-start(bf16[16,64,128]{2,1,0:T(8,128)(2,1)} %get-tuple-element.41), calls=%async_computation.1 | async-start | bytes 524288 | tf_op jit(solution)/shard_map/all_to_all | solution.py:485
  60.5 5.6 %collective-permute-done.6.rest_0_.d1_ref = bf16[1,1024,512]{2,1,0:T(8,128)(2,1)} collective-permute-done((bf16[1,1024,512]{2,1,0:T(8,128)(2,1)S(1)}, bf16[1,1024,512]{2,1,0:T(8,128)(2,1)}, u32[]{:S(2)}, u32[]{:S(2)}) %collective-permute-start.6) | collective-permute-done | bytes 1048608 | tf_op jit(solution)/shard_map/ppermute | solution.py:422
  66.1 5.0 %all-to-all-done.1.att_ref = bf16[16,64,128]{2,1,0:T(8,128)(2,1)S(1)} async-done(((bf16[16,64,128]{2,1,0:T(8,128)(2,1)}), bf16[16,64,128]{2,1,0:T(8,128)(2,1)S(1)}, u32[]{:S(2)}, u32[]{:S(2)}) %all-to-all-start.1) | async-done | bytes 262176 | tf_op jit(solution)/shard_map/all_to_all | solution.py:485
  71.8 5.2 %shard_map.197 = (f32[128,256]{1,0:T(8,128)}, bf16[128,256]{1,0:T(8,128)(2,1)}, bf16[128,256]{1,0:T(8,128)(2,1)}, bf16[128,256]{1,0:T(8,128)(2,1)}, bf16[128,256]{1,0:T(8,128)(2,1)}) custom-call(bf16[16,64,128]{2,1,0:T(8,128)(2,1)} %copy-done.17, bf16[128,1024]{1,0:T(8,128)(2,1)} %get-tuple-element.42.x_ref, f32[1,1024]{1,0:T(1,128)} %bitcast.27, ...), custom_call_target="tpu_custom_call" | custom-call | flops 1 | bytes 1 | tf_op jit(solution)/shard_map/pallas_call | solution.py:184
  79.9 4.0 %collective-permute-done.8.p1_ref = bf16[128,256]{1,0:T(8,128)(2,1)S(1)} collective-permute-done((bf16[128,256]{1,0:T(8,128)(2,1)}, bf16[128,256]{1,0:T(8,128)(2,1)S(1)}, u32[]{:S(2)}, u32[]{:S(2)}) %collective-permute-start.8) | collective-permute-done | bytes 65568 | tf_op jit(solution)/shard_map/ppermute | solution.py:422
  83.8 2.1 %collective-permute-done.9.p2_ref = bf16[128,256]{1,0:T(8,128)(2,1)S(1)} collective-permute-done((bf16[128,256]{1,0:T(8,128)(2,1)}, bf16[128,256]{1,0:T(8,128)(2,1)S(1)}, u32[]{:S(2)}, u32[]{:S(2)}) %collective-permute-start.9) | collective-permute-done | bytes 65568 | tf_op jit(solution)/shard_map/ppermute | solution.py:422
  90.6 3.1 %collective-permute-done.13.c3_ref = bf16[128,256]{1,0:T(8,128)(2,1)S(1)} collective-permute-done((bf16[128,256]{1,0:T(8,128)(2,1)S(1)}, bf16[128,256]{1,0:T(8,128)(2,1)S(1)}, u32[]{:S(2)}, u32[]{:S(2)}) %collective-permute-start.13) | collective-permute-done | bytes 65568 | tf_op jit(solution)/shard_map/ppermute | solution.py:422
  93.7 2.4 %collective-permute-done.12.c2_ref = bf16[128,256]{1,0:T(8,128)(2,1)S(1)} collective-permute-done((bf16[128,256]{1,0:T(8,128)(2,1)S(1)}, bf16[128,256]{1,0:T(8,128)(2,1)S(1)}, u32[]{:S(2)}, u32[]{:S(2)}) %collective-permute-start.12) | collective-permute-done | bytes 65568 | tf_op jit(solution)/shard_map/ppermute | solution.py:422
  98.2 3.0 %shard_map.199 = (bf16[128,1024]{1,0:T(8,128)(2,1)}, bf16[512,1024]{1,0:T(8,128)(2,1)}) custom-call(bf16[512,128]{1,0:T(8,128)(2,1)} %copy-done.7, bf16[128,256]{1,0:T(8,128)(2,1)} %copy-done.6, bf16[128,256]{1,0:T(8,128)(2,1)} %copy-done.24, bf16[128,256]{1,0:T(8,128)(2,1)} %copy-done.23, bf16[128,256]{1,0:T(8,128)(2,1)} %copy-done.22), custom_call_target="tpu_custom_call" | custom-call | bytes 1 | tf_op jit(solution)/shard_map/pallas_call | solution.py:41
  101.2 9.0 %all-to-all-start.2 = ((bf16[32,16,1024]{2,1,0:T(8,128)(2,1)}), bf16[32,16,1024]{2,1,0:T(8,128)(2,1)S(1)}, u32[]{:S(2)}, u32[]{:S(2)}) async-start(bf16[32,16,1024]{2,1,0:T(8,128)(2,1)} %bitcast.22), calls=%async_computation.2 | async-start | bytes 2097152 | tf_op jit(solution)/shard_map/all_to_all | solution.py:507
  110.9 2.1 %collective-permute-start.15 = (bf16[1,1024,512]{2,1,0:T(8,128)(2,1)}, bf16[1,1024,512]{2,1,0:T(8,128)(2,1)S(1)}, u32[]{:S(2)}, u32[]{:S(2)}) collective-permute-start(bf16[1,1024,512]{2,1,0:T(8,128)(2,1)} %u0_ref.1), channel_id=1, source_target_pairs={{0,3},{1,0},{2,1},{3,2},{4,7},{5,4},{6,5},{7,6},{8,11},{9,8},{10,9... | collective-permute-start | bytes 3145736 | tf_op jit(solution)/shard_map/ppermute | solution.py:422
  113.0 6.7 %shard_map.200 = (bf16[4,1024,512]{2,1,0:T(8,128)(2,1)}, bf16[1024,512]{1,0:T(8,128)(2,1)}, bf16[3,1024,512]{2,1,0:T(8,128)(2,1)}, f32[8,128]{1,0:T(8,128)S(1)}) custom-call(bf16[4,1024,512]{2,1,0:T(8,128)(2,1)} %all-gather.5.cloned.1.call-done.gate_ref, bf16[1,1024,512]{2,1,0:T(8,128)(2,1)} %u0_ref.1, bf16[1,1024,512]{2,1,0:T(8,128)(2,1)} %d0_ref.1, ...), custom_call_target="tpu_custom_call" | custom-call | flops 1 | bytes 1 | tf_op jit(solution)/shard_map/pallas_call | solution.py:274
  120.3 6.8 %all-to-all-done.2 = bf16[32,16,1024]{2,1,0:T(8,128)(2,1)S(1)} async-done(((bf16[32,16,1024]{2,1,0:T(8,128)(2,1)}), bf16[32,16,1024]{2,1,0:T(8,128)(2,1)S(1)}, u32[]{:S(2)}, u32[]{:S(2)}) %all-to-all-start.2) | async-done | bytes 1048608 | tf_op jit(solution)/shard_map/all_to_all | solution.py:507
  128.1 4.1 %shard_map.201 = (f32[160,1024]{1,0:T(8,128)}, bf16[512,1024]{1,0:T(8,128)(2,1)}) custom-call(bf16[512,1024]{1,0:T(8,128)(2,1)} %bitcast.21, s32[160,1]{1,0:T(8,128)} %get-tuple-element.50.pidx_ref, bf16[160,1024]{1,0:T(8,128)(2,1)} %fine_ref.1, s32[1,160]{1,0:T(1,128)} %bitcast.30, bf16[8,1024]{1,0:T(8,128)(2,1)} %table_ref.1, f32[1,1024]{1,0:T(1,128)} %bitcast.28, ...), custom_call_target="tpu_custom_call" | custom-call | bytes 1 | tf_op jit(solution)/shard_map/pallas_call | solution.py:41
  132.2 4.0 %all-to-all-start.3 = ((bf16[32,16,1024]{2,1,0:T(8,128)(2,1)}), bf16[32,16,1024]{2,1,0:T(8,128)(2,1)S(1)}, u32[]{:S(2)}, u32[]{:S(2)}) async-start(bf16[32,16,1024]{2,1,0:T(8,128)(2,1)} %bitcast.23), calls=%async_computation.3 | async-start | bytes 2097152 | tf_op jit(solution)/shard_map/all_to_all | solution.py:527
  137.9 2.2 %shard_map.204 = bf16[1,1024,512]{2,1,0:T(8,128)(2,1)} custom-call(bf16[1,1024,512]{2,1,0:T(8,128)(2,1)} %copy-done.15, bf16[1,1024,512]{2,1,0:T(8,128)(2,1)} %copy-done.2), custom_call_target="tpu_custom_call" | custom-call | flops 1 | bytes 1 | tf_op jit(solution)/shard_map/pallas_call | solution.py:297
  140.1 2.2 %collective-permute-start.19 = (bf16[1,1024,512]{2,1,0:T(8,128)(2,1)}, bf16[1,1024,512]{2,1,0:T(8,128)(2,1)}, u32[]{:S(2)}, u32[]{:S(2)}) collective-permute-start(bf16[1,1024,512]{2,1,0:T(8,128)(2,1)} %shard_map.204), channel_id=1, source_target_pairs={{0,3},{1,0},{2,1},{3,2},{4,7},{5,4},{6,5},{7,6},{8,11},{9,8},{10,9... | collective-permute-start | bytes 3145736 | tf_op jit(solution)/shard_map/ppermute | solution.py:422
  142.3 10.7 %all-to-all-done.3 = bf16[32,16,1024]{2,1,0:T(8,128)(2,1)S(1)} async-done(((bf16[32,16,1024]{2,1,0:T(8,128)(2,1)}), bf16[32,16,1024]{2,1,0:T(8,128)(2,1)S(1)}, u32[]{:S(2)}, u32[]{:S(2)}) %all-to-all-start.3) | async-done | bytes 1048608 | tf_op jit(solution)/shard_map/all_to_all | solution.py:527
  153.7 2.2 %copy-done = bf16[4,1024,512]{2,1,0:T(8,128)(2,1)S(1)} copy-done((bf16[4,1024,512]{2,1,0:T(8,128)(2,1)S(1)}, bf16[4,1024,512]{2,1,0:T(8,128)(2,1)}, u32[]{:S(2)}) %copy-start) | copy-done | bytes 4194328
  155.9 1.9 copy-done.1
  157.8 5.6 %shard_map.202 = (f32[512,1024]{1,0:T(8,128)S(1)}, bf16[2,1024,512]{2,1,0:T(8,128)(2,1)S(1)}) custom-call(bf16[512,1024]{1,0:T(8,128)(2,1)S(1)} %bitcast.16, bf16[4,1024,512]{2,1,0:T(8,128)(2,1)S(1)} %copy-done, bf16[1024,512]{1,0:T(8,128)(2,1)S(1)} %copy-done.4, bf16[3,1024,512]{2,1,0:T(8,128)(2,1)S(1)} %copy-done.1, ...), custom_call_target="tpu_custom_call" | custom-call | flops 1 | bytes 1 | tf_op jit(solution)/shard_map/pallas_call | solution.py:331
  163.5 5.2 %shard_map.203 = (f32[512,1024]{1,0:T(8,128)S(1)}, bf16[512,1024]{1,0:T(8,128)(2,1)S(1)}) custom-call(bf16[256,1024]{1,0:T(8,128)(2,1)S(1)} %collective-permute-done.16.x0_ref, bf16[256,1024]{1,0:T(8,128)(2,1)S(1)} %collective-permute-done.17.x1_ref, bf16[4,1024,512]{2,1,0:T(8,128)(2,1)S(1)} %copy-done, bf16[1024,512]{1,0:T(8,128)(2,1)S(1)} %copy-done.4, ...), custom_call_target="tpu_custom_call" | custom-call | flops 1 | bytes 1 | tf_op jit(solution)/shard_map/pallas_call | solution.py:353
  168.7 2.7 %shard_map.205 = (bf16[512,1024]{1,0:T(8,128)(2,1)S(1)}, bf16[1024,512]{1,0:T(8,128)(2,1)S(1)}, bf16[1024,512]{1,0:T(8,128)(2,1)S(1)}) custom-call(bf16[512,1024]{1,0:T(8,128)(2,1)S(1)} %get-tuple-element.59.x_ref, f32[512,1024]{1,0:T(8,128)S(1)} %get-tuple-element.60.acc_ref, bf16[4,1024,512]{2,1,0:T(8,128)(2,1)S(1)} %copy-done, ...), custom_call_target="tpu_custom_call" | custom-call | flops 1 | bytes 1 | tf_op jit(solution)/shard_map/pallas_call | solution.py:381
  174.4 21.2 %all_to_all.43 = bf16[32,16,1024]{2,1,0:T(8,128)(2,1)S(1)} all-to-all(bf16[32,16,1024]{2,1,0:T(8,128)(2,1)S(1)} %bitcast.19), channel_id=1, replica_groups=mesh['seq'=32,'exp'=4] {'seq'}, dimensions={0} | all-to-all | bytes 2097152 | tf_op jit(solution)/shard_map/all_to_all | solution.py:536
  (97 shorter events, 28.5 us)
Async XLA Ops:
  7.2 63.9 %all-gather.3.cloned.1.call-start = ((), (), s32[]{:S(2)}) async-start(), calls=%async_computation.5 | async-start | bytes 2621440 | tf_op jit(solution)/shard_map/all_gather | solution.py:447
  7.9 105.1 %all-gather.5.cloned.1.call-start = ((), (), s32[]{:S(2)}) async-start(), calls=%async_computation.6 | async-start | bytes 5242880 | tf_op jit(solution)/shard_map/all_gather | solution.py:448
  8.6 8.3 %collective-permute-start.1 = (bf16[128,256]{1,0:T(8,128)(2,1)}, bf16[128,256]{1,0:T(8,128)(2,1)S(1)}, u32[]{:S(2)}, u32[]{:S(2)}) collective-permute-start(bf16[128,256]{1,0:T(8,128)(2,1)} %f0_ref.1), channel_id=1, source_target_pairs={{0,2},{1,3},{2,0},{3,1},{4,6},{5,7},{6,4},{7,5},{8,10},{9,11},{10,... | collective-permute-start | bytes 196616 | tf_op jit(solution)/shard_map/ppermute | solution.py:422
  12.5 4.5 %collective-permute-start = (bf16[128,256]{1,0:T(8,128)(2,1)}, bf16[128,256]{1,0:T(8,128)(2,1)S(1)}, u32[]{:S(2)}, u32[]{:S(2)}) collective-permute-start(bf16[128,256]{1,0:T(8,128)(2,1)} %f0_ref.1), channel_id=1, source_target_pairs={{0,1},{1,2},{2,3},{3,0},{4,5},{5,6},{6,7},{7,4},{8,9},{9,10},{10,1... | collective-permute-start | bytes 196616 | tf_op jit(solution)/shard_map/ppermute | solution.py:422
  12.9 4.2 %collective-permute-start.2 = (bf16[128,256]{1,0:T(8,128)(2,1)}, bf16[128,256]{1,0:T(8,128)(2,1)S(1)}, u32[]{:S(2)}, u32[]{:S(2)}) collective-permute-start(bf16[128,256]{1,0:T(8,128)(2,1)} %f0_ref.1), channel_id=1, source_target_pairs={{0,3},{1,0},{2,1},{3,2},{4,7},{5,4},{6,5},{7,6},{8,11},{9,8},{10,9... | collective-permute-start | bytes 196616 | tf_op jit(solution)/shard_map/ppermute | solution.py:422
  17.7 32.8 %copy-start.14 = (f32[4]{0:T(128)S(1)}, f32[4]{0:T(128)}, u32[]{:S(2)}) copy-start(f32[4]{0:T(128)} %scale_ref.1) | copy-start | bytes 52
  21.8 28.6 %copy-start.11 = (bf16[128,128]{1,0:T(8,128)(2,1)S(1)}, bf16[128,128]{1,0:T(8,128)(2,1)}, u32[]{:S(2)}) copy-start(bf16[128,128]{1,0:T(8,128)(2,1)} %get-tuple-element.35.q0_ref) | copy-start | bytes 98308
  21.9 28.6 %all-to-all-start = ((bf16[32,144,128]{2,1,0:T(8,128)(2,1)}), bf16[32,144,128]{2,1,0:T(8,128)(2,1)S(1)}, u32[]{:S(2)}, u32[]{:S(2)}) async-start(bf16[32,144,128]{2,1,0:T(8,128)(2,1)} %get-tuple-element.39), calls=%async_computation | async-start | bytes 2359296 | tf_op jit(solution)/shard_map/all_to_all | solution.py:475
  32.1 34.0 %collective-permute-start.6 = (bf16[1,1024,512]{2,1,0:T(8,128)(2,1)S(1)}, bf16[1,1024,512]{2,1,0:T(8,128)(2,1)}, u32[]{:S(2)}, u32[]{:S(2)}) collective-permute-start(bf16[1,1024,512]{2,1,0:T(8,128)(2,1)S(1)} %copy-done.18), channel_id=1, source_target_pairs={{0,1},{1,2},{2,3},{3,0},{4,5},{5,6},{6,7},{7,4},{8,9},{9,10},{10,1... | collective-permute-start | bytes 3145736 | tf_op jit(solution)/shard_map/ppermute | solution.py:422
  32.2 33.9 %collective-permute-start.7 = (bf16[1,1024,512]{2,1,0:T(8,128)(2,1)S(1)}, bf16[1,1024,512]{2,1,0:T(8,128)(2,1)S(1)}, u32[]{:S(2)}, u32[]{:S(2)}) collective-permute-start(bf16[1,1024,512]{2,1,0:T(8,128)(2,1)S(1)} %copy-done.18), channel_id=1, source_target_pairs={{0,3},{1,0},{2,1},{3,2},{4,7},{5,4},{6,5},{7,6},{8,11},{9,8},{10,9... | collective-permute-start | bytes 3145736 | tf_op jit(solution)/shard_map/ppermute | solution.py:422
  35.2 2.2 %collective-permute-start.3 = (bf16[128,128]{1,0:T(8,128)(2,1)S(1)}, bf16[128,128]{1,0:T(8,128)(2,1)S(1)}, u32[]{:S(2)}, u32[]{:S(2)}) collective-permute-start(bf16[128,128]{1,0:T(8,128)(2,1)S(1)} %copy-done.27), channel_id=1, source_target_pairs={{0,4},{4,0},{8,12},{12,8},{16,20},{20,16},{24,28},{28,24},{32,36},... | collective-permute-start | bytes 98312 | tf_op jit(solution)/shard_map/ppermute | solution.py:473
  35.8 8.3 %collective-permute-start.4 = (bf16[128,128]{1,0:T(8,128)(2,1)S(1)}, bf16[128,128]{1,0:T(8,128)(2,1)S(1)}, u32[]{:S(2)}, u32[]{:S(2)}) collective-permute-start(bf16[128,128]{1,0:T(8,128)(2,1)S(1)} %copy-done.26), channel_id=1, source_target_pairs={{0,8},{4,12},{8,0},{12,4},{16,24},{20,28},{24,16},{28,20},{32,40},... | collective-permute-start | bytes 98312 | tf_op jit(solution)/shard_map/ppermute | solution.py:473
  37.3 11.3 %collective-permute-start.5 = (bf16[128,128]{1,0:T(8,128)(2,1)S(1)}, bf16[128,128]{1,0:T(8,128)(2,1)S(1)}, u32[]{:S(2)}, u32[]{:S(2)}) collective-permute-start(bf16[128,128]{1,0:T(8,128)(2,1)S(1)} %copy-done.25), channel_id=1, source_target_pairs={{0,12},{4,8},{8,4},{12,0},{16,28},{20,24},{24,20},{28,16},{32,44},... | collective-permute-start | bytes 98312 | tf_op jit(solution)/shard_map/ppermute | solution.py:473
  55.7 15.4 %all-to-all-start.1 = ((bf16[16,64,128]{2,1,0:T(8,128)(2,1)}), bf16[16,64,128]{2,1,0:T(8,128)(2,1)S(1)}, u32[]{:S(2)}, u32[]{:S(2)}) async-start(bf16[16,64,128]{2,1,0:T(8,128)(2,1)} %get-tuple-element.41), calls=%async_computation.1 | async-start | bytes 524288 | tf_op jit(solution)/shard_map/all_to_all | solution.py:485
  77.0 6.9 %collective-permute-start.8 = (bf16[128,256]{1,0:T(8,128)(2,1)}, bf16[128,256]{1,0:T(8,128)(2,1)S(1)}, u32[]{:S(2)}, u32[]{:S(2)}) collective-permute-start(bf16[128,256]{1,0:T(8,128)(2,1)} %get-tuple-element.44), channel_id=1, source_target_pairs={{0,1},{1,2},{2,3},{3,0},{4,5},{5,6},{6,7},{7,4},{8,9},{9,10},{10,1... | collective-permute-start | bytes 196616 | tf_op jit(solution)/shard_map/ppermute | solution.py:422
  77.4 8.5 %collective-permute-start.9 = (bf16[128,256]{1,0:T(8,128)(2,1)}, bf16[128,256]{1,0:T(8,128)(2,1)S(1)}, u32[]{:S(2)}, u32[]{:S(2)}) collective-permute-start(bf16[128,256]{1,0:T(8,128)(2,1)} %get-tuple-element.45), channel_id=1, source_target_pairs={{0,2},{1,3},{2,0},{3,1},{4,6},{5,7},{6,4},{7,5},{8,10},{9,11},{10,... | collective-permute-start | bytes 196616 | tf_op jit(solution)/shard_map/ppermute | solution.py:422
  79.1 7.9 %collective-permute-start.10 = (bf16[128,256]{1,0:T(8,128)(2,1)}, bf16[128,256]{1,0:T(8,128)(2,1)S(1)}, u32[]{:S(2)}, u32[]{:S(2)}) collective-permute-start(bf16[128,256]{1,0:T(8,128)(2,1)} %get-tuple-element.46), channel_id=1, source_target_pairs={{0,3},{1,0},{2,1},{3,2},{4,7},{5,4},{6,5},{7,6},{8,11},{9,8},{10,9... | collective-permute-start | bytes 196616 | tf_op jit(solution)/shard_map/ppermute | solution.py:422
  88.8 5.0 %collective-permute-start.13 = (bf16[128,256]{1,0:T(8,128)(2,1)S(1)}, bf16[128,256]{1,0:T(8,128)(2,1)S(1)}, u32[]{:S(2)}, u32[]{:S(2)}) collective-permute-start(bf16[128,256]{1,0:T(8,128)(2,1)S(1)} %shard_map.198.c0_ref), channel_id=1, source_target_pairs={{0,3},{1,0},{2,1},{3,2},{4,7},{5,4},{6,5},{7,6},{8,11},{9,8},{10,9... | collective-permute-start | bytes 196616 | tf_op jit(solution)/shard_map/ppermute | solution.py:422
  89.8 6.3 %collective-permute-start.12 = (bf16[128,256]{1,0:T(8,128)(2,1)S(1)}, bf16[128,256]{1,0:T(8,128)(2,1)S(1)}, u32[]{:S(2)}, u32[]{:S(2)}) collective-permute-start(bf16[128,256]{1,0:T(8,128)(2,1)S(1)} %shard_map.198.c0_ref), channel_id=1, source_target_pairs={{0,2},{1,3},{2,0},{3,1},{4,6},{5,7},{6,4},{7,5},{8,10},{9,11},{10,... | collective-permute-start | bytes 196616 | tf_op jit(solution)/shard_map/ppermute | solution.py:422
  90.3 7.3 %collective-permute-start.11 = (bf16[128,256]{1,0:T(8,128)(2,1)S(1)}, bf16[128,256]{1,0:T(8,128)(2,1)S(1)}, u32[]{:S(2)}, u32[]{:S(2)}) collective-permute-start(bf16[128,256]{1,0:T(8,128)(2,1)S(1)} %shard_map.198.c0_ref), channel_id=1, source_target_pairs={{0,1},{1,2},{2,3},{3,0},{4,5},{5,6},{6,7},{7,4},{8,9},{9,10},{10,1... | collective-permute-start | bytes 196616 | tf_op jit(solution)/shard_map/ppermute | solution.py:422
  101.2 25.9 %all-to-all-start.2 = ((bf16[32,16,1024]{2,1,0:T(8,128)(2,1)}), bf16[32,16,1024]{2,1,0:T(8,128)(2,1)S(1)}, u32[]{:S(2)}, u32[]{:S(2)}) async-start(bf16[32,16,1024]{2,1,0:T(8,128)(2,1)} %bitcast.22), calls=%async_computation.2 | async-start | bytes 2097152 | tf_op jit(solution)/shard_map/all_to_all | solution.py:507
  110.2 26.1 %collective-permute-start.14 = (bf16[1,1024,512]{2,1,0:T(8,128)(2,1)}, bf16[1,1024,512]{2,1,0:T(8,128)(2,1)}, u32[]{:S(2)}, u32[]{:S(2)}) collective-permute-start(bf16[1,1024,512]{2,1,0:T(8,128)(2,1)} %u0_ref.1), channel_id=1, source_target_pairs={{0,1},{1,2},{2,3},{3,0},{4,5},{5,6},{6,7},{7,4},{8,9},{9,10},{10,1... | collective-permute-start | bytes 3145736 | tf_op jit(solution)/shard_map/ppermute | solution.py:422
  110.9 26.0 %collective-permute-start.15 = (bf16[1,1024,512]{2,1,0:T(8,128)(2,1)}, bf16[1,1024,512]{2,1,0:T(8,128)(2,1)S(1)}, u32[]{:S(2)}, u32[]{:S(2)}) collective-permute-start(bf16[1,1024,512]{2,1,0:T(8,128)(2,1)} %u0_ref.1), channel_id=1, source_target_pairs={{0,3},{1,0},{2,1},{3,2},{4,7},{5,4},{6,5},{7,6},{8,11},{9,8},{10,9... | collective-permute-start | bytes 3145736 | tf_op jit(solution)/shard_map/ppermute | solution.py:422
  132.2 20.9 %all-to-all-start.3 = ((bf16[32,16,1024]{2,1,0:T(8,128)(2,1)}), bf16[32,16,1024]{2,1,0:T(8,128)(2,1)S(1)}, u32[]{:S(2)}, u32[]{:S(2)}) async-start(bf16[32,16,1024]{2,1,0:T(8,128)(2,1)} %bitcast.23), calls=%async_computation.3 | async-start | bytes 2097152 | tf_op jit(solution)/shard_map/all_to_all | solution.py:527
  136.3 32.3 %collective-permute-start.18 = (bf16[1,1024,512]{2,1,0:T(8,128)(2,1)}, bf16[1,1024,512]{2,1,0:T(8,128)(2,1)}, u32[]{:S(2)}, u32[]{:S(2)}) collective-permute-start(bf16[1,1024,512]{2,1,0:T(8,128)(2,1)} %collective-permute-done.14.u1_ref), channel_id=1, source_target_pairs={{0,1},{1,2},{2,3},{3,0},{4,5},{5,6},{6,7},{7,4},{8,9},{9,10},{10,1... | collective-permute-start | bytes 3145736 | tf_op jit(solution)/shard_map/ppermute | solution.py:422
  140.1 28.6 %collective-permute-start.19 = (bf16[1,1024,512]{2,1,0:T(8,128)(2,1)}, bf16[1,1024,512]{2,1,0:T(8,128)(2,1)}, u32[]{:S(2)}, u32[]{:S(2)}) collective-permute-start(bf16[1,1024,512]{2,1,0:T(8,128)(2,1)} %shard_map.204), channel_id=1, source_target_pairs={{0,3},{1,0},{2,1},{3,2},{4,7},{5,4},{6,5},{7,6},{8,11},{9,8},{10,9... | collective-permute-start | bytes 3145736 | tf_op jit(solution)/shard_map/ppermute | solution.py:422
  153.2 10.3 %collective-permute-start.16 = (bf16[256,1024]{1,0:T(8,128)(2,1)S(1)}, bf16[256,1024]{1,0:T(8,128)(2,1)S(1)}, u32[]{:S(2)}, u32[]{:S(2)}) collective-permute-start(bf16[256,1024]{1,0:T(8,128)(2,1)S(1)} %bitcast.25), channel_id=1, source_target_pairs={{0,4},{4,0},{8,12},{12,8},{16,20},{20,16},{24,28},{28,24},{32,36},... | collective-permute-start | bytes 1572872 | tf_op jit(solution)/shard_map/ppermute | solution.py:529
  153.4 10.1 %collective-permute-start.17 = (bf16[256,1024]{1,0:T(8,128)(2,1)S(1)}, bf16[256,1024]{1,0:T(8,128)(2,1)S(1)}, u32[]{:S(2)}, u32[]{:S(2)}) collective-permute-start(bf16[256,1024]{1,0:T(8,128)(2,1)S(1)} %bitcast.24), channel_id=1, source_target_pairs={{0,4},{4,0},{8,12},{12,8},{16,20},{20,16},{24,28},{28,24},{32,36},... | collective-permute-start | bytes 1572872 | tf_op jit(solution)/shard_map/ppermute | solution.py:529
  171.4 2.7 %collective-permute-start.20 = (bf16[512,1024]{1,0:T(8,128)(2,1)S(1)}, bf16[512,1024]{1,0:T(8,128)(2,1)S(1)}, u32[]{:S(2)}, u32[]{:S(2)}) collective-permute-start(bf16[512,1024]{1,0:T(8,128)(2,1)S(1)} %get-tuple-element.63), channel_id=1, source_target_pairs={{0,4},{4,0},{8,12},{12,8},{16,20},{20,16},{24,28},{28,24},{32,36},... | collective-permute-start | bytes 3145736 | tf_op jit(solution)/shard_map/ppermute | solution.py:533
  174.3 21.3 %copy-start.5 = (f32[160,1024]{1,0:T(8,128)S(1)}, f32[160,1024]{1,0:T(8,128)}, u32[]{:S(2)}) copy-start(f32[160,1024]{1,0:T(8,128)} %get-tuple-element.65.sum_ref) | copy-start | bytes 1966084
  174.4 21.2 %copy-start.9 = (s32[160,2]{1,0:T(8,128)S(1)}, s32[160,2]{1,0:T(8,128)}, u32[]{:S(2)}) copy-start(s32[160,2]{1,0:T(8,128)} %get-tuple-element.64.didx_ref) | copy-start | bytes 3844
  174.4 21.2 %copy-start.13 = (f32[160,2]{0,1:T(2,128)S(1)}, f32[160,2]{0,1:T(2,128)}, u32[]{:S(2)}) copy-start(f32[160,2]{0,1:T(2,128)} %param.34) | copy-start | bytes 3844
  (23 other events, 120.0 us)
Sparse Core Ops, SparseCore 0:
  9.7 40.9 all-gather.2
  52.3 56.2 all-gather.4

commit v7 on v6

--- a/solution.py
+++ b/solution.py
@@ -490,7 +490,7 @@
         att, x, norm2_gain.reshape(1, D), wo, mlp_in, mlp_out, dr, dl
     )
     parts = [parts[0]] + [turn(parts[k], k) for k in (1, 2, 3)]
-    piece = call(coarse_kernel, sds((ROWS, 256), BF), *parts, mixed, limit=8)
+    piece = call(coarse_kernel, sds((ROWS, 256), BF), *parts, mixed)
     pieces = [piece] + [turn(piece, k) for k in (1, 2, 3)]
     coarse_new, served = call(
         serve_kernel,
@@ -517,7 +517,7 @@
         norm3_gain.reshape(1, D),
         didxt,
         ready=(token,),
-        limit=56,
+        limit=52,
         far=(1,),
         scratch_shapes=[
             pltpu.VMEM((EXPERTS * SLOTS, D), BF),

time: 205 us -> 205 us (level)
    unnamed x56 -> x68, local copies, waits for them, and re-layouts: 11 us -> 10.2 us
where the time goes in v7:
time: 205 us; the launch traced here: 204 us
  waiting for transfers between devices  58.1 us (28%)
  starting transfers between devices  51 us (25%)
  Pallas kernels  49.3 us (24%)
  blocking collectives  21.3 us (10%)
  between operations  14.4 us (7%)
  local copies, waits for them, and re-layouts  10.3 us (5%)
    all_to_all x1, blocking collectives, per_device(): returned = lax.all_to_all(result, 'seq', 0, 0, tiled=True)  21.3 us
    ppermute x15, waiting for transfers between devices, turn(): return lax.ppermute(v, 'exp', [(i, (i + k) % N_EXP) for i in range(N_EXP)])  20.2 us
    ppermute x15, starting transfers between devices, turn(): return lax.ppermute(v, 'exp', [(i, (i + k) % N_EXP) for i in range(N_EXP)])  19.9 us
    pallas_call x8, Pallas kernels, call(): pl.pallas_call(kernel, out_shape=out_shape, in_specs=space + [pl.BlockSpe...  19.8 us
    ppermute x3, waiting for transfers between devices, per_device(): lax.ppermute(qs[k], 'seq', [(i, i ^ k) for i in range(N_SEQ)])  11.1 us
    all_to_all x1, waiting for transfers between devices, per_device(): mine = lax.all_to_all(outgoing, 'seq', 0, 0, tiled=True)  10.5 us
    unnamed x68, local copies, waits for them, and re-layouts  10.2 us
    all_to_all x1, starting transfers between devices, per_device(): kv = lax.all_to_all(kv, 'seq', 0, 0, tiled=True)  10.2 us
  transfers between devices with their start and end apart: 27, of which 15 were waited for; matrix products, arithmetic and copies ran while one was open for 0% of the time, Pallas kernels for 22%

profile of v7, /device:TPU:1, one launch (start us, length us, event | category | flops | bytes accessed | tf_op | source)
XLA Modules:
  0.0 204.4 jit_solution(12304973222369134058)
XLA Ops:
  8.6 3.8 %collective-permute-start.1 = (bf16[128,256]{1,0:T(8,128)(2,1)}, bf16[128,256]{1,0:T(8,128)(2,1)S(1)}, u32[]{:S(2)}, u32[]{:S(2)}) collective-permute-start(bf16[128,256]{1,0:T(8,128)(2,1)} %f0_ref.1), channel_id=1, source_target_pairs={{0,2},{1,3},{2,0},{3,1},{4,6},{5,7},{6,4},{7,5},{8,10},{9,11},{10,... | collective-permute-start | bytes 196616 | tf_op jit(solution)/shard_map/ppermute | solution.py:422
  12.9 2.3 %collective-permute-start.2 = (bf16[128,256]{1,0:T(8,128)(2,1)}, bf16[128,256]{1,0:T(8,128)(2,1)S(1)}, u32[]{:S(2)}, u32[]{:S(2)}) collective-permute-start(bf16[128,256]{1,0:T(8,128)(2,1)} %f0_ref.1), channel_id=1, source_target_pairs={{0,3},{1,0},{2,1},{3,2},{4,7},{5,4},{6,5},{7,6},{8,11},{9,8},{10,9... | collective-permute-start | bytes 196616 | tf_op jit(solution)/shard_map/ppermute | solution.py:422
  17.7 4.2 %shard_map.195 = (bf16[128,1024]{1,0:T(8,128)(2,1)}, bf16[128,128]{1,0:T(8,128)(2,1)}, bf16[128,128]{1,0:T(8,128)(2,1)}, bf16[128,128]{1,0:T(8,128)(2,1)}, bf16[...) custom-call(bf16[128,256]{1,0:T(8,128)(2,1)} %f0_ref.1, bf16[128,256]{1,0:T(8,128)(2,1)} %copy-done.23, ...), custom_call_target="tpu_custom_call" | custom-call | bytes 1 | tf_op jit(solution)/shard_map/pallas_call | solution.py:41
  21.9 10.2 %all-to-all-start = ((bf16[32,144,128]{2,1,0:T(8,128)(2,1)}), bf16[32,144,128]{2,1,0:T(8,128)(2,1)S(1)}, u32[]{:S(2)}, u32[]{:S(2)}) async-start(bf16[32,144,128]{2,1,0:T(8,128)(2,1)} %get-tuple-element.39), calls=%async_computation | async-start | bytes 2359296 | tf_op jit(solution)/shard_map/all_to_all | solution.py:475
  32.2 3.0 %collective-permute-start.7 = (bf16[1,1024,512]{2,1,0:T(8,128)(2,1)S(1)}, bf16[1,1024,512]{2,1,0:T(8,128)(2,1)S(1)}, u32[]{:S(2)}, u32[]{:S(2)}) collective-permute-start(bf16[1,1024,512]{2,1,0:T(8,128)(2,1)S(1)} %copy-done.21), channel_id=1, source_target_pairs={{0,3},{1,0},{2,1},{3,2},{4,7},{5,4},{6,5},{7,6},{8,11},{9,8},{10,9... | collective-permute-start | bytes 3145736 | tf_op jit(solution)/shard_map/ppermute | solution.py:422
  37.5 6.6 %collective-permute-done.4.q2_ref = bf16[128,128]{1,0:T(8,128)(2,1)S(1)} collective-permute-done((bf16[128,128]{1,0:T(8,128)(2,1)S(1)}, bf16[128,128]{1,0:T(8,128)(2,1)S(1)}, u32[]{:S(2)}, u32[]{:S(2)}) %collective-permute-start.4) | collective-permute-done | bytes 32800 | tf_op jit(solution)/shard_map/ppermute | solution.py:473
  44.1 4.5 %collective-permute-done.5.q3_ref = bf16[128,128]{1,0:T(8,128)(2,1)S(1)} collective-permute-done((bf16[128,128]{1,0:T(8,128)(2,1)S(1)}, bf16[128,128]{1,0:T(8,128)(2,1)S(1)}, u32[]{:S(2)}, u32[]{:S(2)}) %collective-permute-start.5) | collective-permute-done | bytes 32800 | tf_op jit(solution)/shard_map/ppermute | solution.py:473
  50.5 4.6 %shard_map.196 = (bf16[16,64,128]{2,1,0:T(8,128)(2,1)}, bf16[512,128]{1,0:T(8,128)(2,1)S(1)}) custom-call(f32[4]{0:T(128)S(1)} %copy-done.17, bf16[128,128]{1,0:T(8,128)(2,1)S(1)} %copy-done.11, bf16[128,128]{1,0:T(8,128)(2,1)S(1)} %collective-permute-done.3.q1_ref, bf16[128,128]{1,0:T(8,128)(2,1)S(1)} %collective-permute-done.4.q2_ref, ...), custom_call_target="tpu_custom_call" | custom-call | bytes 1 | tf_op jit(solution)/shard_map/pallas_call | solution.py:41
  55.7 4.8 %all-to-all-start.1 = ((bf16[16,64,128]{2,1,0:T(8,128)(2,1)}), bf16[16,64,128]{2,1,0:T(8,128)(2,1)S(1)}, u32[]{:S(2)}, u32[]{:S(2)}) async-start(bf16[16,64,128]{2,1,0:T(8,128)(2,1)} %get-tuple-element.41), calls=%async_computation.1 | async-start | bytes 524288 | tf_op jit(solution)/shard_map/all_to_all | solution.py:485
  60.5 5.6 %collective-permute-done.6.rest_0_.d1_ref = bf16[1,1024,512]{2,1,0:T(8,128)(2,1)} collective-permute-done((bf16[1,1024,512]{2,1,0:T(8,128)(2,1)S(1)}, bf16[1,1024,512]{2,1,0:T(8,128)(2,1)}, u32[]{:S(2)}, u32[]{:S(2)}) %collective-permute-start.6) | collective-permute-done | bytes 1048608 | tf_op jit(solution)/shard_map/ppermute | solution.py:422
  66.1 5.0 %all-to-all-done.1.att_ref = bf16[16,64,128]{2,1,0:T(8,128)(2,1)S(1)} async-done(((bf16[16,64,128]{2,1,0:T(8,128)(2,1)}), bf16[16,64,128]{2,1,0:T(8,128)(2,1)S(1)}, u32[]{:S(2)}, u32[]{:S(2)}) %all-to-all-start.1) | async-done | bytes 262176 | tf_op jit(solution)/shard_map/all_to_all | solution.py:485
  71.8 5.1 %shard_map.197 = (f32[128,256]{1,0:T(8,128)}, bf16[128,256]{1,0:T(8,128)(2,1)}, bf16[128,256]{1,0:T(8,128)(2,1)}, bf16[128,256]{1,0:T(8,128)(2,1)}, bf16[128,256]{1,0:T(8,128)(2,1)}) custom-call(bf16[16,64,128]{2,1,0:T(8,128)(2,1)} %copy-done.20, bf16[128,1024]{1,0:T(8,128)(2,1)} %get-tuple-element.42.x_ref, f32[1,1024]{1,0:T(1,128)} %bitcast.29, ...), custom_call_target="tpu_custom_call" | custom-call | flops 1 | bytes 1 | tf_op jit(solution)/shard_map/pallas_call | solution.py:184
  79.9 3.9 %collective-permute-done.8.p1_ref = bf16[128,256]{1,0:T(8,128)(2,1)S(1)} collective-permute-done((bf16[128,256]{1,0:T(8,128)(2,1)}, bf16[128,256]{1,0:T(8,128)(2,1)S(1)}, u32[]{:S(2)}, u32[]{:S(2)}) %collective-permute-start.8) | collective-permute-done | bytes 65568 | tf_op jit(solution)/shard_map/ppermute | solution.py:422
  83.8 2.1 %collective-permute-done.9.p2_ref = bf16[128,256]{1,0:T(8,128)(2,1)S(1)} collective-permute-done((bf16[128,256]{1,0:T(8,128)(2,1)}, bf16[128,256]{1,0:T(8,128)(2,1)S(1)}, u32[]{:S(2)}, u32[]{:S(2)}) %collective-permute-start.9) | collective-permute-done | bytes 65568 | tf_op jit(solution)/shard_map/ppermute | solution.py:422
  91.1 3.3 %collective-permute-done.13.c3_ref = bf16[128,256]{1,0:T(8,128)(2,1)S(1)} collective-permute-done((bf16[128,256]{1,0:T(8,128)(2,1)}, bf16[128,256]{1,0:T(8,128)(2,1)S(1)}, u32[]{:S(2)}, u32[]{:S(2)}) %collective-permute-start.13) | collective-permute-done | bytes 65568 | tf_op jit(solution)/shard_map/ppermute | solution.py:422
  94.4 2.4 %collective-permute-done.12.c2_ref = bf16[128,256]{1,0:T(8,128)(2,1)S(1)} collective-permute-done((bf16[128,256]{1,0:T(8,128)(2,1)}, bf16[128,256]{1,0:T(8,128)(2,1)S(1)}, u32[]{:S(2)}, u32[]{:S(2)}) %collective-permute-start.12) | collective-permute-done | bytes 65568 | tf_op jit(solution)/shard_map/ppermute | solution.py:422
  98.9 3.0 %shard_map.199 = (bf16[128,1024]{1,0:T(8,128)(2,1)}, bf16[512,1024]{1,0:T(8,128)(2,1)}) custom-call(bf16[512,128]{1,0:T(8,128)(2,1)} %copy-done.8, bf16[128,256]{1,0:T(8,128)(2,1)} %shard_map.198.c0_ref, bf16[128,256]{1,0:T(8,128)(2,1)} %copy-done.30, bf16[128,256]{1,0:T(8,128)(2,1)} %copy-done.29, bf16[128,256]{1,0:T(8,128)(2,1)} %copy-done.28), custom_call_target="tpu_custom_call" | custom-call | bytes 1 | tf_op jit(solution)/shard_map/pallas_call | solution.py:41
  101.9 9.0 %all-to-all-start.2 = ((bf16[32,16,1024]{2,1,0:T(8,128)(2,1)}), bf16[32,16,1024]{2,1,0:T(8,128)(2,1)S(1)}, u32[]{:S(2)}, u32[]{:S(2)}) async-start(bf16[32,16,1024]{2,1,0:T(8,128)(2,1)} %bitcast.24), calls=%async_computation.2 | async-start | bytes 2097152 | tf_op jit(solution)/shard_map/all_to_all | solution.py:507
  111.7 2.1 %collective-permute-start.15 = (bf16[1,1024,512]{2,1,0:T(8,128)(2,1)}, bf16[1,1024,512]{2,1,0:T(8,128)(2,1)S(1)}, u32[]{:S(2)}, u32[]{:S(2)}) collective-permute-start(bf16[1,1024,512]{2,1,0:T(8,128)(2,1)} %u0_ref.1), channel_id=1, source_target_pairs={{0,3},{1,0},{2,1},{3,2},{4,7},{5,4},{6,5},{7,6},{8,11},{9,8},{10,9... | collective-permute-start | bytes 3145736 | tf_op jit(solution)/shard_map/ppermute | solution.py:422
  113.7 6.8 %shard_map.200 = (bf16[4,1024,512]{2,1,0:T(8,128)(2,1)}, bf16[1024,512]{1,0:T(8,128)(2,1)}, bf16[3,1024,512]{2,1,0:T(8,128)(2,1)}, f32[8,128]{1,0:T(8,128)S(1)}) custom-call(bf16[4,1024,512]{2,1,0:T(8,128)(2,1)} %all-gather.5.cloned.1.call-done.gate_ref, bf16[1,1024,512]{2,1,0:T(8,128)(2,1)} %u0_ref.1, bf16[1,1024,512]{2,1,0:T(8,128)(2,1)} %d0_ref.1, ...), custom_call_target="tpu_custom_call" | custom-call | flops 1 | bytes 1 | tf_op jit(solution)/shard_map/pallas_call | solution.py:274
  120.5 7.3 %all-to-all-done.2 = bf16[32,16,1024]{2,1,0:T(8,128)(2,1)S(1)} async-done(((bf16[32,16,1024]{2,1,0:T(8,128)(2,1)}), bf16[32,16,1024]{2,1,0:T(8,128)(2,1)S(1)}, u32[]{:S(2)}, u32[]{:S(2)}) %all-to-all-start.2) | async-done | bytes 1048608 | tf_op jit(solution)/shard_map/all_to_all | solution.py:507
  128.9 3.0 %shard_map.201 = (f32[160,1024]{1,0:T(8,128)S(1)}, bf16[512,1024]{1,0:T(8,128)(2,1)}) custom-call(bf16[512,1024]{1,0:T(8,128)(2,1)} %bitcast.23, s32[160,1]{1,0:T(8,128)S(1)} %copy-done.10, bf16[160,1024]{1,0:T(8,128)(2,1)S(1)} %copy-done.7, s32[1,160]{1,0:T(1,128)S(1)} %bitcast.22, bf16[8,1024]{1,0:T(8,128)(2,1)S(1)} %copy-done.12, f32[1,1024]{1,0:T(1,128)S(1)} %bitcast.20, ...), custom_call_target="tpu_custom_call" | custom-call | bytes 1 | tf_op jit(solution)/shard_map/pallas_call | solution.py:41
  132.7 4.0 %all-to-all-start.3 = ((bf16[32,16,1024]{2,1,0:T(8,128)(2,1)}), bf16[32,16,1024]{2,1,0:T(8,128)(2,1)S(1)}, u32[]{:S(2)}, u32[]{:S(2)}) async-start(bf16[32,16,1024]{2,1,0:T(8,128)(2,1)} %bitcast.25), calls=%async_computation.3 | async-start | bytes 2097152 | tf_op jit(solution)/shard_map/all_to_all | solution.py:527
  138.4 2.2 %shard_map.204 = bf16[1,1024,512]{2,1,0:T(8,128)(2,1)} custom-call(bf16[1,1024,512]{2,1,0:T(8,128)(2,1)} %copy-done.18, bf16[1,1024,512]{2,1,0:T(8,128)(2,1)} %copy-done.2), custom_call_target="tpu_custom_call" | custom-call | flops 1 | bytes 1 | tf_op jit(solution)/shard_map/pallas_call | solution.py:297
  140.6 2.5 %collective-permute-start.19 = (bf16[1,1024,512]{2,1,0:T(8,128)(2,1)}, bf16[1,1024,512]{2,1,0:T(8,128)(2,1)}, u32[]{:S(2)}, u32[]{:S(2)}) collective-permute-start(bf16[1,1024,512]{2,1,0:T(8,128)(2,1)} %shard_map.204), channel_id=1, source_target_pairs={{0,3},{1,0},{2,1},{3,2},{4,7},{5,4},{6,5},{7,6},{8,11},{9,8},{10,9... | collective-permute-start | bytes 3145736 | tf_op jit(solution)/shard_map/ppermute | solution.py:422
  143.1 10.5 %all-to-all-done.3 = bf16[32,16,1024]{2,1,0:T(8,128)(2,1)S(1)} async-done(((bf16[32,16,1024]{2,1,0:T(8,128)(2,1)}), bf16[32,16,1024]{2,1,0:T(8,128)(2,1)S(1)}, u32[]{:S(2)}, u32[]{:S(2)}) %all-to-all-start.3) | async-done | bytes 1048608 | tf_op jit(solution)/shard_map/all_to_all | solution.py:527
  154.3 2.2 %copy-done = bf16[4,1024,512]{2,1,0:T(8,128)(2,1)S(1)} copy-done((bf16[4,1024,512]{2,1,0:T(8,128)(2,1)S(1)}, bf16[4,1024,512]{2,1,0:T(8,128)(2,1)}, u32[]{:S(2)}) %copy-start) | copy-done | bytes 4194328
  156.5 1.9 copy-done.1
  158.4 5.6 %shard_map.202 = (f32[512,1024]{1,0:T(8,128)S(1)}, bf16[2,1024,512]{2,1,0:T(8,128)(2,1)S(1)}) custom-call(bf16[512,1024]{1,0:T(8,128)(2,1)S(1)} %bitcast.16, bf16[4,1024,512]{2,1,0:T(8,128)(2,1)S(1)} %copy-done, bf16[1024,512]{1,0:T(8,128)(2,1)S(1)} %copy-done.4, bf16[3,1024,512]{2,1,0:T(8,128)(2,1)S(1)} %copy-done.1, ...), custom_call_target="tpu_custom_call" | custom-call | flops 1 | bytes 1 | tf_op jit(solution)/shard_map/pallas_call | solution.py:331
  164.0 5.2 %shard_map.203 = (f32[512,1024]{1,0:T(8,128)S(1)}, bf16[512,1024]{1,0:T(8,128)(2,1)S(1)}) custom-call(bf16[256,1024]{1,0:T(8,128)(2,1)S(1)} %collective-permute-done.16.x0_ref, bf16[256,1024]{1,0:T(8,128)(2,1)S(1)} %collective-permute-done.17.x1_ref, bf16[4,1024,512]{2,1,0:T(8,128)(2,1)S(1)} %copy-done, bf16[1024,512]{1,0:T(8,128)(2,1)S(1)} %copy-done.4, ...), custom_call_target="tpu_custom_call" | custom-call | flops 1 | bytes 1 | tf_op jit(solution)/shard_map/pallas_call | solution.py:353
  169.2 2.7 %shard_map.205 = (bf16[512,1024]{1,0:T(8,128)(2,1)S(1)}, bf16[1024,512]{1,0:T(8,128)(2,1)S(1)}, bf16[1024,512]{1,0:T(8,128)(2,1)S(1)}) custom-call(bf16[512,1024]{1,0:T(8,128)(2,1)S(1)} %get-tuple-element.59.x_ref, f32[512,1024]{1,0:T(8,128)S(1)} %get-tuple-element.60.acc_ref, bf16[4,1024,512]{2,1,0:T(8,128)(2,1)S(1)} %copy-done, ...), custom_call_target="tpu_custom_call" | custom-call | flops 1 | bytes 1 | tf_op jit(solution)/shard_map/pallas_call | solution.py:381
  174.9 21.3 %all_to_all.43 = bf16[32,16,1024]{2,1,0:T(8,128)(2,1)S(1)} all-to-all(bf16[32,16,1024]{2,1,0:T(8,128)(2,1)S(1)} %bitcast.19), channel_id=1, replica_groups=mesh['seq'=32,'exp'=4] {'seq'}, dimensions={0} | all-to-all | bytes 2097152 | tf_op jit(solution)/shard_map/all_to_all | solution.py:536
  (109 shorter events, 29.3 us)
Async XLA Ops:
  7.2 63.9 %all-gather.3.cloned.1.call-start = ((), (), s32[]{:S(2)}) async-start(), calls=%async_computation.5 | async-start | bytes 2621440 | tf_op jit(solution)/shard_map/all_gather | solution.py:447
  7.9 105.8 %all-gather.5.cloned.1.call-start = ((), (), s32[]{:S(2)}) async-start(), calls=%async_computation.6 | async-start | bytes 5242880 | tf_op jit(solution)/shard_map/all_gather | solution.py:448
  8.6 8.3 %collective-permute-start.1 = (bf16[128,256]{1,0:T(8,128)(2,1)}, bf16[128,256]{1,0:T(8,128)(2,1)S(1)}, u32[]{:S(2)}, u32[]{:S(2)}) collective-permute-start(bf16[128,256]{1,0:T(8,128)(2,1)} %f0_ref.1), channel_id=1, source_target_pairs={{0,2},{1,3},{2,0},{3,1},{4,6},{5,7},{6,4},{7,5},{8,10},{9,11},{10,... | collective-permute-start | bytes 196616 | tf_op jit(solution)/shard_map/ppermute | solution.py:422
  12.5 4.5 %collective-permute-start = (bf16[128,256]{1,0:T(8,128)(2,1)}, bf16[128,256]{1,0:T(8,128)(2,1)S(1)}, u32[]{:S(2)}, u32[]{:S(2)}) collective-permute-start(bf16[128,256]{1,0:T(8,128)(2,1)} %f0_ref.1), channel_id=1, source_target_pairs={{0,1},{1,2},{2,3},{3,0},{4,5},{5,6},{6,7},{7,4},{8,9},{9,10},{10,1... | collective-permute-start | bytes 196616 | tf_op jit(solution)/shard_map/ppermute | solution.py:422
  12.9 4.1 %collective-permute-start.2 = (bf16[128,256]{1,0:T(8,128)(2,1)}, bf16[128,256]{1,0:T(8,128)(2,1)S(1)}, u32[]{:S(2)}, u32[]{:S(2)}) collective-permute-start(bf16[128,256]{1,0:T(8,128)(2,1)} %f0_ref.1), channel_id=1, source_target_pairs={{0,3},{1,0},{2,1},{3,2},{4,7},{5,4},{6,5},{7,6},{8,11},{9,8},{10,9... | collective-permute-start | bytes 196616 | tf_op jit(solution)/shard_map/ppermute | solution.py:422
  17.7 32.8 %copy-start.17 = (f32[4]{0:T(128)S(1)}, f32[4]{0:T(128)}, u32[]{:S(2)}) copy-start(f32[4]{0:T(128)} %scale_ref.1) | copy-start | bytes 52
  21.9 28.6 %copy-start.11 = (bf16[128,128]{1,0:T(8,128)(2,1)S(1)}, bf16[128,128]{1,0:T(8,128)(2,1)}, u32[]{:S(2)}) copy-start(bf16[128,128]{1,0:T(8,128)(2,1)} %get-tuple-element.35.q0_ref) | copy-start | bytes 98308
  21.9 28.6 %all-to-all-start = ((bf16[32,144,128]{2,1,0:T(8,128)(2,1)}), bf16[32,144,128]{2,1,0:T(8,128)(2,1)S(1)}, u32[]{:S(2)}, u32[]{:S(2)}) async-start(bf16[32,144,128]{2,1,0:T(8,128)(2,1)} %get-tuple-element.39), calls=%async_computation | async-start | bytes 2359296 | tf_op jit(solution)/shard_map/all_to_all | solution.py:475
  32.1 34.0 %collective-permute-start.6 = (bf16[1,1024,512]{2,1,0:T(8,128)(2,1)S(1)}, bf16[1,1024,512]{2,1,0:T(8,128)(2,1)}, u32[]{:S(2)}, u32[]{:S(2)}) collective-permute-start(bf16[1,1024,512]{2,1,0:T(8,128)(2,1)S(1)} %copy-done.21), channel_id=1, source_target_pairs={{0,1},{1,2},{2,3},{3,0},{4,5},{5,6},{6,7},{7,4},{8,9},{9,10},{10,1... | collective-permute-start | bytes 3145736 | tf_op jit(solution)/shard_map/ppermute | solution.py:422
  32.2 33.9 %collective-permute-start.7 = (bf16[1,1024,512]{2,1,0:T(8,128)(2,1)S(1)}, bf16[1,1024,512]{2,1,0:T(8,128)(2,1)S(1)}, u32[]{:S(2)}, u32[]{:S(2)}) collective-permute-start(bf16[1,1024,512]{2,1,0:T(8,128)(2,1)S(1)} %copy-done.21), channel_id=1, source_target_pairs={{0,3},{1,0},{2,1},{3,2},{4,7},{5,4},{6,5},{7,6},{8,11},{9,8},{10,9... | collective-permute-start | bytes 3145736 | tf_op jit(solution)/shard_map/ppermute | solution.py:422
  35.3 2.2 %collective-permute-start.3 = (bf16[128,128]{1,0:T(8,128)(2,1)S(1)}, bf16[128,128]{1,0:T(8,128)(2,1)S(1)}, u32[]{:S(2)}, u32[]{:S(2)}) collective-permute-start(bf16[128,128]{1,0:T(8,128)(2,1)S(1)} %copy-done.33), channel_id=1, source_target_pairs={{0,4},{4,0},{8,12},{12,8},{16,20},{20,16},{24,28},{28,24},{32,36},... | collective-permute-start | bytes 98312 | tf_op jit(solution)/shard_map/ppermute | solution.py:473
  35.8 8.3 %collective-permute-start.4 = (bf16[128,128]{1,0:T(8,128)(2,1)S(1)}, bf16[128,128]{1,0:T(8,128)(2,1)S(1)}, u32[]{:S(2)}, u32[]{:S(2)}) collective-permute-start(bf16[128,128]{1,0:T(8,128)(2,1)S(1)} %copy-done.32), channel_id=1, source_target_pairs={{0,8},{4,12},{8,0},{12,4},{16,24},{20,28},{24,16},{28,20},{32,40},... | collective-permute-start | bytes 98312 | tf_op jit(solution)/shard_map/ppermute | solution.py:473
  37.3 11.3 %collective-permute-start.5 = (bf16[128,128]{1,0:T(8,128)(2,1)S(1)}, bf16[128,128]{1,0:T(8,128)(2,1)S(1)}, u32[]{:S(2)}, u32[]{:S(2)}) collective-permute-start(bf16[128,128]{1,0:T(8,128)(2,1)S(1)} %copy-done.31), channel_id=1, source_target_pairs={{0,12},{4,8},{8,4},{12,0},{16,28},{20,24},{24,20},{28,16},{32,44},... | collective-permute-start | bytes 98312 | tf_op jit(solution)/shard_map/ppermute | solution.py:473
  55.7 15.4 %all-to-all-start.1 = ((bf16[16,64,128]{2,1,0:T(8,128)(2,1)}), bf16[16,64,128]{2,1,0:T(8,128)(2,1)S(1)}, u32[]{:S(2)}, u32[]{:S(2)}) async-start(bf16[16,64,128]{2,1,0:T(8,128)(2,1)} %get-tuple-element.41), calls=%async_computation.1 | async-start | bytes 524288 | tf_op jit(solution)/shard_map/all_to_all | solution.py:485
  76.9 6.9 %collective-permute-start.8 = (bf16[128,256]{1,0:T(8,128)(2,1)}, bf16[128,256]{1,0:T(8,128)(2,1)S(1)}, u32[]{:S(2)}, u32[]{:S(2)}) collective-permute-start(bf16[128,256]{1,0:T(8,128)(2,1)} %get-tuple-element.44), channel_id=1, source_target_pairs={{0,1},{1,2},{2,3},{3,0},{4,5},{5,6},{6,7},{7,4},{8,9},{9,10},{10,1... | collective-permute-start | bytes 196616 | tf_op jit(solution)/shard_map/ppermute | solution.py:422
  77.4 8.5 %collective-permute-start.9 = (bf16[128,256]{1,0:T(8,128)(2,1)}, bf16[128,256]{1,0:T(8,128)(2,1)S(1)}, u32[]{:S(2)}, u32[]{:S(2)}) collective-permute-start(bf16[128,256]{1,0:T(8,128)(2,1)} %get-tuple-element.45), channel_id=1, source_target_pairs={{0,2},{1,3},{2,0},{3,1},{4,6},{5,7},{6,4},{7,5},{8,10},{9,11},{10,... | collective-permute-start | bytes 196616 | tf_op jit(solution)/shard_map/ppermute | solution.py:422
  79.1 7.8 %collective-permute-start.10 = (bf16[128,256]{1,0:T(8,128)(2,1)}, bf16[128,256]{1,0:T(8,128)(2,1)S(1)}, u32[]{:S(2)}, u32[]{:S(2)}) collective-permute-start(bf16[128,256]{1,0:T(8,128)(2,1)} %get-tuple-element.46), channel_id=1, source_target_pairs={{0,3},{1,0},{2,1},{3,2},{4,7},{5,4},{6,5},{7,6},{8,11},{9,8},{10,9... | collective-permute-start | bytes 196616 | tf_op jit(solution)/shard_map/ppermute | solution.py:422
  89.3 5.1 %collective-permute-start.13 = (bf16[128,256]{1,0:T(8,128)(2,1)}, bf16[128,256]{1,0:T(8,128)(2,1)S(1)}, u32[]{:S(2)}, u32[]{:S(2)}) collective-permute-start(bf16[128,256]{1,0:T(8,128)(2,1)} %shard_map.198.c0_ref), channel_id=1, source_target_pairs={{0,3},{1,0},{2,1},{3,2},{4,7},{5,4},{6,5},{7,6},{8,11},{9,8},{10,9... | collective-permute-start | bytes 196616 | tf_op jit(solution)/shard_map/ppermute | solution.py:422
  90.2 6.6 %collective-permute-start.12 = (bf16[128,256]{1,0:T(8,128)(2,1)}, bf16[128,256]{1,0:T(8,128)(2,1)S(1)}, u32[]{:S(2)}, u32[]{:S(2)}) collective-permute-start(bf16[128,256]{1,0:T(8,128)(2,1)} %shard_map.198.c0_ref), channel_id=1, source_target_pairs={{0,2},{1,3},{2,0},{3,1},{4,6},{5,7},{6,4},{7,5},{8,10},{9,11},{10,... | collective-permute-start | bytes 196616 | tf_op jit(solution)/shard_map/ppermute | solution.py:422
  90.8 7.5 %collective-permute-start.11 = (bf16[128,256]{1,0:T(8,128)(2,1)}, bf16[128,256]{1,0:T(8,128)(2,1)S(1)}, u32[]{:S(2)}, u32[]{:S(2)}) collective-permute-start(bf16[128,256]{1,0:T(8,128)(2,1)} %shard_map.198.c0_ref), channel_id=1, source_target_pairs={{0,1},{1,2},{2,3},{3,0},{4,5},{5,6},{6,7},{7,4},{8,9},{9,10},{10,1... | collective-permute-start | bytes 196616 | tf_op jit(solution)/shard_map/ppermute | solution.py:422
  101.9 26.0 %all-to-all-start.2 = ((bf16[32,16,1024]{2,1,0:T(8,128)(2,1)}), bf16[32,16,1024]{2,1,0:T(8,128)(2,1)S(1)}, u32[]{:S(2)}, u32[]{:S(2)}) async-start(bf16[32,16,1024]{2,1,0:T(8,128)(2,1)} %bitcast.24), calls=%async_computation.2 | async-start | bytes 2097152 | tf_op jit(solution)/shard_map/all_to_all | solution.py:507
  111.0 26.1 %collective-permute-start.14 = (bf16[1,1024,512]{2,1,0:T(8,128)(2,1)}, bf16[1,1024,512]{2,1,0:T(8,128)(2,1)}, u32[]{:S(2)}, u32[]{:S(2)}) collective-permute-start(bf16[1,1024,512]{2,1,0:T(8,128)(2,1)} %u0_ref.1), channel_id=1, source_target_pairs={{0,1},{1,2},{2,3},{3,0},{4,5},{5,6},{6,7},{7,4},{8,9},{9,10},{10,1... | collective-permute-start | bytes 3145736 | tf_op jit(solution)/shard_map/ppermute | solution.py:422
  111.7 25.7 %collective-permute-start.15 = (bf16[1,1024,512]{2,1,0:T(8,128)(2,1)}, bf16[1,1024,512]{2,1,0:T(8,128)(2,1)S(1)}, u32[]{:S(2)}, u32[]{:S(2)}) collective-permute-start(bf16[1,1024,512]{2,1,0:T(8,128)(2,1)} %u0_ref.1), channel_id=1, source_target_pairs={{0,3},{1,0},{2,1},{3,2},{4,7},{5,4},{6,5},{7,6},{8,11},{9,8},{10,9... | collective-permute-start | bytes 3145736 | tf_op jit(solution)/shard_map/ppermute | solution.py:422
  132.7 20.9 %all-to-all-start.3 = ((bf16[32,16,1024]{2,1,0:T(8,128)(2,1)}), bf16[32,16,1024]{2,1,0:T(8,128)(2,1)S(1)}, u32[]{:S(2)}, u32[]{:S(2)}) async-start(bf16[32,16,1024]{2,1,0:T(8,128)(2,1)} %bitcast.25), calls=%async_computation.3 | async-start | bytes 2097152 | tf_op jit(solution)/shard_map/all_to_all | solution.py:527
  137.1 32.1 %collective-permute-start.18 = (bf16[1,1024,512]{2,1,0:T(8,128)(2,1)}, bf16[1,1024,512]{2,1,0:T(8,128)(2,1)}, u32[]{:S(2)}, u32[]{:S(2)}) collective-permute-start(bf16[1,1024,512]{2,1,0:T(8,128)(2,1)} %collective-permute-done.14.u1_ref), channel_id=1, source_target_pairs={{0,1},{1,2},{2,3},{3,0},{4,5},{5,6},{6,7},{7,4},{8,9},{9,10},{10,1... | collective-permute-start | bytes 3145736 | tf_op jit(solution)/shard_map/ppermute | solution.py:422
  140.6 28.6 %collective-permute-start.19 = (bf16[1,1024,512]{2,1,0:T(8,128)(2,1)}, bf16[1,1024,512]{2,1,0:T(8,128)(2,1)}, u32[]{:S(2)}, u32[]{:S(2)}) collective-permute-start(bf16[1,1024,512]{2,1,0:T(8,128)(2,1)} %shard_map.204), channel_id=1, source_target_pairs={{0,3},{1,0},{2,1},{3,2},{4,7},{5,4},{6,5},{7,6},{8,11},{9,8},{10,9... | collective-permute-start | bytes 3145736 | tf_op jit(solution)/shard_map/ppermute | solution.py:422
  153.7 10.3 %collective-permute-start.16 = (bf16[256,1024]{1,0:T(8,128)(2,1)S(1)}, bf16[256,1024]{1,0:T(8,128)(2,1)S(1)}, u32[]{:S(2)}, u32[]{:S(2)}) collective-permute-start(bf16[256,1024]{1,0:T(8,128)(2,1)S(1)} %bitcast.27), channel_id=1, source_target_pairs={{0,4},{4,0},{8,12},{12,8},{16,20},{20,16},{24,28},{28,24},{32,36},... | collective-permute-start | bytes 1572872 | tf_op jit(solution)/shard_map/ppermute | solution.py:529
  153.9 10.1 %collective-permute-start.17 = (bf16[256,1024]{1,0:T(8,128)(2,1)S(1)}, bf16[256,1024]{1,0:T(8,128)(2,1)S(1)}, u32[]{:S(2)}, u32[]{:S(2)}) collective-permute-start(bf16[256,1024]{1,0:T(8,128)(2,1)S(1)} %bitcast.26), channel_id=1, source_target_pairs={{0,4},{4,0},{8,12},{12,8},{16,20},{20,16},{24,28},{28,24},{32,36},... | collective-permute-start | bytes 1572872 | tf_op jit(solution)/shard_map/ppermute | solution.py:529
  172.0 2.7 %collective-permute-start.20 = (bf16[512,1024]{1,0:T(8,128)(2,1)S(1)}, bf16[512,1024]{1,0:T(8,128)(2,1)S(1)}, u32[]{:S(2)}, u32[]{:S(2)}) collective-permute-start(bf16[512,1024]{1,0:T(8,128)(2,1)S(1)} %get-tuple-element.63), channel_id=1, source_target_pairs={{0,4},{4,0},{8,12},{12,8},{16,20},{20,16},{24,28},{28,24},{32,36},... | collective-permute-start | bytes 3145736 | tf_op jit(solution)/shard_map/ppermute | solution.py:533
  174.9 21.3 %copy-start.6 = (f32[160,1024]{1,0:T(8,128)S(1)}, f32[160,1024]{1,0:T(8,128)}, u32[]{:S(2)}) copy-start(f32[160,1024]{1,0:T(8,128)} %copy-done.5) | copy-start | bytes 1966084
  174.9 21.3 %copy-start.9 = (s32[160,2]{1,0:T(8,128)S(1)}, s32[160,2]{1,0:T(8,128)}, u32[]{:S(2)}) copy-start(s32[160,2]{1,0:T(8,128)} %get-tuple-element.64.didx_ref) | copy-start | bytes 3844
  174.9 21.3 %copy-start.14 = (f32[160,2]{0,1:T(2,128)S(1)}, f32[160,2]{0,1:T(2,128)}, u32[]{:S(2)}) copy-start(f32[160,2]{0,1:T(2,128)} %param.34) | copy-start | bytes 3844
  (29 other events, 221.8 us)
Sparse Core Ops, SparseCore 0:
  9.7 40.9 all-gather.2
  52.3 56.2 all-gather.4
